TPU v7x, 32 devices: a whole 2x2x4 slice. The times are simulated.
32 devices in a mesh: groups: 2 (over x), hid: 16 (over z, y, core).
Axes of the slice: x: 2, y: 2, z: 4, core: 2. Of those that a mesh axis runs over, the one named last changes fastest.
Arguments:
- queries: bfloat16 [128, 64, 128], P(('groups', 'hid')), parts along dimension 0, may hold values from -12 to 12
- k_cache: bfloat16 [128, 192, 1024], P(('groups', 'hid')), parts along dimension 0, may hold values from -450 to 450
- v_cache: bfloat16 [128, 192, 1024], P(('groups', 'hid')), parts along dimension 0, may hold values from -6 to 6
- lengths: int32 [128], P(('groups', 'hid')), parts along dimension 0, may hold values from 24 to 192, as said below
- residual_in: bfloat16 [128, 8192], P(('groups', 'hid')), parts along dimension 0, may hold values from -6 to 6
- norm_gain: float32 [8192], replicated, may hold values from 0.25 to 1.75
- gate_w: bfloat16 [16, 56, 1024, 128], P('hid'), may hold values from -0.0625 to 0.0625
- up_w: bfloat16 [16, 56, 1024, 128], P('hid'), may hold values from -0.0625 to 0.0625
- down_w: bfloat16 [16, 56, 128, 1024], P('hid'), may hold values from -0.09375 to 0.09375
- block_list: int32 [4, 28], P('groups'), parts along dimension 0, may hold values from 0 to 55, as said below
- block_count: int32 [4], P('groups'), parts along dimension 0, may hold values from 1 to 28, as said below
Outputs:
- layer_out: bfloat16 [128, 8192], P(('groups', 'hid')), parts along dimension 0
There are 2 independent parts, one for each index of `groups`. A program takes and returns all parts, laid end to end along the dimension named above; an argument that names none is the same for every part. Nothing has to cross between parts.
Inputs may be any that keep to these rules, and one draw needn't show every extreme that they name: `lengths`: some request's length is 192. `block_list`: each row holds 28 distinct block indices of its group. `block_count`: exactly one group has all 28 listed blocks active.
All inputs are finite; a program needn't handle non-finite values.
Results may differ from a plain program's by a relative error of at most 0.006.
Values may be sent and summed in bfloat16 or wider, within the bound.
No kernel may reach another device: no remote copies, remote signals or barrier semaphores. Data moves between devices by JAX's collectives and lax.ppermute only.
A program may use at most 128 MiB of HBM per device.

v0:
```python
import math

import jax
import jax.numpy as jnp
from jax import lax
from jax.sharding import PartitionSpec as P

MDL = 8


def from_partner(value, axis, apart):
    mask = 2**apart
    pairs = [(source, source ^ mask) for source in range(lax.axis_size(axis))]
    return lax.ppermute(value, axis, pairs)


def on_device(
    queries,
    k_cache,
    v_cache,
    lengths,
    residual_in,
    norm_gain,
    gate_w,
    up_w,
    down_w,
    block_list,
    block_count,
):
    dev_count = lax.axis_size("hid")
    position = lax.axis_index("hid")
    group_id = position // MDL
    member = position % MDL
    group_total = dev_count // MDL
    rows_dev = queries.shape[0]
    head_count = queries.shape[1]
    head_size = queries.shape[2]
    cache_len = k_cache.shape[1]
    kv_count = k_cache.shape[2] // head_size
    model_width = residual_in.shape[1]
    slice_width = model_width // MDL
    all_rows = rows_dev * dev_count
    query_heads = queries.reshape(rows_dev, kv_count, head_count // kv_count, head_size)
    key_heads = k_cache.reshape(rows_dev, cache_len, kv_count, head_size)
    value_heads = v_cache.reshape(rows_dev, cache_len, kv_count, head_size)
    scores = jnp.einsum(
        "rkgd,rtkd->rkgt", query_heads, key_heads, preferred_element_type=jnp.float32
    ) / math.sqrt(head_size)
    valid = jnp.arange(cache_len)[None, None, None, :] < lengths[:, None, None, None]
    scores = jnp.where(valid, scores, -1e30)
    row_top = jnp.max(scores, axis=-1, keepdims=True)
    exp_terms = jnp.where(valid, jnp.exp(scores - row_top), 0.0)
    attn_probs = (exp_terms / jnp.sum(exp_terms, axis=-1, keepdims=True)).astype(jnp.bfloat16)
    attended = jnp.einsum(
        "rkgt,rtkd->rkgd", attn_probs, value_heads, preferred_element_type=jnp.float32
    )
    mixed_rows = residual_in.astype(jnp.float32) + attended.reshape(rows_dev, model_width)
    mean_sq = jnp.mean(mixed_rows * mixed_rows, axis=1, keepdims=True)
    normed = (mixed_rows * lax.rsqrt(mean_sq + 1e-05) * norm_gain).astype(jnp.bfloat16)
    send_tiles = jnp.broadcast_to(
        normed.reshape(rows_dev, 1, MDL, slice_width), (rows_dev, group_total, MDL, slice_width)
    )
    send_tiles = send_tiles.reshape(rows_dev, dev_count, slice_width)
    arrived = lax.all_to_all(send_tiles, "hid", split_axis=1, concat_axis=0, tiled=True).reshape(
        all_rows, slice_width
    )
    chosen = lax.dynamic_index_in_dim(block_list, group_id, 0, keepdims=False)
    live_count = lax.dynamic_index_in_dim(block_count, group_id, 0, keepdims=False)
    gate_sel = jnp.take(gate_w[0], chosen, axis=0)
    up_sel = jnp.take(up_w[0], chosen, axis=0)
    down_sel = jnp.take(down_w[0], chosen, axis=0)
    active = jnp.arange(chosen.shape[0]) < live_count
    gate_part = jnp.einsum("bs,csu->bcu", arrived, gate_sel, preferred_element_type=jnp.float32)
    up_part = jnp.einsum("bs,csu->bcu", arrived, up_sel, preferred_element_type=jnp.float32)
    level_count = MDL.bit_length() - 1
    half_rows = all_rows
    for bit_num in range(level_count):
        half_rows = half_rows // 2
        upper_half = member // (1 << bit_num) % 2
        keep_at = upper_half * half_rows
        send_at = (1 - upper_half) * half_rows
        sent_gate = lax.dynamic_slice_in_dim(gate_part, send_at, half_rows, 0)
        sent_up = lax.dynamic_slice_in_dim(up_part, send_at, half_rows, 0)
        other_gate, other_up = from_partner((sent_gate, sent_up), "hid", bit_num)
        gate_part = lax.dynamic_slice_in_dim(gate_part, keep_at, half_rows, 0) + other_gate
        up_part = lax.dynamic_slice_in_dim(up_part, keep_at, half_rows, 0) + other_up
    hidden = jnp.where(active[None, :, None], jnp.maximum(gate_part, 0.0) * up_part, 0.0).astype(
        jnp.bfloat16
    )
    for bit_num in reversed(range(level_count)):
        upper_half = member // (1 << bit_num) % 2
        other_rows = from_partner(hidden, "hid", bit_num)
        hidden = jnp.where(
            upper_half == 0,
            jnp.concatenate([hidden, other_rows], axis=0),
            jnp.concatenate([other_rows, hidden], axis=0),
        )
    ffn_part = jnp.einsum("bcu,cus->bs", hidden, down_sel, preferred_element_type=jnp.float32)
    returned = lax.all_to_all(
        ffn_part.reshape(dev_count, rows_dev, slice_width).astype(jnp.bfloat16),
        "hid",
        split_axis=0,
        concat_axis=2,
        tiled=True,
    ).astype(jnp.float32)
    summed = jnp.sum(returned.reshape(rows_dev, group_total, model_width), axis=1)
    return (mixed_rows + summed).astype(jnp.bfloat16)


def solution(mesh):
    in_specs = (
        P(("groups", "hid"), None, None),
        P(("groups", "hid"), None, None),
        P(("groups", "hid"), None, None),
        P(("groups", "hid")),
        P(("groups", "hid"), None),
        P(),
        P("hid", None, None, None),
        P("hid", None, None, None),
        P("hid", None, None, None),
        P("groups", None),
        P("groups"),
    )
    out_specs = P(("groups", "hid"), None)
    return jax.shard_map(
        on_device, mesh=mesh, in_specs=in_specs, out_specs=out_specs, check_vma=False
    )
```

profile of v0, /device:TPU:0, one launch (start us, length us, event | category | flops | bytes accessed | tf_op | source)
XLA Modules:
  0.0 103.9 jit_solution(8355834859897504025)
XLA Ops:
  0.0 0.8 iota_compare_fusion
  1.4 1.7 %fusion.26 = f32[4,8,8,192]{3,2,1,0:T(8,128)S(1)} fusion(pred[4,192]{1,0:T(4,128)(4,1)S(1)} %iota_compare_fusion, bf16[4,64,128]{2,1,0:T(8,128)(2,1)} %param.13, bf16[4,192,1024]{2,1,0:T(8,128)(2,1)S(1)} %copy-done), kind=kOutput, calls=%fused_computation.25 | convolution fusion | flops 12681216 | bytes 1835776 | tf_op jit(solution)/shard_map/rkgd,rtkd->rkgt/dot_general | solution.py:46
  3.4 2.0 %fusion.34 = f32[1,4,64,128]{3,2,1,0:T(8,128)S(1)} fusion(f32[4,8,8]{2,1,0:T(8,128)S(1)} %fusion.50, f32[4,8,8,192]{3,2,1,0:T(8,128)S(1)} %fusion.26, pred[4,192]{1,0:T(4,128)(4,1)S(1)} %iota_compare_fusion, bf16[4,192,1024]{2,1,0:T(8,128)(2,1)} %param.15), kind=kOutput, calls=%fused_computation.29 | convolution fusion | flops 12779967 | bytes 1902336 | tf_op jit(solution)/shard_map/rkgt,rtkd->rkgd/dot_general | solution.py:54
  5.4 1.1 %multiply_reduce_fusion = f32[4]{0:T(128)S(1)} fusion(f32[1,4,64,128]{3,2,1,0:T(8,128)S(1)} %fusion.34, bf16[4,8192]{1,0:T(4,128)(2,1)} %param.17), kind=kLoop, calls=%fused_computation.47 | loop fusion | flops 131068 | bytes 196624 | tf_op jit(solution)/shard_map/reduce_sum | solution.py:58
  6.5 1.0 multiply_convert_fusion
  7.4 0.7 broadcast_in_dim.66
  8.1 7.4 %all-to-all-start = ((bf16[4,16,1024]{2,0,1:T(4,128)(2,1)}), bf16[4,16,1024]{2,0,1:T(4,128)(2,1)S(1)}, u32[]{:S(2)}, u32[]{:S(2)}) async-start(bf16[4,16,1024]{2,0,1:T(4,128)(2,1)} %bitcast.3), calls=%async_computation | async-start | bytes 262144 | tf_op jit(solution)/shard_map/all_to_all | solution.py:64
  15.6 0.7 compare_and_fusion
  16.3 10.0 %gather_fusion.1 = bf16[28,1024,128]{2,1,0:T(8,128)(2,1)} fusion(bf16[56,1024,128]{2,1,0:T(8,128)(2,1)} %bitcast.69, s32[1024]{0:T(1024)S(1)} %pad_clamp_fusion.1), kind=kCustom, calls=%fused_computation.clone | custom fusion | bytes 14680176 | tf_op jit(solution)/shard_map/jit(_take)/gather | solution.py:69
  26.3 9.9 %gather_fusion.2 = bf16[28,1024,128]{2,1,0:T(8,128)(2,1)} fusion(bf16[56,1024,128]{2,1,0:T(8,128)(2,1)} %bitcast.70, s32[1024]{0:T(1024)S(1)} %pad_clamp_fusion.1), kind=kCustom, calls=%fused_computation.1.clone | custom fusion | bytes 14680176 | tf_op jit(solution)/shard_map/jit(_take)/gather | solution.py:70
  36.2 4.9 %fusion.3 = f32[64,28,128]{2,0,1:T(8,128)S(1)} fusion(bf16[64,1024,1]{1,0,2:T(8,128)(2,1)S(1)} %reshape.145, bf16[28,1024,128]{2,1,0:T(8,128)(2,1)} %gather_fusion.1, pred[28]{0:T(512)(128)(4,1)S(1)} %get-tuple-element.6), kind=kOutput, calls=%fused_computation.6 | convolution fusion | flops 473432064 | bytes 8388636 | tf_op jit(solution)/shard_map/bs,csu->bcu/dot_general | solution.py:73
  41.2 1.0 constant_dynamic-slice_fusion.5
  42.6 1.7 %fusion.1 = f32[64,28,128]{2,0,1:T(8,128)S(1)} fusion(bf16[64,1024,1]{1,0,2:T(8,128)(2,1)S(1)} %reshape.145, bf16[28,1024,128]{2,1,0:T(8,128)(2,1)S(1)} %bitcast.68, pred[28]{0:T(512)(128)(4,1)S(1)} %get-tuple-element.6), kind=kOutput, calls=%fused_computation.4 | convolution fusion | flops 473432064 | bytes 8388636 | tf_op jit(solution)/shard_map/bs,csu->bcu/dot_general | solution.py:74
  44.4 0.9 copy-done.2
  45.6 1.2 %dynamic-slice_add_fusion.1 = f32[32,28,128]{2,0,1:T(8,128)S(1)} fusion(f32[32,28,128]{2,0,1:T(8,128)} %collective-permute-done, f32[64,28,128]{2,0,1:T(8,128)} %copy-done.3, s32[]{:T(128)S(6)} %select_n.143), kind=kLoop, calls=%fused_computation.37 | loop fusion | flops 114688 | bytes 1376260 | tf_op jit(solution)/shard_map/add | solution.py:85
  46.8 1.9 %collective-permute-start.1 = (f32[16,28,128]{2,0,1:T(8,128)S(1)}, f32[16,28,128]{2,0,1:T(8,128)S(1)}, u32[]{:S(2)}, u32[]{:S(2)}) collective-permute-start(f32[16,28,128]{2,0,1:T(8,128)S(1)} %constant_dynamic-slice_fusion.4), channel_id=1, source_target_pairs={{0,2},{1,3},{2,0},{3,1},{4,6},{5,7},{6,4},{7,5},{8,10},{9,11},{10,... | collective-permute-start | bytes 688136 | tf_op jit(solution)/shard_map/ppermute | solution.py:14
  48.8 1.1 %dynamic-slice_add_fusion = f32[32,28,128]{2,0,1:T(8,128)S(1)} fusion(f32[32,28,128]{2,0,1:T(8,128)S(1)} %collective-permute-done.3, f32[64,28,128]{2,0,1:T(8,128)} %copy-done.2, s32[]{:T(128)S(6)} %select_n.143), kind=kLoop, calls=%fused_computation.36 | loop fusion | flops 114688 | bytes 1376260 | tf_op jit(solution)/shard_map/add | solution.py:86
  50.1 5.2 %collective-permute-done.1 = f32[16,28,128]{2,0,1:T(8,128)S(1)} collective-permute-done((f32[16,28,128]{2,0,1:T(8,128)S(1)}, f32[16,28,128]{2,0,1:T(8,128)S(1)}, u32[]{:S(2)}, u32[]{:S(2)}) %collective-permute-start.1) | collective-permute-done | bytes 229408 | tf_op jit(solution)/shard_map/ppermute | solution.py:14
  55.4 1.9 %collective-permute-start.2 = (f32[8,28,128]{2,0,1:T(8,128)S(1)}, f32[8,28,128]{2,0,1:T(8,128)S(1)}, u32[]{:S(2)}, u32[]{:S(2)}) collective-permute-start(f32[8,28,128]{2,0,1:T(8,128)S(1)} %constant_dynamic-slice_fusion.3), channel_id=1, source_target_pairs={{0,4},{1,5},{2,6},{3,7},{4,0},{5,1},{6,2},{7,3},{8,12},{9,13},{10,... | collective-permute-start | bytes 344072 | tf_op jit(solution)/shard_map/ppermute | solution.py:14
  57.3 2.3 %collective-permute-done.4 = f32[16,28,128]{2,0,1:T(8,128)S(1)} collective-permute-done((f32[16,28,128]{2,0,1:T(8,128)S(1)}, f32[16,28,128]{2,0,1:T(8,128)S(1)}, u32[]{:S(2)}, u32[]{:S(2)}) %collective-permute-start.4) | collective-permute-done | bytes 229408 | tf_op jit(solution)/shard_map/ppermute | solution.py:14
  59.7 1.7 %collective-permute-start.5 = (f32[8,28,128]{2,0,1:T(8,128)S(1)}, f32[8,28,128]{2,0,1:T(8,128)S(1)}, u32[]{:S(2)}, u32[]{:S(2)}) collective-permute-start(f32[8,28,128]{2,0,1:T(8,128)S(1)} %constant_dynamic-slice_fusion), channel_id=1, source_target_pairs={{0,4},{1,5},{2,6},{3,7},{4,0},{5,1},{6,2},{7,3},{8,12},{9,13},{10,... | collective-permute-start | bytes 344072 | tf_op jit(solution)/shard_map/ppermute | solution.py:14
  61.5 0.6 dynamic_slice.44
  62.1 0.6 iota_compare_fusion.1
  62.7 1.9 %collective-permute-done.5 = f32[8,28,128]{2,0,1:T(8,128)S(1)} collective-permute-done((f32[8,28,128]{2,0,1:T(8,128)S(1)}, f32[8,28,128]{2,0,1:T(8,128)S(1)}, u32[]{:S(2)}, u32[]{:S(2)}) %collective-permute-start.5) | collective-permute-done | bytes 114720 | tf_op jit(solution)/shard_map/ppermute | solution.py:14
  64.7 1.7 %collective-permute-start.6 = (bf16[8,28,128]{2,0,1:T(8,128)(2,1)S(1)}, bf16[8,28,128]{2,0,1:T(8,128)(2,1)S(1)}, u32[]{:S(2)}, u32[]{:S(2)}) collective-permute-start(bf16[8,28,128]{2,0,1:T(8,128)(2,1)S(1)} %select_convert_fusion), channel_id=1, source_target_pairs={{0,4},{1,5},{2,6},{3,7},{4,0},{5,1},{6,2},{7,3},{8,12},{9,13},{10,... | collective-permute-start | bytes 172040 | tf_op jit(solution)/shard_map/ppermute | solution.py:14
  66.4 2.5 %collective-permute-done.6 = bf16[8,28,128]{2,0,1:T(8,128)(2,1)S(1)} collective-permute-done((bf16[8,28,128]{2,0,1:T(8,128)(2,1)S(1)}, bf16[8,28,128]{2,0,1:T(8,128)(2,1)S(1)}, u32[]{:S(2)}, u32[]{:S(2)}) %collective-permute-start.6) | collective-permute-done | bytes 57376 | tf_op jit(solution)/shard_map/ppermute | solution.py:14
  69.0 1.7 %collective-permute-start.7 = (bf16[16,28,128]{2,0,1:T(8,128)(2,1)S(1)}, bf16[16,28,128]{2,0,1:T(8,128)(2,1)S(1)}, u32[]{:S(2)}, u32[]{:S(2)}) collective-permute-start(bf16[16,28,128]{2,0,1:T(8,128)(2,1)S(1)} %maximum_select_fusion.3), channel_id=1, source_target_pairs={{0,2},{1,3},{2,0},{3,1},{4,6},{5,7},{6,4},{7,5},{8,10},{9,11},{10,... | collective-permute-start | bytes 344072 | tf_op jit(solution)/shard_map/ppermute | solution.py:14
  70.7 3.1 %collective-permute-done.7 = bf16[16,28,128]{2,0,1:T(8,128)(2,1)S(1)} collective-permute-done((bf16[16,28,128]{2,0,1:T(8,128)(2,1)S(1)}, bf16[16,28,128]{2,0,1:T(8,128)(2,1)S(1)}, u32[]{:S(2)}, u32[]{:S(2)}) %collective-permute-start.7) | collective-permute-done | bytes 114720 | tf_op jit(solution)/shard_map/ppermute | solution.py:14
  74.1 10.0 %gather_fusion = bf16[28,128,1024]{2,1,0:T(8,128)(2,1)} fusion(bf16[56,128,1024]{2,1,0:T(8,128)(2,1)} %bitcast.71, s32[1024]{0:T(1024)S(1)} %pad_clamp_fusion), kind=kCustom, calls=%fused_computation.2 | custom fusion | bytes 14680176 | tf_op jit(solution)/shard_map/jit(_take)/gather | solution.py:71
  84.1 4.6 %fusion.31 = bf16[64,1024]{1,0:T(8,128)(2,1)S(1)} fusion(bf16[28,128,1024]{2,1,0:T(8,128)(2,1)} %gather_fusion, pred[28]{0:T(512)(128)(4,1)S(1)} %get-tuple-element.6, bf16[32,28,128]{2,0,1:T(8,128)(2,1)S(1)} %collective-permute-done.8, bf16[32,28,128]{2,0,1:T(8,128)(2,1)S(1)} %maximum_select_fusion.2, pred[]{:T(512)S(6)} %eq.17), kind=kOutput, calls=%fused_computation.28 | convolution fusion | flops 475561984 | bytes 7929885 | tf_op jit(solution)/shard_map/bcu,cus->bs/dot_general | solution.py:98
  88.8 13.6 %all_to_all.24 = bf16[16,4,1024]{2,1,0:T(4,128)(2,1)S(1)} all-to-all(bf16[16,4,1024]{2,1,0:T(4,128)(2,1)S(1)} %convert_element_type.45), channel_id=1, replica_groups=mesh['groups'=2,'hid'=16] {'hid'}, dimensions={0} | all-to-all | bytes 262144 | tf_op jit(solution)/shard_map/all_to_all | solution.py:99
  103.1 0.8 add_convert_fusion
  (48 shorter events, 3.1 us)
Async XLA Ops:
  0.0 1.4 %copy-start = (bf16[4,192,1024]{2,1,0:T(8,128)(2,1)S(1)}, bf16[4,192,1024]{2,1,0:T(8,128)(2,1)}, u32[]{:S(2)}) copy-start(bf16[4,192,1024]{2,1,0:T(8,128)(2,1)} %param.14) | copy-start | bytes 4718596
  8.1 28.0 %all-to-all-start = ((bf16[4,16,1024]{2,0,1:T(4,128)(2,1)}), bf16[4,16,1024]{2,0,1:T(4,128)(2,1)S(1)}, u32[]{:S(2)}, u32[]{:S(2)}) async-start(bf16[4,16,1024]{2,0,1:T(4,128)(2,1)} %bitcast.3), calls=%async_computation | async-start | bytes 262144 | tf_op jit(solution)/shard_map/all_to_all | solution.py:64
  36.2 6.5 %slice-start = ((s8[7340032]{0:T(1024)(128)(4,1)}), s8[3145728]{0:T(1024)(128)(4,1)S(1)}, s32[]{:S(2)}) async-start(s8[7340032]{0:T(1024)(128)(4,1)} %bitcast.67), calls=%async_computation.2 | async-start | bytes 6291456
  36.2 6.4 %slice-start.1 = ((s8[7340032]{0:T(1024)(128)(4,1)}), s8[4194304]{0:T(1024)(128)(4,1)S(1)}, s32[]{:S(2)}) async-start(s8[7340032]{0:T(1024)(128)(4,1)} %bitcast.67), calls=%async_computation.3 | async-start | bytes 8388608
  41.2 1.1 %copy-start.3 = (f32[64,28,128]{2,0,1:T(8,128)}, f32[64,28,128]{2,0,1:T(8,128)S(1)}, u32[]{:S(2)}) copy-start(f32[64,28,128]{2,0,1:T(8,128)S(1)} %fusion.3) | copy-start | bytes 2752516
  42.3 19.2 %copy-start.6 = (s32[2]{0:T(128)S(1)}, s32[2]{0:T(128)}, u32[]{:S(2)}) copy-start(s32[2]{0:T(128)} %param.23) | copy-start | bytes 28
  42.3 31.7 %copy-start.5 = (s32[2,28]{1,0:T(2,128)S(1)}, s32[2,28]{1,0:T(2,128)}, u32[]{:S(2)}) copy-start(s32[2,28]{1,0:T(2,128)} %param.22) | copy-start | bytes 676
  42.3 3.3 %collective-permute-start = (f32[32,28,128]{2,0,1:T(8,128)}, f32[32,28,128]{2,0,1:T(8,128)}, u32[]{:S(2)}, u32[]{:S(2)}) collective-permute-start(f32[32,28,128]{2,0,1:T(8,128)} %constant_dynamic-slice_fusion.5), channel_id=1, source_target_pairs={{0,1},{1,0},{2,3},{3,2},{4,5},{5,4},{6,7},{7,6},{8,9},{9,8},{10,11... | collective-permute-start | bytes 1376264 | tf_op jit(solution)/shard_map/ppermute | solution.py:14
  44.4 0.9 copy-start.2
  45.3 3.4 %collective-permute-start.3 = (f32[32,28,128]{2,0,1:T(8,128)S(1)}, f32[32,28,128]{2,0,1:T(8,128)S(1)}, u32[]{:S(2)}, u32[]{:S(2)}) collective-permute-start(f32[32,28,128]{2,0,1:T(8,128)S(1)} %constant_dynamic-slice_fusion.2), channel_id=1, source_target_pairs={{0,1},{1,0},{2,3},{3,2},{4,5},{5,4},{6,7},{7,6},{8,9},{9,8},{10,11... | collective-permute-start | bytes 1376264 | tf_op jit(solution)/shard_map/ppermute | solution.py:14
  46.8 8.5 %collective-permute-start.1 = (f32[16,28,128]{2,0,1:T(8,128)S(1)}, f32[16,28,128]{2,0,1:T(8,128)S(1)}, u32[]{:S(2)}, u32[]{:S(2)}) collective-permute-start(f32[16,28,128]{2,0,1:T(8,128)S(1)} %constant_dynamic-slice_fusion.4), channel_id=1, source_target_pairs={{0,2},{1,3},{2,0},{3,1},{4,6},{5,7},{6,4},{7,5},{8,10},{9,11},{10,... | collective-permute-start | bytes 688136 | tf_op jit(solution)/shard_map/ppermute | solution.py:14
  49.9 9.8 %collective-permute-start.4 = (f32[16,28,128]{2,0,1:T(8,128)S(1)}, f32[16,28,128]{2,0,1:T(8,128)S(1)}, u32[]{:S(2)}, u32[]{:S(2)}) collective-permute-start(f32[16,28,128]{2,0,1:T(8,128)S(1)} %constant_dynamic-slice_fusion.1), channel_id=1, source_target_pairs={{0,2},{1,3},{2,0},{3,1},{4,6},{5,7},{6,4},{7,5},{8,10},{9,11},{10,... | collective-permute-start | bytes 688136 | tf_op jit(solution)/shard_map/ppermute | solution.py:14
  55.4 7.3 %collective-permute-start.2 = (f32[8,28,128]{2,0,1:T(8,128)S(1)}, f32[8,28,128]{2,0,1:T(8,128)S(1)}, u32[]{:S(2)}, u32[]{:S(2)}) collective-permute-start(f32[8,28,128]{2,0,1:T(8,128)S(1)} %constant_dynamic-slice_fusion.3), channel_id=1, source_target_pairs={{0,4},{1,5},{2,6},{3,7},{4,0},{5,1},{6,2},{7,3},{8,12},{9,13},{10,... | collective-permute-start | bytes 344072 | tf_op jit(solution)/shard_map/ppermute | solution.py:14
  59.7 4.9 %collective-permute-start.5 = (f32[8,28,128]{2,0,1:T(8,128)S(1)}, f32[8,28,128]{2,0,1:T(8,128)S(1)}, u32[]{:S(2)}, u32[]{:S(2)}) collective-permute-start(f32[8,28,128]{2,0,1:T(8,128)S(1)} %constant_dynamic-slice_fusion), channel_id=1, source_target_pairs={{0,4},{1,5},{2,6},{3,7},{4,0},{5,1},{6,2},{7,3},{8,12},{9,13},{10,... | collective-permute-start | bytes 344072 | tf_op jit(solution)/shard_map/ppermute | solution.py:14
  64.7 4.2 %collective-permute-start.6 = (bf16[8,28,128]{2,0,1:T(8,128)(2,1)S(1)}, bf16[8,28,128]{2,0,1:T(8,128)(2,1)S(1)}, u32[]{:S(2)}, u32[]{:S(2)}) collective-permute-start(bf16[8,28,128]{2,0,1:T(8,128)(2,1)S(1)} %select_convert_fusion), channel_id=1, source_target_pairs={{0,4},{1,5},{2,6},{3,7},{4,0},{5,1},{6,2},{7,3},{8,12},{9,13},{10,... | collective-permute-start | bytes 172040 | tf_op jit(solution)/shard_map/ppermute | solution.py:14
  69.0 4.9 %collective-permute-start.7 = (bf16[16,28,128]{2,0,1:T(8,128)(2,1)S(1)}, bf16[16,28,128]{2,0,1:T(8,128)(2,1)S(1)}, u32[]{:S(2)}, u32[]{:S(2)}) collective-permute-start(bf16[16,28,128]{2,0,1:T(8,128)(2,1)S(1)} %maximum_select_fusion.3), channel_id=1, source_target_pairs={{0,2},{1,3},{2,0},{3,1},{4,6},{5,7},{6,4},{7,5},{8,10},{9,11},{10,... | collective-permute-start | bytes 344072 | tf_op jit(solution)/shard_map/ppermute | solution.py:14
  73.9 10.2 %collective-permute-start.8 = (bf16[32,28,128]{2,0,1:T(8,128)(2,1)S(1)}, bf16[32,28,128]{2,0,1:T(8,128)(2,1)S(1)}, u32[]{:S(2)}, u32[]{:S(2)}) collective-permute-start(bf16[32,28,128]{2,0,1:T(8,128)(2,1)S(1)} %maximum_select_fusion.2), channel_id=1, source_target_pairs={{0,1},{1,0},{2,3},{3,2},{4,5},{5,4},{6,7},{7,6},{8,9},{9,8},{10,11... | collective-permute-start | bytes 688136 | tf_op jit(solution)/shard_map/ppermute | solution.py:14
  74.0 29.8 %copy-start.1 = (bf16[4,192,1024]{2,1,0:T(8,128)(2,1)S(1)}, bf16[4,192,1024]{2,1,0:T(8,128)(2,1)}, u32[]{:S(2)}) copy-start(bf16[4,192,1024]{2,1,0:T(8,128)(2,1)} %param.14) | copy-start | bytes 4718596
  84.1 19.0 %copy-start.4 = (bf16[4,8192]{1,0:T(4,128)(2,1)S(1)}, bf16[4,8192]{1,0:T(4,128)(2,1)}, u32[]{:S(2)}) copy-start(bf16[4,8192]{1,0:T(4,128)(2,1)} %param.17) | copy-start | bytes 196612
where the time goes:
time: 104 us
  local copies, waits for them, and re-layouts  34.4 us (33%)
  starting transfers between devices  17.4 us (17%)
  matrix products  15 us (14%)
  waiting for transfers between devices  15 us (14%)
  blocking collectives  13.6 us (13%)
  other arithmetic  8.2 us (8%)
    ppermute x9, waiting for transfers between devices, from_partner(): return lax.ppermute(value, axis, pairs)  15 us
    all_to_all x1, blocking collectives, on_device(): lax.all_to_all(ffn_part.reshape(dev_count, rows_dev, slice_width).astype(...  13.6 us
    gather x1, local copies, waits for them, and re-layouts, on_device(): down_sel = jnp.take(down_w[0], chosen, axis=0)  10 us
    ppermute x9, starting transfers between devices, from_partner(): return lax.ppermute(value, axis, pairs)  9.97 us
    gather x1, local copies, waits for them, and re-layouts, on_device(): gate_sel = jnp.take(gate_w[0], chosen, axis=0)  9.97 us
    gather x1, local copies, waits for them, and re-layouts, on_device(): up_sel = jnp.take(up_w[0], chosen, axis=0)  9.91 us
    all_to_all x1, starting transfers between devices, on_device(): lax.all_to_all(send_tiles, 'hid', split_axis=1, concat_axis=0, tiled=True)  7.39 us
    dot_general x1, matrix products, on_device(): jnp.einsum('bs,csu->bcu', arrived, gate_sel, preferred_element_type=jnp.f...  4.94 us
  transfers between devices with their start and end apart: 10, of which 5 were waited for; matrix products, arithmetic and copies ran while one was open for 35% of the time, Pallas kernels for 0%

commit v1 on v0

v1 whole, which is shorter than its diff:
```python
import functools
import math

import jax
import jax.numpy as jnp
from jax import lax
from jax.experimental import pallas as pl
from jax.experimental.pallas import tpu as pltpu
from jax.sharding import PartitionSpec as P

MDL = 8
VMEM = pl.BlockSpec(memory_space=pltpu.VMEM)
SMEM = pl.BlockSpec(memory_space=pltpu.SMEM)
ANY = pl.BlockSpec(memory_space=pl.ANY)


def from_partner(value, apart):
    mask = 2**apart
    pairs = [(source, source ^ mask) for source in range(lax.axis_size("hid"))]
    return lax.ppermute(value, "hid", pairs)


def attend_kernel(
    kv_count, len_ref, q_ref, k_hbm, v_hbm, res_ref, gain_ref, mixed_ref, send_ref, k_buf, v_buf, sems
):
    rows, heads, size = q_ref.shape
    slots = k_buf.shape[1]
    width = kv_count * size
    per_kv = heads // kv_count
    k_copies = [pltpu.make_async_copy(k_hbm.at[r], k_buf.at[r], sems.at[0, r]) for r in range(rows)]
    v_copies = [pltpu.make_async_copy(v_hbm.at[r], v_buf.at[r], sems.at[1, r]) for r in range(rows)]
    for r in range(rows):
        k_copies[r].start()
        v_copies[r].start()
    own = (
        lax.broadcasted_iota(jnp.int32, (heads, width), 0) // per_kv
        == lax.broadcasted_iota(jnp.int32, (heads, width), 1) // size
    )
    slot_at = lax.broadcasted_iota(jnp.int32, (heads, slots), 1)
    for r in range(rows):
        wide = jnp.concatenate([q_ref[r]] * kv_count, axis=1)
        wide = jnp.where(own, wide, jnp.zeros_like(wide))
        k_copies[r].wait()
        scores = lax.dot_general(
            wide, k_buf[r], (((1,), (1,)), ((), ())), preferred_element_type=jnp.float32
        ) * (1.0 / math.sqrt(size))
        valid = slot_at < len_ref[r]
        scores = jnp.where(valid, scores, -1e30)
        top = jnp.max(scores, axis=1, keepdims=True)
        terms = jnp.where(valid, jnp.exp(scores - top), 0.0)
        probs = (terms / jnp.sum(terms, axis=1, keepdims=True)).astype(jnp.bfloat16)
        v_copies[r].wait()
        out = jnp.dot(probs, v_buf[r], preferred_element_type=jnp.float32)
        for h in range(heads):
            at = h // per_kv * size
            mixed_ref[r : r + 1, h * size : (h + 1) * size] = out[h : h + 1, at : at + size]
    mixed = mixed_ref[...] + res_ref[...].astype(jnp.float32)
    mixed_ref[...] = mixed
    mean_sq = jnp.mean(mixed * mixed, axis=1, keepdims=True)
    normed = (mixed * lax.rsqrt(mean_sq + 1e-05) * gain_ref[...]).astype(jnp.bfloat16)
    step = send_ref.shape[2]
    for m in range(MDL):
        part = normed[:, m * step : (m + 1) * step]
        for g in range(send_ref.shape[0] // MDL):
            send_ref[g * MDL + m] = part


def attend(queries, k_cache, v_cache, lengths, residual_in, norm_gain, dev_count):
    rows, heads, size = queries.shape
    slots, width = k_cache.shape[1:]
    model = residual_in.shape[1]
    return pl.pallas_call(
        functools.partial(attend_kernel, width // size),
        out_shape=(
            jax.ShapeDtypeStruct((rows, model), jnp.float32),
            jax.ShapeDtypeStruct((dev_count, rows, model // MDL), jnp.bfloat16),
        ),
        in_specs=[SMEM, VMEM, ANY, ANY, VMEM, VMEM],
        out_specs=(VMEM, VMEM),
        scratch_shapes=[
            pltpu.VMEM((rows, slots, width), jnp.bfloat16),
            pltpu.VMEM((rows, slots, width), jnp.bfloat16),
            pltpu.SemaphoreType.DMA((2, rows)),
        ],
        compiler_params=pltpu.CompilerParams(vmem_limit_bytes=16 * 2**20),
        name="attend",
    )(lengths, queries, k_cache, v_cache, residual_in, norm_gain.reshape(1, model))


def fetch_in_kernel(list_ref, gate_hbm, up_hbm, both_ref, sems):
    group = lax.axis_index("hid") // MDL
    count, _, twice = both_ref.shape
    unit = twice // 2

    def copies(c):
        block = list_ref[group, c]
        return (
            pltpu.make_async_copy(gate_hbm.at[0, block], both_ref.at[c, :, pl.ds(0, unit)], sems.at[0, c]),
            pltpu.make_async_copy(up_hbm.at[0, block], both_ref.at[c, :, pl.ds(unit, unit)], sems.at[1, c]),
        )

    @pl.loop(0, count)
    def _(c):
        for copy in copies(c):
            copy.start()

    @pl.loop(0, count)
    def _(c):
        for copy in copies(c):
            copy.wait()


def fetch_in(block_list, gate_w, up_w):
    count = block_list.shape[1]
    depth, unit = gate_w.shape[2:]
    return pl.pallas_call(
        fetch_in_kernel,
        out_shape=jax.ShapeDtypeStruct((count, depth, 2 * unit), jnp.bfloat16),
        in_specs=[SMEM, ANY, ANY],
        out_specs=VMEM,
        scratch_shapes=[pltpu.SemaphoreType.DMA((2, count))],
        compiler_params=pltpu.CompilerParams(vmem_limit_bytes=20 * 2**20),
        cost_estimate=pl.CostEstimate(flops=0, bytes_accessed=4 * count * depth * unit * 2, transcendentals=0),
        name="fetch_in",
    )(block_list, gate_w, up_w)


def fetch_down_kernel(list_ref, down_hbm, down_ref, sems):
    group = lax.axis_index("hid") // MDL
    count = down_ref.shape[0]

    def copy(c):
        return pltpu.make_async_copy(down_hbm.at[0, list_ref[group, c]], down_ref.at[c], sems.at[c])

    @pl.loop(0, count)
    def _(c):
        copy(c).start()

    @pl.loop(0, count)
    def _(c):
        copy(c).wait()


def fetch_down(block_list, down_w):
    count = block_list.shape[1]
    unit, depth = down_w.shape[2:]
    return pl.pallas_call(
        fetch_down_kernel,
        out_shape=jax.ShapeDtypeStruct((count, unit, depth), jnp.bfloat16),
        in_specs=[SMEM, ANY],
        out_specs=VMEM,
        scratch_shapes=[pltpu.SemaphoreType.DMA((count,))],
        compiler_params=pltpu.CompilerParams(vmem_limit_bytes=12 * 2**20),
        cost_estimate=pl.CostEstimate(flops=0, bytes_accessed=2 * count * depth * unit * 2, transcendentals=0),
        name="fetch_down",
    )(block_list, down_w)


def gate_up_kernel(x_ref, both_ref, keep_ref, sent_ref):
    upper = lax.axis_index("hid") % 2
    rows = x_ref.shape[0]
    half = rows // 2
    count, _, twice = both_ref.shape
    unit = twice // 2
    kept = x_ref[pl.ds(pl.multiple_of(upper * half, half), half), :]
    other = x_ref[pl.ds(pl.multiple_of((1 - upper) * half, half), half), :]
    x = jnp.concatenate([kept, other], axis=0)
    for c in range(count):
        pair = jnp.dot(x, both_ref[c], preferred_element_type=jnp.float32)
        for k in range(2):
            part = pair[:, k * unit : (k + 1) * unit]
            at = pl.ds((k * count + c) * unit, unit)
            keep_ref[:, at] = part[:half]
            sent_ref[:, at] = part[half:].astype(jnp.bfloat16)


def gate_up(x, both):
    rows = x.shape[0]
    count, depth, twice = both.shape
    return pl.pallas_call(
        gate_up_kernel,
        out_shape=(
            jax.ShapeDtypeStruct((rows // 2, count * twice), jnp.float32),
            jax.ShapeDtypeStruct((rows // 2, count * twice), jnp.bfloat16),
        ),
        in_specs=[VMEM, VMEM],
        out_specs=(VMEM, VMEM),
        compiler_params=pltpu.CompilerParams(vmem_limit_bytes=30 * 2**20),
        name="gate_up",
    )(x, both)


def down_kernel(h_ref, w_ref, out_ref):
    count, unit, depth = w_ref.shape
    rows = h_ref.shape[0]
    step = min(512, depth)
    for n in range(depth // step):
        at = pl.ds(n * step, step)
        w = w_ref[:, :, at].reshape(count * unit, step)
        total = jnp.dot(h_ref[...], w, preferred_element_type=jnp.float32)
        out_ref[:, at] = total.astype(jnp.bfloat16)


def down(hidden, weights):
    return pl.pallas_call(
        down_kernel,
        out_shape=jax.ShapeDtypeStruct((hidden.shape[0], weights.shape[2]), jnp.bfloat16),
        in_specs=[VMEM, VMEM],
        out_specs=VMEM,
        compiler_params=pltpu.CompilerParams(vmem_limit_bytes=20 * 2**20),
        name="down",
    )(hidden, weights)


def finish_kernel(mixed_ref, back_ref, out_ref):
    step = back_ref.shape[2]
    for m in range(MDL):
        total = mixed_ref[:, m * step : (m + 1) * step]
        for g in range(back_ref.shape[0] // MDL):
            total = total + back_ref[g * MDL + m].astype(jnp.float32)
        out_ref[:, m * step : (m + 1) * step] = total.astype(jnp.bfloat16)


def finish(mixed, back):
    return pl.pallas_call(
        finish_kernel,
        out_shape=jax.ShapeDtypeStruct(mixed.shape, jnp.bfloat16),
        in_specs=[VMEM, VMEM],
        out_specs=VMEM,
        compiler_params=pltpu.CompilerParams(vmem_limit_bytes=16 * 2**20),
        name="finish",
    )(mixed, back)


def on_device(
    queries,
    k_cache,
    v_cache,
    lengths,
    residual_in,
    norm_gain,
    gate_w,
    up_w,
    down_w,
    block_list,
    block_count,
):
    dev_count = lax.axis_size("hid")
    position = lax.axis_index("hid")
    group_id = position // MDL
    member = position % MDL
    rows_dev = queries.shape[0]
    model_width = residual_in.shape[1]
    slice_width = model_width // MDL
    all_rows = rows_dev * dev_count
    unit = gate_w.shape[3]
    units = block_list.shape[1] * unit

    mixed_rows, send_tiles = attend(
        queries, k_cache, v_cache, lengths, residual_in, norm_gain, dev_count
    )
    arrived = lax.all_to_all(send_tiles, "hid", split_axis=0, concat_axis=0, tiled=True).reshape(
        all_rows, slice_width
    )
    both = fetch_in(block_list, gate_w, up_w)
    part, sent = gate_up(arrived, both)
    part = part + from_partner(sent, 0).astype(jnp.float32)
    half_rows = all_rows // 2
    for bit_num in (1, 2):
        half_rows = half_rows // 2
        upper_half = member // (1 << bit_num) % 2
        sent = lax.dynamic_slice_in_dim(part, (1 - upper_half) * half_rows, half_rows, 0)
        other = from_partner(sent.astype(jnp.bfloat16), bit_num)
        part = lax.dynamic_slice_in_dim(part, upper_half * half_rows, half_rows, 0)
        part = part + other.astype(jnp.float32)
    live_count = lax.dynamic_index_in_dim(block_count, group_id, 0, keepdims=False)
    active = lax.broadcasted_iota(jnp.int32, (1, units), 1) < live_count * unit
    hidden = jnp.where(
        active, jnp.maximum(part[:, :units], 0.0) * part[:, units:], 0.0
    ).astype(jnp.bfloat16)
    for bit_num in (2, 1, 0):
        upper_half = member // (1 << bit_num) % 2
        other = from_partner(hidden, bit_num)
        hidden = jnp.where(
            upper_half == 0,
            jnp.concatenate([hidden, other], axis=0),
            jnp.concatenate([other, hidden], axis=0),
        )
    ffn_part = down(hidden, fetch_down(block_list, down_w))
    returned = lax.all_to_all(
        ffn_part.reshape(dev_count, rows_dev, slice_width),
        "hid",
        split_axis=0,
        concat_axis=0,
        tiled=True,
    )
    return finish(mixed_rows, returned)


def solution(mesh):
    in_specs = (
        P(("groups", "hid"), None, None),
        P(("groups", "hid"), None, None),
        P(("groups", "hid"), None, None),
        P(("groups", "hid")),
        P(("groups", "hid"), None),
        P(),
        P("hid", None, None, None),
        P("hid", None, None, None),
        P("hid", None, None, None),
        P("groups", None),
        P("groups"),
    )
    out_specs = P(("groups", "hid"), None)
    return jax.shard_map(
        on_device, mesh=mesh, in_specs=in_specs, out_specs=out_specs, check_vma=False
    )
```

time: 104 us -> 90.2 us (0.87)
  Pallas kernels: 0 us -> 16.8 us
  matrix products: 15 us -> 0 us
  other arithmetic: 8.2 us -> 0.34 us
  local copies, waits for them, and re-layouts: 34.4 us -> 28 us
  starting transfers between devices: 17.4 us -> 15.1 us
    gather x3 -> x0, local copies, waits for them, and re-layouts: 29.9 us -> none  [the longest x1 10 us: on_device(): down_sel = jnp.take(down_w[0], chosen, axis=0)]
    unnamed x18 -> x26, local copies, waits for them, and re-layouts: 1.7 us -> 27.3 us
    pallas_call x0 -> x6, Pallas kernels: none -> 16.8 us  [the longest x1 5.9 us: attend(): pl.pallas_call(functools.partial(attend_kernel, width // size), out_shape...]
    dot_general x5 -> x0, matrix products: 15 us -> none  [the longest x1 4.94 us: on_device(): jnp.einsum('bs,csu->bcu', arrived, gate_sel, preferred_element_type=jnp.f...]
    ppermute x9 -> x6, starting transfers between devices: 9.97 us -> 7.69 us  [from_partner(): return lax.ppermute(value, 'hid', pairs)]
    add x4 -> x3, other arithmetic: 2.39 us -> 0.17 us  [the longest x1 0.1 us: on_device(): part = part + from_partner(sent, 0).astype(jnp.float32)]
    convert_element_type x4 -> x1, other arithmetic: 1.86 us -> 0.03 us  [on_device(): hidden = jnp.where(active, jnp.maximum(part[:, :units], 0.0) * part[:, un...]
    lt x2 -> x1, other arithmetic: 1.49 us -> 0.01 us  [on_device(): active = lax.broadcasted_iota(jnp.int32, (1, units), 1) < live_count * unit]
  transfers between devices with their start and end apart: 10 -> 7, of which waited for: 5 -> 5; matrix products, arithmetic and copies ran while one was open for 35% -> 1% of each run, Pallas kernels for 0% -> 7%
where the time goes in v1:
time: 90.2 us; the launch traced here: 89.6 us
  local copies, waits for them, and re-layouts  28 us (31%)
  Pallas kernels  16.8 us (19%)
  starting transfers between devices  15.1 us (17%)
  waiting for transfers between devices  15 us (17%)
  blocking collectives  13.6 us (15%)
    unnamed x26, local copies, waits for them, and re-layouts  27.3 us
    ppermute x6, waiting for transfers between devices, from_partner(): return lax.ppermute(value, 'hid', pairs)  14.9 us
    all_to_all x1, blocking collectives, on_device(): lax.all_to_all(ffn_part.reshape(dev_count, rows_dev, slice_width), 'hid',...  13.6 us
    ppermute x6, starting transfers between devices, from_partner(): return lax.ppermute(value, 'hid', pairs)  7.69 us
    all_to_all x1, starting transfers between devices, on_device(): lax.all_to_all(send_tiles, 'hid', split_axis=0, concat_axis=0, tiled=True)  7.39 us
    pallas_call x1, Pallas kernels, attend(): pl.pallas_call(functools.partial(attend_kernel, width // size), out_shape...  5.9 us
    pallas_call x1, Pallas kernels, fetch_in(): pl.pallas_call(fetch_in_kernel, out_shape=jax.ShapeDtypeStruct((count, de...  4.37 us
    pallas_call x1, Pallas kernels, gate_up(): pl.pallas_call(gate_up_kernel, out_shape=(jax.ShapeDtypeStruct((rows // 2...  2.64 us
  transfers between devices with their start and end apart: 7, of which 5 were waited for; matrix products, arithmetic and copies ran while one was open for 1% of the time, Pallas kernels for 7%

profile of v1, /device:TPU:0, one launch (start us, length us, event | category | flops | bytes accessed | tf_op | source)
XLA Modules:
  0.0 89.6 jit_solution(18123347567893080701)
XLA Ops:
  0.0 1.4 %copy-done.4 = bf16[4,192,1024]{2,1,0:T(8,128)(2,1)S(1)} copy-done((bf16[4,192,1024]{2,1,0:T(8,128)(2,1)S(1)}, bf16[4,192,1024]{2,1,0:T(8,128)(2,1)}, u32[]{:S(2)}) %copy-start.4) | copy-done | bytes 1572888
  1.4 1.4 %copy-done.5 = bf16[4,192,1024]{2,1,0:T(8,128)(2,1)S(1)} copy-done((bf16[4,192,1024]{2,1,0:T(8,128)(2,1)S(1)}, bf16[4,192,1024]{2,1,0:T(8,128)(2,1)}, u32[]{:S(2)}) %copy-start.5) | copy-done | bytes 1572888
  2.8 0.8 copy-done.6
  3.7 0.8 copy-done.7
  4.5 0.8 copy-done.8
  5.3 0.7 copy-done.11
  5.9 5.9 %attend.1 = (f32[4,8192]{1,0:T(4,128)S(1)}, bf16[16,4,1024]{2,1,0:T(4,128)(2,1)}) custom-call(s32[4]{0:T(128)S(1)} %copy-done.11, bf16[4,64,128]{2,1,0:T(8,128)(2,1)S(1)} %copy-done.6, bf16[4,192,1024]{2,1,0:T(8,128)(2,1)S(1)} %copy-done.4, bf16[4,192,1024]{2,1,0:T(8,128)(2,1)S(1)} %copy-done.5, bf16[4,8192]{1,0:T(4,128)(2,1)S(1)} %copy-done.7, ...), custom_call_target="tpu_custom_call" | custom-call | tf_op jit(solution)/shard_map/attend/pallas_call | solution.py:72
  11.8 7.4 %all-to-all-start = ((bf16[16,4,1024]{2,1,0:T(4,128)(2,1)}), bf16[16,4,1024]{2,1,0:T(4,128)(2,1)S(1)}, u32[]{:S(2)}, u32[]{:S(2)}) async-start(bf16[16,4,1024]{2,1,0:T(4,128)(2,1)} %get-tuple-element.10), calls=%async_computation | async-start | bytes 262144 | tf_op jit(solution)/shard_map/all_to_all | solution.py:262
  19.2 5.2 %copy-done.2 = bf16[1,56,1024,128]{3,2,1,0:T(8,128)(2,1)S(1)} copy-done((bf16[1,56,1024,128]{3,2,1,0:T(8,128)(2,1)S(1)}, bf16[1,56,1024,128]{3,2,1,0:T(8,128)(2,1)}, u32[]{:S(2)}) %copy-start.2) | copy-done | bytes 14680088
  24.4 0.7 copy-done.9
  25.1 4.4 %fetch_in.1.both_ref = bf16[28,1024,256]{2,1,0:T(8,128)(2,1)S(1)} custom-call(s32[2,28]{1,0:T(2,128)S(1)} %copy-done.9, bf16[1,56,1024,128]{3,2,1,0:T(8,128)(2,1)S(1)} %copy-done.2, bf16[1,56,1024,128]{3,2,1,0:T(8,128)(2,1)} %up_hbm.1), custom_call_target="tpu_custom_call" | custom-call | bytes 29360128 | tf_op jit(solution)/shard_map/fetch_in/pallas_call | solution.py:116
  29.5 5.2 %copy-done = bf16[28,1024,256]{2,1,0:T(8,128)(2,1)} copy-done((bf16[28,1024,256]{2,1,0:T(8,128)(2,1)}, bf16[28,1024,256]{2,1,0:T(8,128)(2,1)S(1)}, u32[]{:S(2)}) %copy-start) | copy-done | bytes 14680088
  34.7 5.2 %copy-done.1 = bf16[28,1024,256]{2,1,0:T(8,128)(2,1)S(1)} copy-done((bf16[28,1024,256]{2,1,0:T(8,128)(2,1)S(1)}, bf16[28,1024,256]{2,1,0:T(8,128)(2,1)}, u32[]{:S(2)}) %copy-start.1) | copy-done | bytes 14680088
  39.9 2.6 %gate_up.1 = (f32[32,7168]{1,0:T(8,128)S(1)}, bf16[32,7168]{1,0:T(8,128)(2,1)S(1)}) custom-call(bf16[64,1024]{1,0:T(8,128)(2,1)S(1)} %reshape.17.x_ref, bf16[28,1024,256]{2,1,0:T(8,128)(2,1)S(1)} %copy-done.1), custom_call_target="tpu_custom_call" | custom-call | tf_op jit(solution)/shard_map/gate_up/pallas_call | solution.py:180
  42.5 0.5 collective-permute-start
  43.0 1.4 %collective-permute-done = bf16[32,7168]{1,0:T(8,128)(2,1)S(1)} collective-permute-done((bf16[32,7168]{1,0:T(8,128)(2,1)S(1)}, bf16[32,7168]{1,0:T(8,128)(2,1)S(1)}, u32[]{:S(2)}, u32[]{:S(2)}) %collective-permute-start) | collective-permute-done | bytes 458784 | tf_op jit(solution)/shard_map/ppermute | solution.py:20
  44.4 0.1 convert_add_fusion
  44.6 2.0 %collective-permute-start.1 = (bf16[16,7168]{1,0:T(8,128)(2,1)S(1)}, bf16[16,7168]{1,0:T(8,128)(2,1)S(1)}, u32[]{:S(2)}, u32[]{:S(2)}) collective-permute-start(bf16[16,7168]{1,0:T(8,128)(2,1)S(1)} %dynamic-slice_convert_fusion), channel_id=1, source_target_pairs={{0,2},{1,3},{2,0},{3,1},{4,6},{5,7},{6,4},{7,5},{8,10},{9,11},{10,... | collective-permute-start | bytes 688136 | tf_op jit(solution)/shard_map/ppermute | solution.py:20
  46.5 6.0 %collective-permute-done.1 = bf16[16,7168]{1,0:T(8,128)(2,1)S(1)} collective-permute-done((bf16[16,7168]{1,0:T(8,128)(2,1)S(1)}, bf16[16,7168]{1,0:T(8,128)(2,1)S(1)}, u32[]{:S(2)}, u32[]{:S(2)}) %collective-permute-start.1) | collective-permute-done | bytes 229408 | tf_op jit(solution)/shard_map/ppermute | solution.py:20
  52.6 1.7 %collective-permute-start.2 = (bf16[8,7168]{1,0:T(8,128)(2,1)S(1)}, bf16[8,7168]{1,0:T(8,128)(2,1)S(1)}, u32[]{:S(2)}, u32[]{:S(2)}) collective-permute-start(bf16[8,7168]{1,0:T(8,128)(2,1)S(1)} %dynamic-slice_convert_fusion.1), channel_id=1, source_target_pairs={{0,4},{1,5},{2,6},{3,7},{4,0},{5,1},{6,2},{7,3},{8,12},{9,13},{10,... | collective-permute-start | bytes 344072 | tf_op jit(solution)/shard_map/ppermute | solution.py:20
  54.4 0.6 dynamic_slice.16
  55.6 1.9 %collective-permute-done.2 = bf16[8,7168]{1,0:T(8,128)(2,1)S(1)} collective-permute-done((bf16[8,7168]{1,0:T(8,128)(2,1)S(1)}, bf16[8,7168]{1,0:T(8,128)(2,1)S(1)}, u32[]{:S(2)}, u32[]{:S(2)}) %collective-permute-start.2) | collective-permute-done | bytes 114720 | tf_op jit(solution)/shard_map/ppermute | solution.py:20
  57.5 1.7 %collective-permute-start.3 = (bf16[8,3584]{1,0:T(8,128)(2,1)S(1)}, bf16[8,3584]{1,0:T(8,128)(2,1)S(1)}, u32[]{:S(2)}, u32[]{:S(2)}) collective-permute-start(bf16[8,3584]{1,0:T(8,128)(2,1)S(1)} %fusion.1), channel_id=1, source_target_pairs={{0,4},{1,5},{2,6},{3,7},{4,0},{5,1},{6,2},{7,3},{8,12},{9,13},{10,... | collective-permute-start | bytes 172040 | tf_op jit(solution)/shard_map/ppermute | solution.py:20
  59.3 2.5 %collective-permute-done.3 = bf16[8,3584]{1,0:T(8,128)(2,1)S(1)} collective-permute-done((bf16[8,3584]{1,0:T(8,128)(2,1)S(1)}, bf16[8,3584]{1,0:T(8,128)(2,1)S(1)}, u32[]{:S(2)}, u32[]{:S(2)}) %collective-permute-start.3) | collective-permute-done | bytes 57376 | tf_op jit(solution)/shard_map/ppermute | solution.py:20
  61.8 1.7 %collective-permute-start.4 = (bf16[16,3584]{1,0:T(8,128)(2,1)S(1)}, bf16[16,3584]{1,0:T(8,128)(2,1)S(1)}, u32[]{:S(2)}, u32[]{:S(2)}) collective-permute-start(bf16[16,3584]{1,0:T(8,128)(2,1)S(1)} %maximum_select_fusion.2), channel_id=1, source_target_pairs={{0,2},{1,3},{2,0},{3,1},{4,6},{5,7},{6,4},{7,5},{8,10},{9,11},{10,... | collective-permute-start | bytes 344072 | tf_op jit(solution)/shard_map/ppermute | solution.py:20
  63.5 3.1 %collective-permute-done.4 = bf16[16,3584]{1,0:T(8,128)(2,1)S(1)} collective-permute-done((bf16[16,3584]{1,0:T(8,128)(2,1)S(1)}, bf16[16,3584]{1,0:T(8,128)(2,1)S(1)}, u32[]{:S(2)}, u32[]{:S(2)}) %collective-permute-start.4) | collective-permute-done | bytes 114720 | tf_op jit(solution)/shard_map/ppermute | solution.py:20
  66.8 5.2 %copy-done.3 = bf16[1,56,128,1024]{3,2,1,0:T(8,128)(2,1)S(1)} copy-done((bf16[1,56,128,1024]{3,2,1,0:T(8,128)(2,1)S(1)}, bf16[1,56,128,1024]{3,2,1,0:T(8,128)(2,1)}, u32[]{:S(2)}) %copy-start.3) | copy-done | bytes 14680088
  72.0 1.8 %fetch_down.1.w_ref = bf16[28,128,1024]{2,1,0:T(8,128)(2,1)S(1)} custom-call(s32[2,28]{1,0:T(2,128)S(1)} %copy-done.10, bf16[1,56,128,1024]{3,2,1,0:T(8,128)(2,1)S(1)} %copy-done.3), custom_call_target="tpu_custom_call" | custom-call | bytes 14680064 | tf_op jit(solution)/shard_map/fetch_down/pallas_call | solution.py:147
  73.8 0.1 maximum_select_fusion.h_ref
  73.9 1.4 %down.1 = bf16[64,1024]{1,0:T(8,128)(2,1)S(1)} custom-call(bf16[64,3584]{1,0:T(8,128)(2,1)S(1)} %maximum_select_fusion.h_ref, bf16[28,128,1024]{2,1,0:T(8,128)(2,1)S(1)} %fetch_down.1.w_ref), custom_call_target="tpu_custom_call" | custom-call | tf_op jit(solution)/shard_map/down/pallas_call | solution.py:205
  75.4 13.6 %all_to_all.10.back_ref = bf16[16,4,1024]{2,1,0:T(4,128)(2,1)S(1)} all-to-all(bf16[16,4,1024]{2,1,0:T(4,128)(2,1)S(1)} %reshape.18), channel_id=1, replica_groups=mesh['groups'=2,'hid'=16] {'hid'}, dimensions={0} | all-to-all | bytes 262144 | tf_op jit(solution)/shard_map/all_to_all | solution.py:290
  88.9 0.7 finish.1
  (28 shorter events, 0.4 us)
Async XLA Ops:
  0.0 1.4 %copy-start.4 = (bf16[4,192,1024]{2,1,0:T(8,128)(2,1)S(1)}, bf16[4,192,1024]{2,1,0:T(8,128)(2,1)}, u32[]{:S(2)}) copy-start(bf16[4,192,1024]{2,1,0:T(8,128)(2,1)} %k_hbm.1) | copy-start | bytes 4718596
  1.4 1.4 %copy-start.5 = (bf16[4,192,1024]{2,1,0:T(8,128)(2,1)S(1)}, bf16[4,192,1024]{2,1,0:T(8,128)(2,1)}, u32[]{:S(2)}) copy-start(bf16[4,192,1024]{2,1,0:T(8,128)(2,1)} %v_hbm.1) | copy-start | bytes 4718596
  2.8 0.8 copy-start.6
  3.7 0.8 copy-start.7
  4.5 0.8 copy-start.8
  5.3 0.7 copy-start.11
  11.8 22.9 %all-to-all-start = ((bf16[16,4,1024]{2,1,0:T(4,128)(2,1)}), bf16[16,4,1024]{2,1,0:T(4,128)(2,1)S(1)}, u32[]{:S(2)}, u32[]{:S(2)}) async-start(bf16[16,4,1024]{2,1,0:T(4,128)(2,1)} %get-tuple-element.10), calls=%async_computation | async-start | bytes 262144 | tf_op jit(solution)/shard_map/all_to_all | solution.py:262
  19.2 5.2 %copy-start.2 = (bf16[1,56,1024,128]{3,2,1,0:T(8,128)(2,1)S(1)}, bf16[1,56,1024,128]{3,2,1,0:T(8,128)(2,1)}, u32[]{:S(2)}) copy-start(bf16[1,56,1024,128]{3,2,1,0:T(8,128)(2,1)} %gate_hbm.1) | copy-start | bytes 44040196
  24.4 0.7 copy-start.9
  29.5 5.2 %copy-start = (bf16[28,1024,256]{2,1,0:T(8,128)(2,1)}, bf16[28,1024,256]{2,1,0:T(8,128)(2,1)S(1)}, u32[]{:S(2)}) copy-start(bf16[28,1024,256]{2,1,0:T(8,128)(2,1)S(1)} %fetch_in.1.both_ref) | copy-start | bytes 44040196
  34.7 19.7 %copy-start.12 = (s32[2]{0:T(128)S(1)}, s32[2]{0:T(128)}, u32[]{:S(2)}) copy-start(s32[2]{0:T(128)} %param.21) | copy-start | bytes 28
  34.7 32.1 %copy-start.10 = (s32[2,28]{1,0:T(2,128)S(1)}, s32[2,28]{1,0:T(2,128)}, u32[]{:S(2)}) copy-start(s32[2,28]{1,0:T(2,128)} %list_ref.3) | copy-start | bytes 676
  34.7 5.2 %copy-start.1 = (bf16[28,1024,256]{2,1,0:T(8,128)(2,1)S(1)}, bf16[28,1024,256]{2,1,0:T(8,128)(2,1)}, u32[]{:S(2)}) copy-start(bf16[28,1024,256]{2,1,0:T(8,128)(2,1)} %copy-done) | copy-start | bytes 44040196
  42.5 1.9 %collective-permute-start = (bf16[32,7168]{1,0:T(8,128)(2,1)S(1)}, bf16[32,7168]{1,0:T(8,128)(2,1)S(1)}, u32[]{:S(2)}, u32[]{:S(2)}) collective-permute-start(bf16[32,7168]{1,0:T(8,128)(2,1)S(1)} %get-tuple-element.12), channel_id=1, source_target_pairs={{0,1},{1,0},{2,3},{3,2},{4,5},{5,4},{6,7},{7,6},{8,9},{9,8},{10,11... | collective-permute-start | bytes 1376264 | tf_op jit(solution)/shard_map/ppermute | solution.py:20
  44.6 7.9 %collective-permute-start.1 = (bf16[16,7168]{1,0:T(8,128)(2,1)S(1)}, bf16[16,7168]{1,0:T(8,128)(2,1)S(1)}, u32[]{:S(2)}, u32[]{:S(2)}) collective-permute-start(bf16[16,7168]{1,0:T(8,128)(2,1)S(1)} %dynamic-slice_convert_fusion), channel_id=1, source_target_pairs={{0,2},{1,3},{2,0},{3,1},{4,6},{5,7},{6,4},{7,5},{8,10},{9,11},{10,... | collective-permute-start | bytes 688136 | tf_op jit(solution)/shard_map/ppermute | solution.py:20
  52.6 4.9 %collective-permute-start.2 = (bf16[8,7168]{1,0:T(8,128)(2,1)S(1)}, bf16[8,7168]{1,0:T(8,128)(2,1)S(1)}, u32[]{:S(2)}, u32[]{:S(2)}) collective-permute-start(bf16[8,7168]{1,0:T(8,128)(2,1)S(1)} %dynamic-slice_convert_fusion.1), channel_id=1, source_target_pairs={{0,4},{1,5},{2,6},{3,7},{4,0},{5,1},{6,2},{7,3},{8,12},{9,13},{10,... | collective-permute-start | bytes 344072 | tf_op jit(solution)/shard_map/ppermute | solution.py:20
  57.5 4.2 %collective-permute-start.3 = (bf16[8,3584]{1,0:T(8,128)(2,1)S(1)}, bf16[8,3584]{1,0:T(8,128)(2,1)S(1)}, u32[]{:S(2)}, u32[]{:S(2)}) collective-permute-start(bf16[8,3584]{1,0:T(8,128)(2,1)S(1)} %fusion.1), channel_id=1, source_target_pairs={{0,4},{1,5},{2,6},{3,7},{4,0},{5,1},{6,2},{7,3},{8,12},{9,13},{10,... | collective-permute-start | bytes 172040 | tf_op jit(solution)/shard_map/ppermute | solution.py:20
  61.8 4.9 %collective-permute-start.4 = (bf16[16,3584]{1,0:T(8,128)(2,1)S(1)}, bf16[16,3584]{1,0:T(8,128)(2,1)S(1)}, u32[]{:S(2)}, u32[]{:S(2)}) collective-permute-start(bf16[16,3584]{1,0:T(8,128)(2,1)S(1)} %maximum_select_fusion.2), channel_id=1, source_target_pairs={{0,2},{1,3},{2,0},{3,1},{4,6},{5,7},{6,4},{7,5},{8,10},{9,11},{10,... | collective-permute-start | bytes 344072 | tf_op jit(solution)/shard_map/ppermute | solution.py:20
  66.7 7.1 %collective-permute-start.5 = (bf16[32,3584]{1,0:T(8,128)(2,1)S(1)}, bf16[32,3584]{1,0:T(8,128)(2,1)S(1)}, u32[]{:S(2)}, u32[]{:S(2)}) collective-permute-start(bf16[32,3584]{1,0:T(8,128)(2,1)S(1)} %maximum_select_fusion.1), channel_id=1, source_target_pairs={{0,1},{1,0},{2,3},{3,2},{4,5},{5,4},{6,7},{7,6},{8,9},{9,8},{10,11... | collective-permute-start | bytes 688136 | tf_op jit(solution)/shard_map/ppermute | solution.py:20
  66.8 5.2 %copy-start.3 = (bf16[1,56,128,1024]{3,2,1,0:T(8,128)(2,1)S(1)}, bf16[1,56,128,1024]{3,2,1,0:T(8,128)(2,1)}, u32[]{:S(2)}) copy-start(bf16[1,56,128,1024]{3,2,1,0:T(8,128)(2,1)} %down_hbm.1) | copy-start | bytes 44040196

commit v2 on v0

v2 whole, which is shorter than its diff:
```python
import functools
import math

import jax
import jax.numpy as jnp
from jax import lax
from jax.experimental import pallas as pl
from jax.experimental.pallas import tpu as pltpu
from jax.sharding import PartitionSpec as P

MDL = 8
VMEM = pl.BlockSpec(memory_space=pltpu.VMEM)
HBM = pl.BlockSpec(memory_space=pltpu.HBM)
ANY = pl.BlockSpec(memory_space=pl.ANY)


CORES = 2
CHIPS = MDL // CORES


def from_partner(value, mask):
    pairs = [(source, source ^ mask) for source in range(lax.axis_size("hid"))]
    return lax.ppermute(value, "hid", pairs)


def place():
    at = lax.axis_index("hid")
    return at // MDL, at // CORES % CHIPS, at % CORES


def in_hbm(value):
    return pltpu.with_memory_space_constraint(value, pltpu.HBM)


def attend_kernel(
    kv_count,
    len_hbm,
    q_hbm,
    k_hbm,
    v_hbm,
    res_hbm,
    gain_hbm,
    mixed_ref,
    kept_ref,
    sent_ref,
    len_ref,
    q_ref,
    k_buf,
    v_buf,
    res_ref,
    gain_ref,
    sems,
):
    rows, heads, size = q_ref.shape
    slots = k_buf.shape[1]
    width = kv_count * size
    per_kv = heads // kv_count
    lines = heads * rows
    pairs = [
        (len_hbm, len_ref),
        (q_hbm, q_ref),
        (k_hbm, k_buf),
        (v_hbm, v_buf),
        (res_hbm, res_ref),
        (gain_hbm, gain_ref),
    ]
    copies = [pltpu.make_async_copy(s, d, sems.at[i]) for i, (s, d) in enumerate(pairs)]
    for copy in copies:
        copy.start()
    line = lax.broadcasted_iota(jnp.int32, (lines, lines), 0)
    taken = lax.broadcasted_iota(jnp.int32, (lines, lines), 1)
    swap = (taken == line % rows * heads + line // rows).astype(jnp.float32).astype(jnp.bfloat16)
    own = (
        lax.broadcasted_iota(jnp.int32, (lines, width), 0) // (per_kv * rows)
        == lax.broadcasted_iota(jnp.int32, (lines, width), 1) // size
    )
    copies[0].wait()
    request = lax.broadcasted_iota(jnp.int32, (lines, 1), 0) % rows
    first = request * slots
    stop = first
    for r in range(rows):
        stop = jnp.where(request == r, r * slots + len_ref[r], stop)
    slot = lax.broadcasted_iota(jnp.int32, (lines, rows * slots), 1)
    valid = (slot >= first) & (slot < stop)
    copies[1].wait()
    q = jnp.dot(
        swap, q_ref[...].reshape(lines, size), preferred_element_type=jnp.float32
    ).astype(jnp.bfloat16)
    wide = jnp.where(own, jnp.concatenate([q] * kv_count, axis=1), jnp.zeros((), jnp.bfloat16))
    copies[2].wait()
    scores = lax.dot_general(
        wide,
        k_buf[...].reshape(rows * slots, width),
        (((1,), (1,)), ((), ())),
        preferred_element_type=jnp.float32,
    ) * (1.0 / math.sqrt(size))
    scores = jnp.where(valid, scores, -1e30)
    top = jnp.max(scores, axis=1, keepdims=True)
    terms = jnp.where(valid, jnp.exp(scores - top), 0.0)
    probs = (terms / jnp.sum(terms, axis=1, keepdims=True)).astype(jnp.bfloat16)
    copies[3].wait()
    values = v_buf[...].reshape(rows * slots, width)
    for j in range(kv_count):
        span = per_kv * rows
        piece = jnp.dot(
            probs[j * span : (j + 1) * span],
            values[:, j * size : (j + 1) * size],
            preferred_element_type=jnp.float32,
        )
        for i in range(per_kv):
            h = j * per_kv + i
            mixed_ref[:, h * size : (h + 1) * size] = piece[i * rows : (i + 1) * rows]
    copies[4].wait()
    copies[5].wait()
    mixed = mixed_ref[...] + res_ref[...].astype(jnp.float32)
    mixed_ref[...] = mixed
    mean_sq = jnp.mean(mixed * mixed, axis=1, keepdims=True)
    normed = (mixed * lax.rsqrt(mean_sq + 1e-05) * gain_ref[...]).astype(jnp.bfloat16)
    _, chip, core = place()
    step = kept_ref.shape[2]
    for q in range(CHIPS):
        first = normed[:, 2 * q * step : (2 * q + 1) * step]
        second = normed[:, (2 * q + 1) * step : (2 * q + 2) * step]
        kept_ref[q ^ chip] = jnp.where(core == 0, first, second)
        sent_ref[q ^ chip] = jnp.where(core == 0, second, first)


def attend(queries, k_cache, v_cache, lengths, residual_in, norm_gain):
    rows, heads, size = queries.shape
    slots, width = k_cache.shape[1:]
    model = residual_in.shape[1]
    return pl.pallas_call(
        functools.partial(attend_kernel, width // size),
        out_shape=(
            pltpu.VMEM((rows, model), jnp.float32),
            pltpu.VMEM((CHIPS, rows, model // MDL), jnp.bfloat16),
            pltpu.VMEM((CHIPS, rows, model // MDL), jnp.bfloat16),
        ),
        in_specs=[HBM] * 6,
        out_specs=(VMEM,) * 3,
        scratch_shapes=[
            pltpu.SMEM((rows,), jnp.int32),
            pltpu.VMEM((rows, heads, size), jnp.bfloat16),
            pltpu.VMEM((rows, slots, width), jnp.bfloat16),
            pltpu.VMEM((rows, slots, width), jnp.bfloat16),
            pltpu.VMEM((rows, model), jnp.bfloat16),
            pltpu.VMEM((1, model), jnp.float32),
            pltpu.SemaphoreType.DMA((6,)),
        ],
        compiler_params=pltpu.CompilerParams(vmem_limit_bytes=20 * 2**20),
        name="attend",
    )(
        *(
            in_hbm(value)
            for value in (
                lengths,
                queries,
                k_cache,
                v_cache,
                residual_in,
                norm_gain.reshape(1, model),
            )
        )
    )


def fetch_kernel(list_hbm, count_hbm, w_hbm, _, out_ref, __, list_ref, count_ref, sems):
    copies = [
        pltpu.make_async_copy(list_hbm, list_ref, sems.at[0]),
        pltpu.make_async_copy(count_hbm, count_ref, sems.at[1]),
    ]
    for copy in copies:
        copy.start()
    for copy in copies:
        copy.wait()
    group, _, _ = place()
    live = count_ref[group]

    def fetched(c):
        return pltpu.make_async_copy(w_hbm.at[0, list_ref[group, c]], out_ref.at[c], sems.at[c])

    @pl.loop(0, live)
    def _(c):
        fetched(c).start()

    @pl.loop(live, out_ref.shape[0])
    def _(c):
        out_ref[c] = jnp.zeros(out_ref.shape[1:], out_ref.dtype)

    @pl.loop(0, live)
    def _(c):
        fetched(c).wait()


def fetch(block_list, block_count, weights, held, name):
    count = block_list.shape[1]
    size = math.prod(weights.shape[2:])
    return pl.pallas_call(
        fetch_kernel,
        out_shape=(
            pltpu.VMEM((count,) + weights.shape[2:], jnp.bfloat16),
            jax.ShapeDtypeStruct(held.shape, held.dtype),
        ),
        in_specs=[HBM] * 3 + [ANY],
        out_specs=(VMEM, ANY),
        input_output_aliases={3: 1},
        scratch_shapes=[
            pltpu.SMEM(block_list.shape, jnp.int32),
            pltpu.SMEM(block_count.shape, jnp.int32),
            pltpu.SemaphoreType.DMA((count,)),
        ],
        compiler_params=pltpu.CompilerParams(vmem_limit_bytes=10 * 2**20),
        cost_estimate=pl.CostEstimate(flops=0, bytes_accessed=4 * count * size, transcendentals=0),
        name=name,
    )(in_hbm(block_list), in_hbm(block_count), in_hbm(weights), held)


def gate_up_kernel(arrived_ref, gate_ref, up_ref, keep_ref, sent_ref, x_ref):
    groups, _, _, rows, _ = arrived_ref.shape
    half = keep_ref.shape[0]
    count, _, unit = gate_ref.shape
    for core in range(CORES):
        for chip in range(CHIPS):
            for group in range(groups):
                at = ((core * CHIPS + chip) * groups + group) * rows
                x_ref[at : at + rows, :] = arrived_ref[group, chip, core].astype(jnp.float32)
    x = x_ref[...].astype(jnp.bfloat16)
    for c in range(count):
        both = jnp.concatenate([gate_ref[c], up_ref[c]], axis=1)
        pair = jnp.dot(x, both, preferred_element_type=jnp.float32)
        for k in range(2):
            part = pair[:, k * unit : (k + 1) * unit]
            at = pl.ds((k * count + c) * unit, unit)
            keep_ref[:, at] = part[:half]
            sent_ref[:, at] = part[half:].astype(jnp.bfloat16)


def gate_up(arrived, gate, up):
    rows = math.prod(arrived.shape[:4])
    count, depth, unit = gate.shape
    return pl.pallas_call(
        gate_up_kernel,
        out_shape=(
            pltpu.VMEM((rows // 2, 2 * count * unit), jnp.float32),
            pltpu.VMEM((rows // 2, 2 * count * unit), jnp.bfloat16),
        ),
        in_specs=[VMEM] * 3,
        out_specs=(VMEM, VMEM),
        scratch_shapes=[pltpu.VMEM((rows, depth), jnp.float32)],
        compiler_params=pltpu.CompilerParams(vmem_limit_bytes=24 * 2**20),
        name="gate_up",
    )(arrived, gate, up)


def down_kernel(near_ref, far_ref, w_ref, out_ref):
    count, unit, depth = w_ref.shape
    devices, rows, _ = out_ref.shape
    groups = devices // MDL
    group, chip, core = place()
    hidden = jnp.concatenate([near_ref[...], far_ref[...]], axis=0)
    step = min(512, depth)
    for n in range(depth // step):
        at = pl.ds(n * step, step)
        w = w_ref[:, :, at].reshape(count * unit, step)
        total = jnp.dot(hidden, w, preferred_element_type=jnp.float32)
        for r in range(devices):
            c, q, g = r // (CHIPS * groups), r // groups % CHIPS, r % groups
            owner = (group ^ g) * MDL + (chip ^ q) * CORES + (core ^ c)
            out_ref[owner, :, at] = total[r * rows : (r + 1) * rows].astype(jnp.bfloat16)


def down(near, far, weights, devices):
    rows = 2 * near.shape[0] // devices
    return pl.pallas_call(
        down_kernel,
        out_shape=pltpu.VMEM((devices, rows, weights.shape[2]), jnp.bfloat16),
        in_specs=[VMEM] * 3,
        out_specs=VMEM,
        compiler_params=pltpu.CompilerParams(vmem_limit_bytes=20 * 2**20),
        name="down",
    )(near, far, weights)


def finish_kernel(mixed_ref, back_ref, out_ref):
    step = back_ref.shape[2]
    for m in range(MDL):
        total = mixed_ref[:, m * step : (m + 1) * step]
        for g in range(back_ref.shape[0] // MDL):
            total = total + back_ref[g * MDL + m].astype(jnp.float32)
        out_ref[:, m * step : (m + 1) * step] = total.astype(jnp.bfloat16)


def finish(mixed, back):
    return pl.pallas_call(
        finish_kernel,
        out_shape=jax.ShapeDtypeStruct(mixed.shape, jnp.bfloat16),
        in_specs=[VMEM, VMEM],
        out_specs=VMEM,
        compiler_params=pltpu.CompilerParams(vmem_limit_bytes=16 * 2**20),
        name="finish",
    )(mixed, back)


def on_device(
    queries,
    k_cache,
    v_cache,
    lengths,
    residual_in,
    norm_gain,
    gate_w,
    up_w,
    down_w,
    block_list,
    block_count,
):
    dev_count = lax.axis_size("hid")
    group_total = dev_count // MDL
    rows_dev = queries.shape[0]
    units = block_list.shape[1] * gate_w.shape[3]
    masks = [chip * CORES for chip in range(CHIPS)]
    far_first = range(CHIPS - 1, 0, -1)

    mixed_rows, kept, sent = attend(queries, k_cache, v_cache, lengths, residual_in, norm_gain)
    pair = jnp.stack([kept, from_partner(sent, 1)], axis=1)
    came = {chip: from_partner(pair[chip], masks[chip]) for chip in far_first}
    gate, own = fetch(block_list, block_count, gate_w, pair[0], "fetch_gate")
    arrived = jnp.stack([own] + [came[chip] for chip in range(1, CHIPS)])[None]
    came = from_partner(arrived, MDL)
    up, arrived = fetch(block_list, block_count, up_w, arrived, "fetch_up")
    arrived = jnp.concatenate([arrived, came], axis=0)
    for level in range(1, group_total.bit_length() - 1):
        arrived = jnp.concatenate([arrived, from_partner(arrived, MDL << level)], axis=0)

    part, sent = gate_up(arrived, gate, up)
    part = part + from_partner(sent, 1).astype(jnp.float32)
    part = part.reshape(CHIPS, group_total * rows_dev, 2 * units)
    came = [from_partner(part[chip].astype(jnp.bfloat16), masks[chip]) for chip in far_first]
    down_rows, total = fetch(block_list, block_count, down_w, part[0], "fetch_down")
    for piece in came:
        total = total + piece.astype(jnp.float32)
    hidden = (jnp.maximum(total[:, :units], 0.0) * total[:, units:]).astype(jnp.bfloat16)

    came = {chip: from_partner(hidden, masks[chip]) for chip in far_first}
    near = jnp.concatenate([hidden] + [came[chip] for chip in range(1, CHIPS)], axis=0)
    far = from_partner(near, 1)
    ffn_part = down(near, far, down_rows, dev_count)
    returned = lax.all_to_all(ffn_part, "hid", split_axis=0, concat_axis=0, tiled=True)
    return finish(mixed_rows, returned)


def solution(mesh):
    in_specs = (
        P(("groups", "hid"), None, None),
        P(("groups", "hid"), None, None),
        P(("groups", "hid"), None, None),
        P(("groups", "hid")),
        P(("groups", "hid"), None),
        P(),
        P("hid", None, None, None),
        P("hid", None, None, None),
        P("hid", None, None, None),
        P("groups", None),
        P("groups"),
    )
    out_specs = P(("groups", "hid"), None)
    return jax.shard_map(
        on_device, mesh=mesh, in_specs=in_specs, out_specs=out_specs, check_vma=False
    )
```

time: 104 us -> 61 us (0.59)
  local copies, waits for them, and re-layouts: 34.4 us -> 0.04 us
  Pallas kernels: 0 us -> 17.3 us
  matrix products: 15 us -> 0 us
  other arithmetic: 8.2 us -> 0.37 us
  waiting for transfers between devices: 15 us -> 12.8 us
  starting transfers between devices: 17.4 us -> 15.7 us
    gather x3 -> x0, local copies, waits for them, and re-layouts: 29.9 us -> none  [the longest x1 10 us: on_device(): down_sel = jnp.take(down_w[0], chosen, axis=0)]
    pallas_call x0 -> x7, Pallas kernels: none -> 17.3 us  [the longest x3 9.37 us: fetch(): pl.pallas_call(fetch_kernel, out_shape=(pltpu.VMEM((count,) + weights.sha...]
    dot_general x5 -> x0, matrix products: 15 us -> none  [the longest x1 4.94 us: on_device(): jnp.einsum('bs,csu->bcu', arrived, gate_sel, preferred_element_type=jnp.f...]
    all_to_all x1 -> x0, starting transfers between devices: 7.39 us -> none  [on_device(): lax.all_to_all(send_tiles, 'hid', split_axis=1, concat_axis=0, tiled=True)]
    ppermute x9 -> x13, starting transfers between devices: 9.97 us -> 15.7 us  [from_partner(): return lax.ppermute(value, 'hid', pairs)]
    add x4 -> x1, other arithmetic: 2.39 us -> 0.05 us  [on_device(): total = total + piece.astype(jnp.float32)]
    ppermute x9 -> x13, waiting for transfers between devices: 15 us -> 12.8 us  [from_partner(): return lax.ppermute(value, 'hid', pairs)]
    convert_element_type x4 -> x1, other arithmetic: 1.86 us -> 0.02 us  [on_device(): (jnp.maximum(total[:, :units], 0.0) * total[:, units:]).astype(jnp.bfloat16)]
  transfers between devices with their start and end apart: 10 -> 13, of which waited for: 5 -> 10; matrix products, arithmetic and copies ran while one was open for 35% -> 0% of each run, Pallas kernels for 0% -> 10%
where the time goes in v2:
time: 61 us; the launch traced here: 60.7 us
  Pallas kernels  17.3 us (28%)
  starting transfers between devices  15.7 us (26%)
  blocking collectives  14.3 us (23%)
  waiting for transfers between devices  12.8 us (21%)
    ppermute x13, starting transfers between devices, from_partner(): return lax.ppermute(value, 'hid', pairs)  15.7 us
    all_to_all x1, blocking collectives, on_device(): lax.all_to_all(ffn_part, 'hid', split_axis=0, concat_axis=0, tiled=True)  14.3 us
    ppermute x13, waiting for transfers between devices, from_partner(): return lax.ppermute(value, 'hid', pairs)  12.8 us
    pallas_call x3, Pallas kernels, fetch(): pl.pallas_call(fetch_kernel, out_shape=(pltpu.VMEM((count,) + weights.sha...  9.37 us
    pallas_call x1, Pallas kernels, attend(): pl.pallas_call(functools.partial(attend_kernel, width // size), out_shape...  3.28 us
    pallas_call x1, Pallas kernels, gate_up(): pl.pallas_call(gate_up_kernel, out_shape=(pltpu.VMEM((rows // 2, 2 * coun...  2.63 us
    pallas_call x1, Pallas kernels, down(): pl.pallas_call(down_kernel, out_shape=pltpu.VMEM((devices, rows, weights....  1.38 us
  transfers between devices with their start and end apart: 13, of which 10 were waited for; matrix products, arithmetic and copies ran while one was open for 0% of the time, Pallas kernels for 10%

profile of v2, /device:TPU:0, one launch (start us, length us, event | category | flops | bytes accessed | tf_op | source)
XLA Modules:
  0.0 60.7 jit_solution(9258607833233651493)
XLA Ops:
  0.0 3.3 %attend.1 = (f32[4,8192]{1,0:T(4,128)S(1)}, bf16[4,4,1024]{2,1,0:T(4,128)(2,1)S(1)}, bf16[4,4,1024]{2,1,0:T(4,128)(2,1)S(1)}) custom-call(s32[4]{0:T(128)} %len_hbm.1, bf16[4,64,128]{2,1,0:T(8,128)(2,1)} %q_hbm.1, bf16[4,192,1024]{2,1,0:T(8,128)(2,1)} %k_hbm.1, bf16[4,192,1024]{2,1,0:T(8,128)(2,1)} %v_hbm.1, bf16[4,8192]{1,0:T(4,128)(2,1)} %res_hbm.1, ...), custom_call_target="tpu_custom_call" | custom-call | tf_op jit(solution)/shard_map/attend/pallas_call | solution.py:132
  3.3 0.5 collective-permute-start
  3.8 0.9 %collective-permute-done = bf16[4,4,1024]{2,1,0:T(4,128)(2,1)S(1)} collective-permute-done((bf16[4,4,1024]{2,1,0:T(4,128)(2,1)S(1)}, bf16[4,4,1024]{2,1,0:T(4,128)(2,1)S(1)}, u32[]{:S(2)}, u32[]{:S(2)}) %collective-permute-start) | collective-permute-done | bytes 32800 | tf_op jit(solution)/shard_map/ppermute | solution.py:23
  4.7 2.9 %collective-permute-start.1 = (bf16[2,4,1024]{2,1,0:T(4,128)(2,1)S(1)}, bf16[2,4,1024]{2,1,0:T(4,128)(2,1)S(1)}, u32[]{:S(2)}, u32[]{:S(2)}) collective-permute-start(bf16[2,4,1024]{2,1,0:T(4,128)(2,1)S(1)} %get-tuple-element.33), channel_id=1, source_target_pairs={{0,2},{1,3},{2,0},{3,1},{4,6},{5,7},{6,4},{7,5},{8,10},{9,11},{10,... | collective-permute-start | bytes 49160 | tf_op jit(solution)/shard_map/ppermute | solution.py:23
  7.6 1.5 %collective-permute-start.3 = (bf16[2,4,1024]{2,1,0:T(4,128)(2,1)S(1)}, bf16[2,4,1024]{2,1,0:T(4,128)(2,1)S(1)}, u32[]{:S(2)}, u32[]{:S(2)}) collective-permute-start(bf16[2,4,1024]{2,1,0:T(4,128)(2,1)S(1)} %get-tuple-element.34), channel_id=1, source_target_pairs={{0,6},{1,7},{2,4},{3,5},{4,2},{5,3},{6,0},{7,1},{8,14},{9,15},{10,... | collective-permute-start | bytes 49160 | tf_op jit(solution)/shard_map/ppermute | solution.py:23
  9.2 3.1 %fetch_gate.1 = (bf16[28,1024,128]{2,1,0:T(8,128)(2,1)S(1)}, bf16[2,4,1024]{2,1,0:T(4,128)(2,1)S(1)}) custom-call(s32[2,28]{1,0:T(2,128)} %list_hbm.5, s32[2]{0:T(128)} %count_hbm.5, bf16[1,56,1024,128]{3,2,1,0:T(8,128)(2,1)} %w_hbm.3, bf16[2,4,1024]{2,1,0:T(4,128)(2,1)S(1)} %get-tuple-element.32._), custom_call_target="tpu_custom_call", output_to_operand_aliasing={{1}: (3, {})} | custom-call | bytes 14680064 | tf_op jit(solution)/shard_map/fetch_gate/pallas_call | solution.py:198
  12.4 0.5 collective-permute-done.2
  13.0 3.5 %collective-permute-start.4 = (bf16[1,4,2,4,1024]{4,3,2,1,0:T(4,128)(2,1)S(1)}, bf16[1,4,2,4,1024]{4,3,2,1,0:T(4,128)(2,1)S(1)}, u32[]{:S(2)}, u32[]{:S(2)}) collective-permute-start(bf16[1,4,2,4,1024]{4,3,2,1,0:T(4,128)(2,1)S(1)} %maximum_bitcast_fusion._), channel_id=1, source_target_pairs={{0,8},{1,9},{2,10},{3,11},{4,12},{5,13},{6,14},{7,15},{8,0},{9,1},... | collective-permute-start | bytes 196616 | tf_op jit(solution)/shard_map/ppermute | solution.py:23
  16.4 2.6 %collective-permute-done.4 = bf16[1,4,2,4,1024]{4,3,2,1,0:T(4,128)(2,1)S(1)} collective-permute-done((bf16[1,4,2,4,1024]{4,3,2,1,0:T(4,128)(2,1)S(1)}, bf16[1,4,2,4,1024]{4,3,2,1,0:T(4,128)(2,1)S(1)}, u32[]{:S(2)}, u32[]{:S(2)}) %collective-permute-start.4) | collective-permute-done | bytes 65568 | tf_op jit(solution)/shard_map/ppermute | solution.py:23
  19.0 3.1 %fetch_up.1 = (bf16[28,1024,128]{2,1,0:T(8,128)(2,1)S(1)}, bf16[1,4,2,4,1024]{4,3,2,1,0:T(4,128)(2,1)S(1)}) custom-call(s32[2,28]{1,0:T(2,128)} %list_hbm.5, s32[2]{0:T(128)} %count_hbm.5, bf16[1,56,1024,128]{3,2,1,0:T(8,128)(2,1)} %w_hbm.4, bf16[1,4,2,4,1024]{4,3,2,1,0:T(4,128)(2,1)S(1)} %maximum_bitcast_fusion._), custom_call_target="tpu_custom_call", output_to_operand_aliasing={{1}: (3, {})} | custom-call | bytes 14680064 | tf_op jit(solution)/shard_map/fetch_up/pallas_call | solution.py:198
  22.2 0.1 pad_maximum_fusion.1.arrived_ref
  22.3 2.6 %gate_up.1 = (f32[32,7168]{1,0:T(8,128)S(1)}, bf16[32,7168]{1,0:T(8,128)(2,1)S(1)}) custom-call(bf16[2,4,2,4,1024]{4,3,2,1,0:T(4,128)(2,1)S(1)} %pad_maximum_fusion.1.arrived_ref, bf16[28,1024,128]{2,1,0:T(8,128)(2,1)S(1)} %get-tuple-element.21.gate_ref, bf16[28,1024,128]{2,1,0:T(8,128)(2,1)S(1)} %get-tuple-element.22.up_ref), custom_call_target="tpu_custom_call" | custom-call | tf_op jit(solution)/shard_map/gate_up/pallas_call | solution.py:241
  24.9 0.1 collective-permute-start.5
  25.0 1.8 %collective-permute-done.5 = bf16[32,7168]{1,0:T(8,128)(2,1)S(1)} collective-permute-done((bf16[32,7168]{1,0:T(8,128)(2,1)S(1)}, bf16[32,7168]{1,0:T(8,128)(2,1)S(1)}, u32[]{:S(2)}, u32[]{:S(2)}) %collective-permute-start.5) | collective-permute-done | bytes 458784 | tf_op jit(solution)/shard_map/ppermute | solution.py:23
  26.8 0.1 fusion.8
  26.9 2.4 %collective-permute-start.6 = (bf16[8,7168]{1,0:T(8,128)(2,1)S(1)}, bf16[8,7168]{1,0:T(8,128)(2,1)S(1)}, u32[]{:S(2)}, u32[]{:S(2)}) collective-permute-start(bf16[8,7168]{1,0:T(8,128)(2,1)S(1)} %get-tuple-element.29), channel_id=1, source_target_pairs={{0,6},{1,7},{2,4},{3,5},{4,2},{5,3},{6,0},{7,1},{8,14},{9,15},{10,... | collective-permute-start | bytes 344072 | tf_op jit(solution)/shard_map/ppermute | solution.py:23
  29.3 0.5 collective-permute-start.8
  29.8 0.7 %collective-permute-start.7 = (bf16[8,7168]{1,0:T(8,128)(2,1)S(1)}, bf16[8,7168]{1,0:T(8,128)(2,1)S(1)}, u32[]{:S(2)}, u32[]{:S(2)}) collective-permute-start(bf16[8,7168]{1,0:T(8,128)(2,1)S(1)} %get-tuple-element.31), channel_id=1, source_target_pairs={{0,4},{1,5},{2,6},{3,7},{4,0},{5,1},{6,2},{7,3},{8,12},{9,13},{10,... | collective-permute-start | bytes 344072 | tf_op jit(solution)/shard_map/ppermute | solution.py:23
  30.5 3.1 %fetch_down.1 = (bf16[28,128,1024]{2,1,0:T(8,128)(2,1)S(1)}, f32[8,7168]{1,0:T(8,128)S(1)}) custom-call(s32[2,28]{1,0:T(2,128)} %list_hbm.5, s32[2]{0:T(128)} %count_hbm.5, bf16[1,56,128,1024]{3,2,1,0:T(8,128)(2,1)} %w_hbm.5, f32[8,7168]{1,0:T(8,128)S(1)} %slice.53._), custom_call_target="tpu_custom_call", output_to_operand_aliasing={{1}: (3, {})} | custom-call | bytes 14680064 | tf_op jit(solution)/shard_map/fetch_down/pallas_call | solution.py:198
  33.6 1.9 %collective-permute-done.8 = bf16[8,7168]{1,0:T(8,128)(2,1)S(1)} collective-permute-done((bf16[8,7168]{1,0:T(8,128)(2,1)S(1)}, bf16[8,7168]{1,0:T(8,128)(2,1)S(1)}, u32[]{:S(2)}, u32[]{:S(2)}) %collective-permute-start.8) | collective-permute-done | bytes 114720 | tf_op jit(solution)/shard_map/ppermute | solution.py:23
  35.5 0.1 collective-permute-done.7
  35.7 1.8 %collective-permute-start.11 = (bf16[8,3584]{1,0:T(8,128)(2,1)S(1)}, bf16[8,3584]{1,0:T(8,128)(2,1)S(1)}, u32[]{:S(2)}, u32[]{:S(2)}) collective-permute-start(bf16[8,3584]{1,0:T(8,128)(2,1)S(1)} %fusion), channel_id=1, source_target_pairs={{0,6},{1,7},{2,4},{3,5},{4,2},{5,3},{6,0},{7,1},{8,14},{9,15},{10,... | collective-permute-start | bytes 172040 | tf_op jit(solution)/shard_map/ppermute | solution.py:23
  37.4 1.2 %collective-permute-start.10 = (bf16[8,3584]{1,0:T(8,128)(2,1)S(1)}, bf16[8,3584]{1,0:T(8,128)(2,1)S(1)}, u32[]{:S(2)}, u32[]{:S(2)}) collective-permute-start(bf16[8,3584]{1,0:T(8,128)(2,1)S(1)} %fusion), channel_id=1, source_target_pairs={{0,4},{1,5},{2,6},{3,7},{4,0},{5,1},{6,2},{7,3},{8,12},{9,13},{10,... | collective-permute-start | bytes 172040 | tf_op jit(solution)/shard_map/ppermute | solution.py:23
  38.7 0.6 collective-permute-start.9
  39.2 2.1 %collective-permute-done.11 = bf16[8,3584]{1,0:T(8,128)(2,1)S(1)} collective-permute-done((bf16[8,3584]{1,0:T(8,128)(2,1)S(1)}, bf16[8,3584]{1,0:T(8,128)(2,1)S(1)}, u32[]{:S(2)}, u32[]{:S(2)}) %collective-permute-start.11) | collective-permute-done | bytes 57376 | tf_op jit(solution)/shard_map/ppermute | solution.py:23
  41.4 0.3 collective-permute-done.10
  41.7 1.1 %collective-permute-done.9 = bf16[8,3584]{1,0:T(8,128)(2,1)S(1)} collective-permute-done((bf16[8,3584]{1,0:T(8,128)(2,1)S(1)}, bf16[8,3584]{1,0:T(8,128)(2,1)S(1)}, u32[]{:S(2)}, u32[]{:S(2)}) %collective-permute-start.9) | collective-permute-done | bytes 57376 | tf_op jit(solution)/shard_map/ppermute | solution.py:23
  42.9 0.1 collective-permute-start.12
  42.9 1.5 %collective-permute-done.12.far_ref = bf16[32,3584]{1,0:T(8,128)(2,1)S(1)} collective-permute-done((bf16[32,3584]{1,0:T(8,128)(2,1)S(1)}, bf16[32,3584]{1,0:T(8,128)(2,1)S(1)}, u32[]{:S(2)}, u32[]{:S(2)}) %collective-permute-start.12) | collective-permute-done | bytes 229408 | tf_op jit(solution)/shard_map/ppermute | solution.py:23
  44.4 1.4 %down.1 = bf16[16,4,1024]{2,1,0:T(4,128)(2,1)S(1)} custom-call(bf16[32,3584]{1,0:T(8,128)(2,1)S(1)} %pad_maximum_fusion.near_ref, bf16[32,3584]{1,0:T(8,128)(2,1)S(1)} %collective-permute-done.12.far_ref, bf16[28,128,1024]{2,1,0:T(8,128)(2,1)S(1)} %get-tuple-element.26.w_ref), custom_call_target="tpu_custom_call" | custom-call | tf_op jit(solution)/shard_map/down/pallas_call | solution.py:274
  45.8 14.3 %all_to_all.5.back_ref = bf16[16,4,1024]{2,1,0:T(4,128)(2,1)S(1)} all-to-all(bf16[16,4,1024]{2,1,0:T(4,128)(2,1)S(1)} %down.1), channel_id=1, replica_groups=mesh['groups'=2,'hid'=16] {'hid'}, dimensions={0} | all-to-all | bytes 262144 | tf_op jit(solution)/shard_map/all_to_all | solution.py:348
  60.1 0.7 %finish.1 = bf16[4,8192]{1,0:T(4,128)(2,1)} custom-call(f32[4,8192]{1,0:T(4,128)S(1)} %get-tuple-element.16.mixed_ref, bf16[16,4,1024]{2,1,0:T(4,128)(2,1)S(1)} %all_to_all.5.back_ref), custom_call_target="tpu_custom_call" | custom-call | tf_op jit(solution)/shard_map/finish/pallas_call | solution.py:294
  (11 shorter events, 0.3 us)
Async XLA Ops:
  3.3 1.4 %collective-permute-start = (bf16[4,4,1024]{2,1,0:T(4,128)(2,1)S(1)}, bf16[4,4,1024]{2,1,0:T(4,128)(2,1)S(1)}, u32[]{:S(2)}, u32[]{:S(2)}) collective-permute-start(bf16[4,4,1024]{2,1,0:T(4,128)(2,1)S(1)} %get-tuple-element.18), channel_id=1, source_target_pairs={{0,1},{1,0},{2,3},{3,2},{4,5},{5,4},{6,7},{7,6},{8,9},{9,8},{10,11... | collective-permute-start | bytes 98312 | tf_op jit(solution)/shard_map/ppermute | solution.py:23
  4.7 7.6 %collective-permute-start.1 = (bf16[2,4,1024]{2,1,0:T(4,128)(2,1)S(1)}, bf16[2,4,1024]{2,1,0:T(4,128)(2,1)S(1)}, u32[]{:S(2)}, u32[]{:S(2)}) collective-permute-start(bf16[2,4,1024]{2,1,0:T(4,128)(2,1)S(1)} %get-tuple-element.33), channel_id=1, source_target_pairs={{0,2},{1,3},{2,0},{3,1},{4,6},{5,7},{6,4},{7,5},{8,10},{9,11},{10,... | collective-permute-start | bytes 49160 | tf_op jit(solution)/shard_map/ppermute | solution.py:23
  7.6 4.7 %collective-permute-start.3 = (bf16[2,4,1024]{2,1,0:T(4,128)(2,1)S(1)}, bf16[2,4,1024]{2,1,0:T(4,128)(2,1)S(1)}, u32[]{:S(2)}, u32[]{:S(2)}) collective-permute-start(bf16[2,4,1024]{2,1,0:T(4,128)(2,1)S(1)} %get-tuple-element.34), channel_id=1, source_target_pairs={{0,6},{1,7},{2,4},{3,5},{4,2},{5,3},{6,0},{7,1},{8,14},{9,15},{10,... | collective-permute-start | bytes 49160 | tf_op jit(solution)/shard_map/ppermute | solution.py:23
  9.2 3.7 %collective-permute-start.2 = (bf16[2,4,1024]{2,1,0:T(4,128)(2,1)S(1)}, bf16[2,4,1024]{2,1,0:T(4,128)(2,1)S(1)}, u32[]{:S(2)}, u32[]{:S(2)}) collective-permute-start(bf16[2,4,1024]{2,1,0:T(4,128)(2,1)S(1)} %get-tuple-element.35), channel_id=1, source_target_pairs={{0,4},{1,5},{2,6},{3,7},{4,0},{5,1},{6,2},{7,3},{8,12},{9,13},{10,... | collective-permute-start | bytes 49160 | tf_op jit(solution)/shard_map/ppermute | solution.py:23
  13.0 6.1 %collective-permute-start.4 = (bf16[1,4,2,4,1024]{4,3,2,1,0:T(4,128)(2,1)S(1)}, bf16[1,4,2,4,1024]{4,3,2,1,0:T(4,128)(2,1)S(1)}, u32[]{:S(2)}, u32[]{:S(2)}) collective-permute-start(bf16[1,4,2,4,1024]{4,3,2,1,0:T(4,128)(2,1)S(1)} %maximum_bitcast_fusion._), channel_id=1, source_target_pairs={{0,8},{1,9},{2,10},{3,11},{4,12},{5,13},{6,14},{7,15},{8,0},{9,1},... | collective-permute-start | bytes 196616 | tf_op jit(solution)/shard_map/ppermute | solution.py:23
  24.9 1.9 %collective-permute-start.5 = (bf16[32,7168]{1,0:T(8,128)(2,1)S(1)}, bf16[32,7168]{1,0:T(8,128)(2,1)S(1)}, u32[]{:S(2)}, u32[]{:S(2)}) collective-permute-start(bf16[32,7168]{1,0:T(8,128)(2,1)S(1)} %get-tuple-element.24), channel_id=1, source_target_pairs={{0,1},{1,0},{2,3},{3,2},{4,5},{5,4},{6,7},{7,6},{8,9},{9,8},{10,11... | collective-permute-start | bytes 1376264 | tf_op jit(solution)/shard_map/ppermute | solution.py:23
  26.9 6.7 %collective-permute-start.6 = (bf16[8,7168]{1,0:T(8,128)(2,1)S(1)}, bf16[8,7168]{1,0:T(8,128)(2,1)S(1)}, u32[]{:S(2)}, u32[]{:S(2)}) collective-permute-start(bf16[8,7168]{1,0:T(8,128)(2,1)S(1)} %get-tuple-element.29), channel_id=1, source_target_pairs={{0,6},{1,7},{2,4},{3,5},{4,2},{5,3},{6,0},{7,1},{8,14},{9,15},{10,... | collective-permute-start | bytes 344072 | tf_op jit(solution)/shard_map/ppermute | solution.py:23
  29.3 6.2 %collective-permute-start.8 = (bf16[8,7168]{1,0:T(8,128)(2,1)S(1)}, bf16[8,7168]{1,0:T(8,128)(2,1)S(1)}, u32[]{:S(2)}, u32[]{:S(2)}) collective-permute-start(bf16[8,7168]{1,0:T(8,128)(2,1)S(1)} %get-tuple-element.30), channel_id=1, source_target_pairs={{0,2},{1,3},{2,0},{3,1},{4,6},{5,7},{6,4},{7,5},{8,10},{9,11},{10,... | collective-permute-start | bytes 344072 | tf_op jit(solution)/shard_map/ppermute | solution.py:23
  29.8 5.8 %collective-permute-start.7 = (bf16[8,7168]{1,0:T(8,128)(2,1)S(1)}, bf16[8,7168]{1,0:T(8,128)(2,1)S(1)}, u32[]{:S(2)}, u32[]{:S(2)}) collective-permute-start(bf16[8,7168]{1,0:T(8,128)(2,1)S(1)} %get-tuple-element.31), channel_id=1, source_target_pairs={{0,4},{1,5},{2,6},{3,7},{4,0},{5,1},{6,2},{7,3},{8,12},{9,13},{10,... | collective-permute-start | bytes 344072 | tf_op jit(solution)/shard_map/ppermute | solution.py:23
  35.7 5.7 %collective-permute-start.11 = (bf16[8,3584]{1,0:T(8,128)(2,1)S(1)}, bf16[8,3584]{1,0:T(8,128)(2,1)S(1)}, u32[]{:S(2)}, u32[]{:S(2)}) collective-permute-start(bf16[8,3584]{1,0:T(8,128)(2,1)S(1)} %fusion), channel_id=1, source_target_pairs={{0,6},{1,7},{2,4},{3,5},{4,2},{5,3},{6,0},{7,1},{8,14},{9,15},{10,... | collective-permute-start | bytes 172040 | tf_op jit(solution)/shard_map/ppermute | solution.py:23
  37.4 4.3 %collective-permute-start.10 = (bf16[8,3584]{1,0:T(8,128)(2,1)S(1)}, bf16[8,3584]{1,0:T(8,128)(2,1)S(1)}, u32[]{:S(2)}, u32[]{:S(2)}) collective-permute-start(bf16[8,3584]{1,0:T(8,128)(2,1)S(1)} %fusion), channel_id=1, source_target_pairs={{0,4},{1,5},{2,6},{3,7},{4,0},{5,1},{6,2},{7,3},{8,12},{9,13},{10,... | collective-permute-start | bytes 172040 | tf_op jit(solution)/shard_map/ppermute | solution.py:23
  38.7 4.2 %collective-permute-start.9 = (bf16[8,3584]{1,0:T(8,128)(2,1)S(1)}, bf16[8,3584]{1,0:T(8,128)(2,1)S(1)}, u32[]{:S(2)}, u32[]{:S(2)}) collective-permute-start(bf16[8,3584]{1,0:T(8,128)(2,1)S(1)} %fusion), channel_id=1, source_target_pairs={{0,2},{1,3},{2,0},{3,1},{4,6},{5,7},{6,4},{7,5},{8,10},{9,11},{10,... | collective-permute-start | bytes 172040 | tf_op jit(solution)/shard_map/ppermute | solution.py:23
  42.9 1.6 %collective-permute-start.12 = (bf16[32,3584]{1,0:T(8,128)(2,1)S(1)}, bf16[32,3584]{1,0:T(8,128)(2,1)S(1)}, u32[]{:S(2)}, u32[]{:S(2)}) collective-permute-start(bf16[32,3584]{1,0:T(8,128)(2,1)S(1)} %pad_maximum_fusion.near_ref), channel_id=1, source_target_pairs={{0,1},{1,0},{2,3},{3,2},{4,5},{5,4},{6,7},{7,6},{8,9},{9,8},{10,11... | collective-permute-start | bytes 688136 | tf_op jit(solution)/shard_map/ppermute | solution.py:23

commit v3 on v2

--- a/solution.py
+++ b/solution.py
@@ -30,6 +30,29 @@
 
 def in_hbm(value):
     return pltpu.with_memory_space_constraint(value, pltpu.HBM)
+
+
+def block_copy(list_ref, w_hbm, out_ref, sems, c):
+    group, _, _ = place()
+    return pltpu.make_async_copy(w_hbm.at[0, list_ref[group, c]], out_ref.at[c], sems.at[c])
+
+
+def start_blocks(list_ref, count_ref, w_hbm, out_ref, sems):
+    live = count_ref[place()[0]]
+
+    @pl.loop(0, live)
+    def _(c):
+        block_copy(list_ref, w_hbm, out_ref, sems, c).start()
+
+    @pl.loop(live, out_ref.shape[0])
+    def _(c):
+        out_ref[c] = jnp.zeros(out_ref.shape[1:], out_ref.dtype)
+
+
+def wait_blocks(list_ref, count_ref, w_hbm, out_ref, sems):
+    @pl.loop(0, count_ref[place()[0]])
+    def _(c):
+        block_copy(list_ref, w_hbm, out_ref, sems, c).wait()
 
 
 def attend_kernel(
@@ -40,16 +63,23 @@
     v_hbm,
     res_hbm,
     gain_hbm,
+    list_hbm,
+    count_hbm,
+    gate_hbm,
     mixed_ref,
     kept_ref,
     sent_ref,
+    gate_ref,
     len_ref,
     q_ref,
     k_buf,
     v_buf,
     res_ref,
     gain_ref,
+    list_ref,
+    count_ref,
     sems,
+    block_sems,
 ):
     rows, heads, size = q_ref.shape
     slots = k_buf.shape[1]
@@ -63,10 +93,15 @@
         (v_hbm, v_buf),
         (res_hbm, res_ref),
         (gain_hbm, gain_ref),
+        (list_hbm, list_ref),
+        (count_hbm, count_ref),
     ]
     copies = [pltpu.make_async_copy(s, d, sems.at[i]) for i, (s, d) in enumerate(pairs)]
-    for copy in copies:
+    for copy in copies[6:] + copies[:6]:
         copy.start()
+    copies[6].wait()
+    copies[7].wait()
+    start_blocks(list_ref, count_ref, gate_hbm, gate_ref, block_sems)
     line = lax.broadcasted_iota(jnp.int32, (lines, lines), 0)
     taken = lax.broadcasted_iota(jnp.int32, (lines, lines), 1)
     swap = (taken == line % rows * heads + line // rows).astype(jnp.float32).astype(jnp.bfloat16)
@@ -123,9 +158,12 @@
         second = normed[:, (2 * q + 1) * step : (2 * q + 2) * step]
         kept_ref[q ^ chip] = jnp.where(core == 0, first, second)
         sent_ref[q ^ chip] = jnp.where(core == 0, second, first)
-
-
-def attend(queries, k_cache, v_cache, lengths, residual_in, norm_gain):
+    wait_blocks(list_ref, count_ref, gate_hbm, gate_ref, block_sems)
+
+
+def attend(
+    queries, k_cache, v_cache, lengths, residual_in, norm_gain, block_list, block_count, gate_w
+):
     rows, heads, size = queries.shape
     slots, width = k_cache.shape[1:]
     model = residual_in.shape[1]
@@ -135,9 +173,10 @@
             pltpu.VMEM((rows, model), jnp.float32),
             pltpu.VMEM((CHIPS, rows, model // MDL), jnp.bfloat16),
             pltpu.VMEM((CHIPS, rows, model // MDL), jnp.bfloat16),
+            pltpu.VMEM(block_list.shape[1:] + gate_w.shape[2:], jnp.bfloat16),
         ),
-        in_specs=[HBM] * 6,
-        out_specs=(VMEM,) * 3,
+        in_specs=[HBM] * 9,
+        out_specs=(VMEM,) * 4,
         scratch_shapes=[
             pltpu.SMEM((rows,), jnp.int32),
             pltpu.VMEM((rows, heads, size), jnp.bfloat16),
@@ -145,7 +184,10 @@
             pltpu.VMEM((rows, slots, width), jnp.bfloat16),
             pltpu.VMEM((rows, model), jnp.bfloat16),
             pltpu.VMEM((1, model), jnp.float32),
-            pltpu.SemaphoreType.DMA((6,)),
+            pltpu.SMEM(block_list.shape, jnp.int32),
+            pltpu.SMEM(block_count.shape, jnp.int32),
+            pltpu.SemaphoreType.DMA((8,)),
+            pltpu.SemaphoreType.DMA(block_list.shape[1:]),
         ],
         compiler_params=pltpu.CompilerParams(vmem_limit_bytes=20 * 2**20),
         name="attend",
@@ -159,12 +201,16 @@
                 v_cache,
                 residual_in,
                 norm_gain.reshape(1, model),
+                block_list,
+                block_count,
+                gate_w,
             )
         )
     )
 
 
-def fetch_kernel(list_hbm, count_hbm, w_hbm, _, out_ref, __, list_ref, count_ref, sems):
+def fetch_kernel(list_hbm, count_hbm, w_hbm, _, out_ref, *rest):
+    list_ref, count_ref, sems, block_sems = rest[-4:]
     copies = [
         pltpu.make_async_copy(list_hbm, list_ref, sems.at[0]),
         pltpu.make_async_copy(count_hbm, count_ref, sems.at[1]),
@@ -173,40 +219,24 @@
         copy.start()
     for copy in copies:
         copy.wait()
-    group, _, _ = place()
-    live = count_ref[group]
-
-    def fetched(c):
-        return pltpu.make_async_copy(w_hbm.at[0, list_ref[group, c]], out_ref.at[c], sems.at[c])
-
-    @pl.loop(0, live)
-    def _(c):
-        fetched(c).start()
-
-    @pl.loop(live, out_ref.shape[0])
-    def _(c):
-        out_ref[c] = jnp.zeros(out_ref.shape[1:], out_ref.dtype)
-
-    @pl.loop(0, live)
-    def _(c):
-        fetched(c).wait()
-
-
-def fetch(block_list, block_count, weights, held, name):
+    start_blocks(list_ref, count_ref, w_hbm, out_ref, block_sems)
+    wait_blocks(list_ref, count_ref, w_hbm, out_ref, block_sems)
+
+
+def fetch(block_list, block_count, weights, held, name, passed=True):
     count = block_list.shape[1]
     size = math.prod(weights.shape[2:])
+    blocks = pltpu.VMEM((count,) + weights.shape[2:], jnp.bfloat16)
     return pl.pallas_call(
         fetch_kernel,
-        out_shape=(
-            pltpu.VMEM((count,) + weights.shape[2:], jnp.bfloat16),
-            jax.ShapeDtypeStruct(held.shape, held.dtype),
-        ),
+        out_shape=(blocks, jax.ShapeDtypeStruct(held.shape, held.dtype)) if passed else blocks,
         in_specs=[HBM] * 3 + [ANY],
-        out_specs=(VMEM, ANY),
-        input_output_aliases={3: 1},
+        out_specs=(VMEM, ANY) if passed else VMEM,
+        input_output_aliases={3: 1} if passed else {},
         scratch_shapes=[
             pltpu.SMEM(block_list.shape, jnp.int32),
             pltpu.SMEM(block_count.shape, jnp.int32),
+            pltpu.SemaphoreType.DMA((2,)),
             pltpu.SemaphoreType.DMA((count,)),
         ],
         compiler_params=pltpu.CompilerParams(vmem_limit_bytes=10 * 2**20),
@@ -321,15 +351,14 @@
     masks = [chip * CORES for chip in range(CHIPS)]
     far_first = range(CHIPS - 1, 0, -1)
 
-    mixed_rows, kept, sent = attend(queries, k_cache, v_cache, lengths, residual_in, norm_gain)
+    mixed_rows, kept, sent, gate = attend(
+        queries, k_cache, v_cache, lengths, residual_in, norm_gain, block_list, block_count, gate_w
+    )
     pair = jnp.stack([kept, from_partner(sent, 1)], axis=1)
     came = {chip: from_partner(pair[chip], masks[chip]) for chip in far_first}
-    gate, own = fetch(block_list, block_count, gate_w, pair[0], "fetch_gate")
-    arrived = jnp.stack([own] + [came[chip] for chip in range(1, CHIPS)])[None]
-    came = from_partner(arrived, MDL)
-    up, arrived = fetch(block_list, block_count, up_w, arrived, "fetch_up")
-    arrived = jnp.concatenate([arrived, came], axis=0)
-    for level in range(1, group_total.bit_length() - 1):
+    arrived = jnp.stack([pair[0]] + [came[chip] for chip in range(1, CHIPS)])[None]
+    up = fetch(block_list, block_count, up_w, arrived, "fetch_up", passed=False)
+    for level in range(group_total.bit_length() - 1):
         arrived = jnp.concatenate([arrived, from_partner(arrived, MDL << level)], axis=0)
 
     part, sent = gate_up(arrived, gate, up)

time: 61 us -> 56.7 us (0.930)
  Pallas kernels: 17.3 us -> 14.5 us
  blocking collectives: 14.3 us -> 12.7 us
    pallas_call x3 -> x2, Pallas kernels: 9.37 us -> 5.8 us  [fetch(): pl.pallas_call(fetch_kernel, out_shape=(blocks, jax.ShapeDtypeStruct(held...]
    all_to_all x1, blocking collectives: 14.3 us -> 12.7 us  [on_device(): lax.all_to_all(ffn_part, 'hid', split_axis=0, concat_axis=0, tiled=True)]
    pallas_call x1, Pallas kernels: 3.28 us -> 4.03 us  [attend(): pl.pallas_call(functools.partial(attend_kernel, width // size), out_shape...]
  transfers between devices with their start and end apart: 13 -> 13, of which waited for: 10 -> 12; matrix products, arithmetic and copies ran while one was open for 0% -> 0% of each run, Pallas kernels for 10% -> 10%
where the time goes in v3:
time: 56.7 us; the launch traced here: 56.5 us
  starting transfers between devices  15.4 us (27%)
  Pallas kernels  14.5 us (26%)
  waiting for transfers between devices  13.4 us (24%)
  blocking collectives  12.7 us (22%)
    ppermute x13, starting transfers between devices, from_partner(): return lax.ppermute(value, 'hid', pairs)  15.4 us
    ppermute x13, waiting for transfers between devices, from_partner(): return lax.ppermute(value, 'hid', pairs)  13.4 us
    all_to_all x1, blocking collectives, on_device(): lax.all_to_all(ffn_part, 'hid', split_axis=0, concat_axis=0, tiled=True)  12.7 us
    pallas_call x2, Pallas kernels, fetch(): pl.pallas_call(fetch_kernel, out_shape=(blocks, jax.ShapeDtypeStruct(held...  5.8 us
    pallas_call x1, Pallas kernels, attend(): pl.pallas_call(functools.partial(attend_kernel, width // size), out_shape...  4.03 us
    pallas_call x1, Pallas kernels, gate_up(): pl.pallas_call(gate_up_kernel, out_shape=(pltpu.VMEM((rows // 2, 2 * coun...  2.64 us
    pallas_call x1, Pallas kernels, down(): pl.pallas_call(down_kernel, out_shape=pltpu.VMEM((devices, rows, weights....  1.38 us
  transfers between devices with their start and end apart: 13, of which 12 were waited for; matrix products, arithmetic and copies ran while one was open for 0% of the time, Pallas kernels for 10%

profile of v3, /device:TPU:0, one launch (start us, length us, event | category | flops | bytes accessed | tf_op | source)
XLA Modules:
  0.0 56.5 jit_solution(16045774994218956470)
XLA Ops:
  0.0 4.0 %attend.1 = (f32[4,8192]{1,0:T(4,128)S(1)}, bf16[4,4,1024]{2,1,0:T(4,128)(2,1)S(1)}, bf16[4,4,1024]{2,1,0:T(4,128)(2,1)S(1)}, bf16[28,1024,128]{2,1,0:T(8,128)(2,1)S(1)}) custom-call(s32[4]{0:T(128)} %len_hbm.1, bf16[4,64,128]{2,1,0:T(8,128)(2,1)} %q_hbm.1, bf16[4,192,1024]{2,1,0:T(8,128)(2,1)} %k_hbm.1, bf16[4,192,1024]{2,1,0:T(8,128)(2,1)} %v_hbm.1, ...), custom_call_target="tpu_custom_call" | custom-call | tf_op jit(solution)/shard_map/attend/pallas_call | solution.py:170
  4.0 0.5 collective-permute-start
  4.6 0.9 %collective-permute-done = bf16[4,4,1024]{2,1,0:T(4,128)(2,1)S(1)} collective-permute-done((bf16[4,4,1024]{2,1,0:T(4,128)(2,1)S(1)}, bf16[4,4,1024]{2,1,0:T(4,128)(2,1)S(1)}, u32[]{:S(2)}, u32[]{:S(2)}) %collective-permute-start) | collective-permute-done | bytes 32800 | tf_op jit(solution)/shard_map/ppermute | solution.py:23
  5.5 2.9 %collective-permute-start.1 = (bf16[2,4,1024]{2,1,0:T(4,128)(2,1)S(1)}, bf16[2,4,1024]{2,1,0:T(4,128)(2,1)S(1)}, u32[]{:S(2)}, u32[]{:S(2)}) collective-permute-start(bf16[2,4,1024]{2,1,0:T(4,128)(2,1)S(1)} %get-tuple-element.27), channel_id=1, source_target_pairs={{0,2},{1,3},{2,0},{3,1},{4,6},{5,7},{6,4},{7,5},{8,10},{9,11},{10,... | collective-permute-start | bytes 49160 | tf_op jit(solution)/shard_map/ppermute | solution.py:23
  8.4 1.5 %collective-permute-start.3 = (bf16[2,4,1024]{2,1,0:T(4,128)(2,1)S(1)}, bf16[2,4,1024]{2,1,0:T(4,128)(2,1)S(1)}, u32[]{:S(2)}, u32[]{:S(2)}) collective-permute-start(bf16[2,4,1024]{2,1,0:T(4,128)(2,1)S(1)} %get-tuple-element.28), channel_id=1, source_target_pairs={{0,6},{1,7},{2,4},{3,5},{4,2},{5,3},{6,0},{7,1},{8,14},{9,15},{10,... | collective-permute-start | bytes 49160 | tf_op jit(solution)/shard_map/ppermute | solution.py:23
  10.0 0.1 collective-permute-done.1
  10.1 2.9 %collective-permute-done.3 = bf16[2,4,1024]{2,1,0:T(4,128)(2,1)S(1)} collective-permute-done((bf16[2,4,1024]{2,1,0:T(4,128)(2,1)S(1)}, bf16[2,4,1024]{2,1,0:T(4,128)(2,1)S(1)}, u32[]{:S(2)}, u32[]{:S(2)}) %collective-permute-start.3) | collective-permute-done | bytes 16416 | tf_op jit(solution)/shard_map/ppermute | solution.py:23
  13.0 0.6 %collective-permute-done.2 = bf16[2,4,1024]{2,1,0:T(4,128)(2,1)S(1)} collective-permute-done((bf16[2,4,1024]{2,1,0:T(4,128)(2,1)S(1)}, bf16[2,4,1024]{2,1,0:T(4,128)(2,1)S(1)}, u32[]{:S(2)}, u32[]{:S(2)}) %collective-permute-start.2) | collective-permute-done | bytes 16416 | tf_op jit(solution)/shard_map/ppermute | solution.py:23
  13.7 3.2 %collective-permute-start.4 = (bf16[1,4,2,4,1024]{4,3,2,1,0:T(4,128)(2,1)S(1)}, bf16[1,4,2,4,1024]{4,3,2,1,0:T(4,128)(2,1)S(1)}, u32[]{:S(2)}, u32[]{:S(2)}) collective-permute-start(bf16[1,4,2,4,1024]{4,3,2,1,0:T(4,128)(2,1)S(1)} %maximum_bitcast_fusion._), channel_id=1, source_target_pairs={{0,8},{1,9},{2,10},{3,11},{4,12},{5,13},{6,14},{7,15},{8,0},{9,1},... | collective-permute-start | bytes 196616 | tf_op jit(solution)/shard_map/ppermute | solution.py:23
  16.9 2.9 %fetch_up.1.up_ref = bf16[28,1024,128]{2,1,0:T(8,128)(2,1)S(1)} custom-call(s32[2,28]{1,0:T(2,128)} %list_hbm.5, s32[2]{0:T(128)} %count_hbm.5, bf16[1,56,1024,128]{3,2,1,0:T(8,128)(2,1)} %w_hbm.2, bf16[1,4,2,4,1024]{4,3,2,1,0:T(4,128)(2,1)S(1)} %maximum_bitcast_fusion._), custom_call_target="tpu_custom_call" | custom-call | bytes 14680064 | tf_op jit(solution)/shard_map/fetch_up/pallas_call | solution.py:230
  19.8 0.1 pad_maximum_fusion.1.arrived_ref
  19.9 2.6 %gate_up.1 = (f32[32,7168]{1,0:T(8,128)S(1)}, bf16[32,7168]{1,0:T(8,128)(2,1)S(1)}) custom-call(bf16[2,4,2,4,1024]{4,3,2,1,0:T(4,128)(2,1)S(1)} %pad_maximum_fusion.1.arrived_ref, bf16[28,1024,128]{2,1,0:T(8,128)(2,1)S(1)} %get-tuple-element.16.gate_ref, bf16[28,1024,128]{2,1,0:T(8,128)(2,1)S(1)} %fetch_up.1.up_ref), custom_call_target="tpu_custom_call" | custom-call | tf_op jit(solution)/shard_map/gate_up/pallas_call | solution.py:271
  22.6 1.8 %collective-permute-done.5 = bf16[32,7168]{1,0:T(8,128)(2,1)S(1)} collective-permute-done((bf16[32,7168]{1,0:T(8,128)(2,1)S(1)}, bf16[32,7168]{1,0:T(8,128)(2,1)S(1)}, u32[]{:S(2)}, u32[]{:S(2)}) %collective-permute-start.5) | collective-permute-done | bytes 458784 | tf_op jit(solution)/shard_map/ppermute | solution.py:23
  24.4 0.1 fusion.7
  24.6 1.4 %collective-permute-start.6 = (bf16[8,7168]{1,0:T(8,128)(2,1)S(1)}, bf16[8,7168]{1,0:T(8,128)(2,1)S(1)}, u32[]{:S(2)}, u32[]{:S(2)}) collective-permute-start(bf16[8,7168]{1,0:T(8,128)(2,1)S(1)} %get-tuple-element.23), channel_id=1, source_target_pairs={{0,6},{1,7},{2,4},{3,5},{4,2},{5,3},{6,0},{7,1},{8,14},{9,15},{10,... | collective-permute-start | bytes 344072 | tf_op jit(solution)/shard_map/ppermute | solution.py:23
  26.0 1.0 %collective-permute-start.8 = (bf16[8,7168]{1,0:T(8,128)(2,1)S(1)}, bf16[8,7168]{1,0:T(8,128)(2,1)S(1)}, u32[]{:S(2)}, u32[]{:S(2)}) collective-permute-start(bf16[8,7168]{1,0:T(8,128)(2,1)S(1)} %get-tuple-element.24), channel_id=1, source_target_pairs={{0,2},{1,3},{2,0},{3,1},{4,6},{5,7},{6,4},{7,5},{8,10},{9,11},{10,... | collective-permute-start | bytes 344072 | tf_op jit(solution)/shard_map/ppermute | solution.py:23
  27.0 1.1 %collective-permute-start.7 = (bf16[8,7168]{1,0:T(8,128)(2,1)S(1)}, bf16[8,7168]{1,0:T(8,128)(2,1)S(1)}, u32[]{:S(2)}, u32[]{:S(2)}) collective-permute-start(bf16[8,7168]{1,0:T(8,128)(2,1)S(1)} %get-tuple-element.25), channel_id=1, source_target_pairs={{0,4},{1,5},{2,6},{3,7},{4,0},{5,1},{6,2},{7,3},{8,12},{9,13},{10,... | collective-permute-start | bytes 344072 | tf_op jit(solution)/shard_map/ppermute | solution.py:23
  28.1 2.9 %fetch_down.1 = (bf16[28,128,1024]{2,1,0:T(8,128)(2,1)S(1)}, f32[8,7168]{1,0:T(8,128)S(1)}) custom-call(s32[2,28]{1,0:T(2,128)} %list_hbm.5, s32[2]{0:T(128)} %count_hbm.5, bf16[1,56,128,1024]{3,2,1,0:T(8,128)(2,1)} %w_hbm.3, f32[8,7168]{1,0:T(8,128)S(1)} %slice.53._), custom_call_target="tpu_custom_call", output_to_operand_aliasing={{1}: (3, {})} | custom-call | bytes 14680064 | tf_op jit(solution)/shard_map/fetch_down/pallas_call | solution.py:230
  31.1 0.5 collective-permute-done.6
  31.5 1.7 %collective-permute-done.8 = bf16[8,7168]{1,0:T(8,128)(2,1)S(1)} collective-permute-done((bf16[8,7168]{1,0:T(8,128)(2,1)S(1)}, bf16[8,7168]{1,0:T(8,128)(2,1)S(1)}, u32[]{:S(2)}, u32[]{:S(2)}) %collective-permute-start.8) | collective-permute-done | bytes 114720 | tf_op jit(solution)/shard_map/ppermute | solution.py:23
  33.2 0.2 collective-permute-done.7
  33.4 1.3 %collective-permute-start.11 = (bf16[8,3584]{1,0:T(8,128)(2,1)S(1)}, bf16[8,3584]{1,0:T(8,128)(2,1)S(1)}, u32[]{:S(2)}, u32[]{:S(2)}) collective-permute-start(bf16[8,3584]{1,0:T(8,128)(2,1)S(1)} %fusion), channel_id=1, source_target_pairs={{0,6},{1,7},{2,4},{3,5},{4,2},{5,3},{6,0},{7,1},{8,14},{9,15},{10,... | collective-permute-start | bytes 172040 | tf_op jit(solution)/shard_map/ppermute | solution.py:23
  34.7 1.3 %collective-permute-start.10 = (bf16[8,3584]{1,0:T(8,128)(2,1)S(1)}, bf16[8,3584]{1,0:T(8,128)(2,1)S(1)}, u32[]{:S(2)}, u32[]{:S(2)}) collective-permute-start(bf16[8,3584]{1,0:T(8,128)(2,1)S(1)} %fusion), channel_id=1, source_target_pairs={{0,4},{1,5},{2,6},{3,7},{4,0},{5,1},{6,2},{7,3},{8,12},{9,13},{10,... | collective-permute-start | bytes 172040 | tf_op jit(solution)/shard_map/ppermute | solution.py:23
  36.0 1.0 %collective-permute-start.9 = (bf16[8,3584]{1,0:T(8,128)(2,1)S(1)}, bf16[8,3584]{1,0:T(8,128)(2,1)S(1)}, u32[]{:S(2)}, u32[]{:S(2)}) collective-permute-start(bf16[8,3584]{1,0:T(8,128)(2,1)S(1)} %fusion), channel_id=1, source_target_pairs={{0,2},{1,3},{2,0},{3,1},{4,6},{5,7},{6,4},{7,5},{8,10},{9,11},{10,... | collective-permute-start | bytes 172040 | tf_op jit(solution)/shard_map/ppermute | solution.py:23
  37.0 1.8 %collective-permute-done.11 = bf16[8,3584]{1,0:T(8,128)(2,1)S(1)} collective-permute-done((bf16[8,3584]{1,0:T(8,128)(2,1)S(1)}, bf16[8,3584]{1,0:T(8,128)(2,1)S(1)}, u32[]{:S(2)}, u32[]{:S(2)}) %collective-permute-start.11) | collective-permute-done | bytes 57376 | tf_op jit(solution)/shard_map/ppermute | solution.py:23
  38.8 0.1 collective-permute-done.10
  38.9 1.3 %collective-permute-done.9 = bf16[8,3584]{1,0:T(8,128)(2,1)S(1)} collective-permute-done((bf16[8,3584]{1,0:T(8,128)(2,1)S(1)}, bf16[8,3584]{1,0:T(8,128)(2,1)S(1)}, u32[]{:S(2)}, u32[]{:S(2)}) %collective-permute-start.9) | collective-permute-done | bytes 57376 | tf_op jit(solution)/shard_map/ppermute | solution.py:23
  40.2 0.1 collective-permute-start.12
  40.3 1.5 %collective-permute-done.12.far_ref = bf16[32,3584]{1,0:T(8,128)(2,1)S(1)} collective-permute-done((bf16[32,3584]{1,0:T(8,128)(2,1)S(1)}, bf16[32,3584]{1,0:T(8,128)(2,1)S(1)}, u32[]{:S(2)}, u32[]{:S(2)}) %collective-permute-start.12) | collective-permute-done | bytes 229408 | tf_op jit(solution)/shard_map/ppermute | solution.py:23
  41.8 1.4 %down.1 = bf16[16,4,1024]{2,1,0:T(4,128)(2,1)S(1)} custom-call(bf16[32,3584]{1,0:T(8,128)(2,1)S(1)} %pad_maximum_fusion.near_ref, bf16[32,3584]{1,0:T(8,128)(2,1)S(1)} %collective-permute-done.12.far_ref, bf16[28,128,1024]{2,1,0:T(8,128)(2,1)S(1)} %get-tuple-element.20.w_ref), custom_call_target="tpu_custom_call" | custom-call | tf_op jit(solution)/shard_map/down/pallas_call | solution.py:304
  43.2 12.7 %all_to_all.5.back_ref = bf16[16,4,1024]{2,1,0:T(4,128)(2,1)S(1)} all-to-all(bf16[16,4,1024]{2,1,0:T(4,128)(2,1)S(1)} %down.1), channel_id=1, replica_groups=mesh['groups'=2,'hid'=16] {'hid'}, dimensions={0} | all-to-all | bytes 262144 | tf_op jit(solution)/shard_map/all_to_all | solution.py:377
  55.8 0.7 %finish.1 = bf16[4,8192]{1,0:T(4,128)(2,1)} custom-call(f32[4,8192]{1,0:T(4,128)S(1)} %get-tuple-element.13.mixed_ref, bf16[16,4,1024]{2,1,0:T(4,128)(2,1)S(1)} %all_to_all.5.back_ref), custom_call_target="tpu_custom_call" | custom-call | tf_op jit(solution)/shard_map/finish/pallas_call | solution.py:324
  (10 shorter events, 0.4 us)
Async XLA Ops:
  4.0 1.4 %collective-permute-start = (bf16[4,4,1024]{2,1,0:T(4,128)(2,1)S(1)}, bf16[4,4,1024]{2,1,0:T(4,128)(2,1)S(1)}, u32[]{:S(2)}, u32[]{:S(2)}) collective-permute-start(bf16[4,4,1024]{2,1,0:T(4,128)(2,1)S(1)} %get-tuple-element.15), channel_id=1, source_target_pairs={{0,1},{1,0},{2,3},{3,2},{4,5},{5,4},{6,7},{7,6},{8,9},{9,8},{10,11... | collective-permute-start | bytes 98312 | tf_op jit(solution)/shard_map/ppermute | solution.py:23
  5.5 4.7 %collective-permute-start.1 = (bf16[2,4,1024]{2,1,0:T(4,128)(2,1)S(1)}, bf16[2,4,1024]{2,1,0:T(4,128)(2,1)S(1)}, u32[]{:S(2)}, u32[]{:S(2)}) collective-permute-start(bf16[2,4,1024]{2,1,0:T(4,128)(2,1)S(1)} %get-tuple-element.27), channel_id=1, source_target_pairs={{0,2},{1,3},{2,0},{3,1},{4,6},{5,7},{6,4},{7,5},{8,10},{9,11},{10,... | collective-permute-start | bytes 49160 | tf_op jit(solution)/shard_map/ppermute | solution.py:23
  8.4 4.6 %collective-permute-start.3 = (bf16[2,4,1024]{2,1,0:T(4,128)(2,1)S(1)}, bf16[2,4,1024]{2,1,0:T(4,128)(2,1)S(1)}, u32[]{:S(2)}, u32[]{:S(2)}) collective-permute-start(bf16[2,4,1024]{2,1,0:T(4,128)(2,1)S(1)} %get-tuple-element.28), channel_id=1, source_target_pairs={{0,6},{1,7},{2,4},{3,5},{4,2},{5,3},{6,0},{7,1},{8,14},{9,15},{10,... | collective-permute-start | bytes 49160 | tf_op jit(solution)/shard_map/ppermute | solution.py:23
  9.9 3.7 %collective-permute-start.2 = (bf16[2,4,1024]{2,1,0:T(4,128)(2,1)S(1)}, bf16[2,4,1024]{2,1,0:T(4,128)(2,1)S(1)}, u32[]{:S(2)}, u32[]{:S(2)}) collective-permute-start(bf16[2,4,1024]{2,1,0:T(4,128)(2,1)S(1)} %get-tuple-element.29), channel_id=1, source_target_pairs={{0,4},{1,5},{2,6},{3,7},{4,0},{5,1},{6,2},{7,3},{8,12},{9,13},{10,... | collective-permute-start | bytes 49160 | tf_op jit(solution)/shard_map/ppermute | solution.py:23
  13.7 6.1 %collective-permute-start.4 = (bf16[1,4,2,4,1024]{4,3,2,1,0:T(4,128)(2,1)S(1)}, bf16[1,4,2,4,1024]{4,3,2,1,0:T(4,128)(2,1)S(1)}, u32[]{:S(2)}, u32[]{:S(2)}) collective-permute-start(bf16[1,4,2,4,1024]{4,3,2,1,0:T(4,128)(2,1)S(1)} %maximum_bitcast_fusion._), channel_id=1, source_target_pairs={{0,8},{1,9},{2,10},{3,11},{4,12},{5,13},{6,14},{7,15},{8,0},{9,1},... | collective-permute-start | bytes 196616 | tf_op jit(solution)/shard_map/ppermute | solution.py:23
  22.6 1.9 %collective-permute-start.5 = (bf16[32,7168]{1,0:T(8,128)(2,1)S(1)}, bf16[32,7168]{1,0:T(8,128)(2,1)S(1)}, u32[]{:S(2)}, u32[]{:S(2)}) collective-permute-start(bf16[32,7168]{1,0:T(8,128)(2,1)S(1)} %get-tuple-element.18), channel_id=1, source_target_pairs={{0,1},{1,0},{2,3},{3,2},{4,5},{5,4},{6,7},{7,6},{8,9},{9,8},{10,11... | collective-permute-start | bytes 1376264 | tf_op jit(solution)/shard_map/ppermute | solution.py:23
  24.6 7.0 %collective-permute-start.6 = (bf16[8,7168]{1,0:T(8,128)(2,1)S(1)}, bf16[8,7168]{1,0:T(8,128)(2,1)S(1)}, u32[]{:S(2)}, u32[]{:S(2)}) collective-permute-start(bf16[8,7168]{1,0:T(8,128)(2,1)S(1)} %get-tuple-element.23), channel_id=1, source_target_pairs={{0,6},{1,7},{2,4},{3,5},{4,2},{5,3},{6,0},{7,1},{8,14},{9,15},{10,... | collective-permute-start | bytes 344072 | tf_op jit(solution)/shard_map/ppermute | solution.py:23
  26.0 7.2 %collective-permute-start.8 = (bf16[8,7168]{1,0:T(8,128)(2,1)S(1)}, bf16[8,7168]{1,0:T(8,128)(2,1)S(1)}, u32[]{:S(2)}, u32[]{:S(2)}) collective-permute-start(bf16[8,7168]{1,0:T(8,128)(2,1)S(1)} %get-tuple-element.24), channel_id=1, source_target_pairs={{0,2},{1,3},{2,0},{3,1},{4,6},{5,7},{6,4},{7,5},{8,10},{9,11},{10,... | collective-permute-start | bytes 344072 | tf_op jit(solution)/shard_map/ppermute | solution.py:23
  27.0 6.3 %collective-permute-start.7 = (bf16[8,7168]{1,0:T(8,128)(2,1)S(1)}, bf16[8,7168]{1,0:T(8,128)(2,1)S(1)}, u32[]{:S(2)}, u32[]{:S(2)}) collective-permute-start(bf16[8,7168]{1,0:T(8,128)(2,1)S(1)} %get-tuple-element.25), channel_id=1, source_target_pairs={{0,4},{1,5},{2,6},{3,7},{4,0},{5,1},{6,2},{7,3},{8,12},{9,13},{10,... | collective-permute-start | bytes 344072 | tf_op jit(solution)/shard_map/ppermute | solution.py:23
  33.4 5.3 %collective-permute-start.11 = (bf16[8,3584]{1,0:T(8,128)(2,1)S(1)}, bf16[8,3584]{1,0:T(8,128)(2,1)S(1)}, u32[]{:S(2)}, u32[]{:S(2)}) collective-permute-start(bf16[8,3584]{1,0:T(8,128)(2,1)S(1)} %fusion), channel_id=1, source_target_pairs={{0,6},{1,7},{2,4},{3,5},{4,2},{5,3},{6,0},{7,1},{8,14},{9,15},{10,... | collective-permute-start | bytes 172040 | tf_op jit(solution)/shard_map/ppermute | solution.py:23
  34.7 4.2 %collective-permute-start.10 = (bf16[8,3584]{1,0:T(8,128)(2,1)S(1)}, bf16[8,3584]{1,0:T(8,128)(2,1)S(1)}, u32[]{:S(2)}, u32[]{:S(2)}) collective-permute-start(bf16[8,3584]{1,0:T(8,128)(2,1)S(1)} %fusion), channel_id=1, source_target_pairs={{0,4},{1,5},{2,6},{3,7},{4,0},{5,1},{6,2},{7,3},{8,12},{9,13},{10,... | collective-permute-start | bytes 172040 | tf_op jit(solution)/shard_map/ppermute | solution.py:23
  36.0 4.2 %collective-permute-start.9 = (bf16[8,3584]{1,0:T(8,128)(2,1)S(1)}, bf16[8,3584]{1,0:T(8,128)(2,1)S(1)}, u32[]{:S(2)}, u32[]{:S(2)}) collective-permute-start(bf16[8,3584]{1,0:T(8,128)(2,1)S(1)} %fusion), channel_id=1, source_target_pairs={{0,2},{1,3},{2,0},{3,1},{4,6},{5,7},{6,4},{7,5},{8,10},{9,11},{10,... | collective-permute-start | bytes 172040 | tf_op jit(solution)/shard_map/ppermute | solution.py:23
  40.2 1.6 %collective-permute-start.12 = (bf16[32,3584]{1,0:T(8,128)(2,1)S(1)}, bf16[32,3584]{1,0:T(8,128)(2,1)S(1)}, u32[]{:S(2)}, u32[]{:S(2)}) collective-permute-start(bf16[32,3584]{1,0:T(8,128)(2,1)S(1)} %pad_maximum_fusion.near_ref), channel_id=1, source_target_pairs={{0,1},{1,0},{2,3},{3,2},{4,5},{5,4},{6,7},{7,6},{8,9},{9,8},{10,11... | collective-permute-start | bytes 688136 | tf_op jit(solution)/shard_map/ppermute | solution.py:23

commit v4 on v3

--- a/solution.py
+++ b/solution.py
@@ -32,27 +32,10 @@
     return pltpu.with_memory_space_constraint(value, pltpu.HBM)
 
 
-def block_copy(list_ref, w_hbm, out_ref, sems, c):
-    group, _, _ = place()
-    return pltpu.make_async_copy(w_hbm.at[0, list_ref[group, c]], out_ref.at[c], sems.at[c])
-
-
-def start_blocks(list_ref, count_ref, w_hbm, out_ref, sems):
-    live = count_ref[place()[0]]
-
-    @pl.loop(0, live)
-    def _(c):
-        block_copy(list_ref, w_hbm, out_ref, sems, c).start()
-
-    @pl.loop(live, out_ref.shape[0])
-    def _(c):
-        out_ref[c] = jnp.zeros(out_ref.shape[1:], out_ref.dtype)
-
-
-def wait_blocks(list_ref, count_ref, w_hbm, out_ref, sems):
-    @pl.loop(0, count_ref[place()[0]])
-    def _(c):
-        block_copy(list_ref, w_hbm, out_ref, sems, c).wait()
+def block_copies(listed, w_hbm, out_ref, sems):
+    return [
+        pltpu.make_async_copy(w_hbm.at[0, block], out_ref.at[c], sems.at[c]) for c, block in enumerate(listed)
+    ]
 
 
 def attend_kernel(
@@ -69,6 +52,8 @@
     mixed_ref,
     kept_ref,
     sent_ref,
+    row_ref,
+    live_ref,
     gate_ref,
     len_ref,
     q_ref,
@@ -95,13 +80,21 @@
         (gain_hbm, gain_ref),
         (list_hbm, list_ref),
         (count_hbm, count_ref),
+        (list_hbm, row_ref),
     ]
     copies = [pltpu.make_async_copy(s, d, sems.at[i]) for i, (s, d) in enumerate(pairs)]
     for copy in copies[6:] + copies[:6]:
         copy.start()
     copies[6].wait()
     copies[7].wait()
-    start_blocks(list_ref, count_ref, gate_hbm, gate_ref, block_sems)
+    group, chip, core = place()
+    early = [list_ref[group, c] for c in range(gate_ref.shape[0])]
+    blocks = block_copies(early, gate_hbm, gate_ref, block_sems)
+    for copy in blocks:
+        copy.start()
+    live_lanes = count_ref[group] * (live_ref.shape[1] // list_ref.shape[1])
+    lane = lax.broadcasted_iota(jnp.int32, live_ref.shape, 1)
+    live_ref[...] = (lane < live_lanes).astype(jnp.float32)
     line = lax.broadcasted_iota(jnp.int32, (lines, lines), 0)
     taken = lax.broadcasted_iota(jnp.int32, (lines, lines), 1)
     swap = (taken == line % rows * heads + line // rows).astype(jnp.float32).astype(jnp.bfloat16)
@@ -151,18 +144,18 @@
     mixed_ref[...] = mixed
     mean_sq = jnp.mean(mixed * mixed, axis=1, keepdims=True)
     normed = (mixed * lax.rsqrt(mean_sq + 1e-05) * gain_ref[...]).astype(jnp.bfloat16)
-    _, chip, core = place()
     step = kept_ref.shape[2]
     for q in range(CHIPS):
         first = normed[:, 2 * q * step : (2 * q + 1) * step]
         second = normed[:, (2 * q + 1) * step : (2 * q + 2) * step]
         kept_ref[q ^ chip] = jnp.where(core == 0, first, second)
         sent_ref[q ^ chip] = jnp.where(core == 0, second, first)
-    wait_blocks(list_ref, count_ref, gate_hbm, gate_ref, block_sems)
+    for copy in blocks + copies[8:]:
+        copy.wait()
 
 
 def attend(
-    queries, k_cache, v_cache, lengths, residual_in, norm_gain, block_list, block_count, gate_w
+    queries, k_cache, v_cache, lengths, residual_in, norm_gain, block_list, block_count, gate_w, early
 ):
     rows, heads, size = queries.shape
     slots, width = k_cache.shape[1:]
@@ -173,10 +166,12 @@
             pltpu.VMEM((rows, model), jnp.float32),
             pltpu.VMEM((CHIPS, rows, model // MDL), jnp.bfloat16),
             pltpu.VMEM((CHIPS, rows, model // MDL), jnp.bfloat16),
-            pltpu.VMEM(block_list.shape[1:] + gate_w.shape[2:], jnp.bfloat16),
+            pltpu.VMEM(block_list.shape, jnp.int32),
+            pltpu.VMEM((1, block_list.shape[1] * gate_w.shape[3]), jnp.float32),
+            pltpu.VMEM((early,) + gate_w.shape[2:], jnp.bfloat16),
         ),
         in_specs=[HBM] * 9,
-        out_specs=(VMEM,) * 4,
+        out_specs=(VMEM,) * 6,
         scratch_shapes=[
             pltpu.SMEM((rows,), jnp.int32),
             pltpu.VMEM((rows, heads, size), jnp.bfloat16),
@@ -186,8 +181,8 @@
             pltpu.VMEM((1, model), jnp.float32),
             pltpu.SMEM(block_list.shape, jnp.int32),
             pltpu.SMEM(block_count.shape, jnp.int32),
-            pltpu.SemaphoreType.DMA((8,)),
-            pltpu.SemaphoreType.DMA(block_list.shape[1:]),
+            pltpu.SemaphoreType.DMA((9,)),
+            pltpu.SemaphoreType.DMA((early,)),
         ],
         compiler_params=pltpu.CompilerParams(vmem_limit_bytes=20 * 2**20),
         name="attend",
@@ -209,46 +204,48 @@
     )
 
 
-def fetch_kernel(list_hbm, count_hbm, w_hbm, _, out_ref, *rest):
-    list_ref, count_ref, sems, block_sems = rest[-4:]
-    copies = [
-        pltpu.make_async_copy(list_hbm, list_ref, sems.at[0]),
-        pltpu.make_async_copy(count_hbm, count_ref, sems.at[1]),
-    ]
+def fetch_kernel(firsts, rows_ref, *rest):
+    parts = len(firsts)
+    row = rows_ref[pl.ds(place()[0], 1), :]
+    at = lax.broadcasted_iota(jnp.int32, row.shape, 1)
+    copies = []
+    for i, first in enumerate(firsts):
+        out_ref = rest[parts + 1 + i]
+        listed = [jnp.sum(jnp.where(at == first + c, row, 0)) for c in range(out_ref.shape[0])]
+        copies += block_copies(listed, rest[i], out_ref, rest[-parts + i])
     for copy in copies:
         copy.start()
     for copy in copies:
         copy.wait()
-    start_blocks(list_ref, count_ref, w_hbm, out_ref, block_sems)
-    wait_blocks(list_ref, count_ref, w_hbm, out_ref, block_sems)
-
-
-def fetch(block_list, block_count, weights, held, name, passed=True):
-    count = block_list.shape[1]
-    size = math.prod(weights.shape[2:])
-    blocks = pltpu.VMEM((count,) + weights.shape[2:], jnp.bfloat16)
+
+
+def fetch(rows, parts, held, name, passed):
+    out_shape = [pltpu.VMEM((stop - first,) + w.shape[2:], jnp.bfloat16) for w, first, stop in parts]
+    size = 2 * sum(math.prod(blocks.shape) for blocks in out_shape)
+    out_specs = [VMEM] * len(parts)
+    if passed:
+        out_shape.append(jax.ShapeDtypeStruct(held.shape, held.dtype))
+        out_specs.append(ANY)
     return pl.pallas_call(
-        fetch_kernel,
-        out_shape=(blocks, jax.ShapeDtypeStruct(held.shape, held.dtype)) if passed else blocks,
-        in_specs=[HBM] * 3 + [ANY],
-        out_specs=(VMEM, ANY) if passed else VMEM,
-        input_output_aliases={3: 1} if passed else {},
-        scratch_shapes=[
-            pltpu.SMEM(block_list.shape, jnp.int32),
-            pltpu.SMEM(block_count.shape, jnp.int32),
-            pltpu.SemaphoreType.DMA((2,)),
-            pltpu.SemaphoreType.DMA((count,)),
-        ],
-        compiler_params=pltpu.CompilerParams(vmem_limit_bytes=10 * 2**20),
-        cost_estimate=pl.CostEstimate(flops=0, bytes_accessed=4 * count * size, transcendentals=0),
+        functools.partial(fetch_kernel, [first for _, first, _ in parts]),
+        out_shape=out_shape,
+        in_specs=[VMEM] + [HBM] * len(parts) + [ANY],
+        out_specs=out_specs,
+        input_output_aliases={1 + len(parts): len(parts)} if passed else {},
+        scratch_shapes=[pltpu.SemaphoreType.DMA((stop - first,)) for _, first, stop in parts],
+        compiler_params=pltpu.CompilerParams(vmem_limit_bytes=12 * 2**20),
+        cost_estimate=pl.CostEstimate(flops=0, bytes_accessed=2 * size, transcendentals=0),
         name=name,
-    )(in_hbm(block_list), in_hbm(block_count), in_hbm(weights), held)
-
-
-def gate_up_kernel(arrived_ref, gate_ref, up_ref, keep_ref, sent_ref, x_ref):
+    )(rows, *(in_hbm(w) for w, _, _ in parts), held)
+
+
+def gate_up_kernel(arrived_ref, gate_near, gate_far, up_near, up_far, live_ref, keep_ref, sent_ref, x_ref):
     groups, _, _, rows, _ = arrived_ref.shape
     half = keep_ref.shape[0]
-    count, _, unit = gate_ref.shape
+    unit = gate_near.shape[2]
+    gates = [near_or_far.at[c] for near_or_far in (gate_near, gate_far) for c in range(near_or_far.shape[0])]
+    ups = [near_or_far.at[c] for near_or_far in (up_near, up_far) for c in range(near_or_far.shape[0])]
+    count = len(gates)
     for core in range(CORES):
         for chip in range(CHIPS):
             for group in range(groups):
@@ -256,38 +253,43 @@
                 x_ref[at : at + rows, :] = arrived_ref[group, chip, core].astype(jnp.float32)
     x = x_ref[...].astype(jnp.bfloat16)
     for c in range(count):
-        both = jnp.concatenate([gate_ref[c], up_ref[c]], axis=1)
+        both = jnp.concatenate([gates[c][...], ups[c][...]], axis=1)
         pair = jnp.dot(x, both, preferred_element_type=jnp.float32)
         for k in range(2):
             part = pair[:, k * unit : (k + 1) * unit]
+            if k == 0:
+                live = live_ref[:, c * unit : (c + 1) * unit] > 0.0
+                part = jnp.where(live, part, 0.0)
             at = pl.ds((k * count + c) * unit, unit)
             keep_ref[:, at] = part[:half]
             sent_ref[:, at] = part[half:].astype(jnp.bfloat16)
 
 
-def gate_up(arrived, gate, up):
+def gate_up(arrived, gate, up, live):
     rows = math.prod(arrived.shape[:4])
-    count, depth, unit = gate.shape
+    _, depth, unit = gate[0].shape
+    wide = 2 * unit * sum(part.shape[0] for part in gate)
     return pl.pallas_call(
         gate_up_kernel,
         out_shape=(
-            pltpu.VMEM((rows // 2, 2 * count * unit), jnp.float32),
-            pltpu.VMEM((rows // 2, 2 * count * unit), jnp.bfloat16),
+            pltpu.VMEM((rows // 2, wide), jnp.float32),
+            pltpu.VMEM((rows // 2, wide), jnp.bfloat16),
         ),
-        in_specs=[VMEM] * 3,
+        in_specs=[VMEM] * 6,
         out_specs=(VMEM, VMEM),
         scratch_shapes=[pltpu.VMEM((rows, depth), jnp.float32)],
         compiler_params=pltpu.CompilerParams(vmem_limit_bytes=24 * 2**20),
         name="gate_up",
-    )(arrived, gate, up)
-
-
-def down_kernel(near_ref, far_ref, w_ref, out_ref):
+    )(arrived, *gate, *up, live)
+
+
+def down_kernel(*refs):
+    *pieces, w_ref, out_ref = refs
     count, unit, depth = w_ref.shape
     devices, rows, _ = out_ref.shape
     groups = devices // MDL
     group, chip, core = place()
-    hidden = jnp.concatenate([near_ref[...], far_ref[...]], axis=0)
+    hidden = jnp.concatenate([piece[...] for piece in pieces], axis=0)
     step = min(512, depth)
     for n in range(depth // step):
         at = pl.ds(n * step, step)
@@ -299,16 +301,16 @@
             out_ref[owner, :, at] = total[r * rows : (r + 1) * rows].astype(jnp.bfloat16)
 
 
-def down(near, far, weights, devices):
-    rows = 2 * near.shape[0] // devices
+def down(pieces, weights, devices):
+    rows = sum(piece.shape[0] for piece in pieces) // devices
     return pl.pallas_call(
         down_kernel,
         out_shape=pltpu.VMEM((devices, rows, weights.shape[2]), jnp.bfloat16),
-        in_specs=[VMEM] * 3,
+        in_specs=[VMEM] * (len(pieces) + 1),
         out_specs=VMEM,
         compiler_params=pltpu.CompilerParams(vmem_limit_bytes=20 * 2**20),
         name="down",
-    )(near, far, weights)
+    )(*pieces, weights)
 
 
 def finish_kernel(mixed_ref, back_ref, out_ref):
@@ -347,33 +349,49 @@
     dev_count = lax.axis_size("hid")
     group_total = dev_count // MDL
     rows_dev = queries.shape[0]
-    units = block_list.shape[1] * gate_w.shape[3]
+    count = block_list.shape[1]
+    units = count * gate_w.shape[3]
     masks = [chip * CORES for chip in range(CHIPS)]
     far_first = range(CHIPS - 1, 0, -1)
-
-    mixed_rows, kept, sent, gate = attend(
-        queries, k_cache, v_cache, lengths, residual_in, norm_gain, block_list, block_count, gate_w
+    gate_early = max(1, count * 4 // 7)
+    up_early = max(1, count * 2 // 7)
+
+    mixed_rows, kept, sent, listed, live, gate_near = attend(
+        queries,
+        k_cache,
+        v_cache,
+        lengths,
+        residual_in,
+        norm_gain,
+        block_list,
+        block_count,
+        gate_w,
+        gate_early,
     )
     pair = jnp.stack([kept, from_partner(sent, 1)], axis=1)
     came = {chip: from_partner(pair[chip], masks[chip]) for chip in far_first}
-    arrived = jnp.stack([pair[0]] + [came[chip] for chip in range(1, CHIPS)])[None]
-    up = fetch(block_list, block_count, up_w, arrived, "fetch_up", passed=False)
+    middle = [(gate_w, gate_early, count), (up_w, 0, up_early)]
+    gate_far, up_near, own = fetch(listed, middle, pair[0], "fetch_middle", True)
+    arrived = jnp.stack([own] + [came[chip] for chip in range(1, CHIPS)])[None]
+    (up_far,) = fetch(listed, [(up_w, up_early, count)], arrived, "fetch_up", False)
     for level in range(group_total.bit_length() - 1):
         arrived = jnp.concatenate([arrived, from_partner(arrived, MDL << level)], axis=0)
 
-    part, sent = gate_up(arrived, gate, up)
+    part, sent = gate_up(arrived, (gate_near, gate_far), (up_near, up_far), live)
     part = part + from_partner(sent, 1).astype(jnp.float32)
     part = part.reshape(CHIPS, group_total * rows_dev, 2 * units)
     came = [from_partner(part[chip].astype(jnp.bfloat16), masks[chip]) for chip in far_first]
-    down_rows, total = fetch(block_list, block_count, down_w, part[0], "fetch_down")
+    down_rows, total = fetch(listed, [(down_w, 0, count)], part[0], "fetch_down", True)
     for piece in came:
         total = total + piece.astype(jnp.float32)
     hidden = (jnp.maximum(total[:, :units], 0.0) * total[:, units:]).astype(jnp.bfloat16)
 
-    came = {chip: from_partner(hidden, masks[chip]) for chip in far_first}
-    near = jnp.concatenate([hidden] + [came[chip] for chip in range(1, CHIPS)], axis=0)
-    far = from_partner(near, 1)
-    ffn_part = down(near, far, down_rows, dev_count)
+    pieces = [hidden] * (2 * CHIPS)
+    pieces[CHIPS] = from_partner(hidden, 1)
+    for chip in far_first:
+        pieces[chip] = from_partner(hidden, masks[chip])
+        pieces[CHIPS + chip] = from_partner(pieces[chip], 1)
+    ffn_part = down(pieces, down_rows, dev_count)
     returned = lax.all_to_all(ffn_part, "hid", split_axis=0, concat_axis=0, tiled=True)
     return finish(mixed_rows, returned)
 

time: 56.7 us -> 55.6 us (0.981)
  waiting for transfers between devices: 13.4 us -> 9.77 us
  Pallas kernels: 14.5 us -> 17.2 us
    ppermute x13 -> x16, waiting for transfers between devices: 13.4 us -> 9.77 us  [from_partner(): return lax.ppermute(value, 'hid', pairs)]
    pallas_call x3 -> x4, Pallas kernels: 8.44 us -> 11.6 us  [the longest x3 8.96 us: fetch(): pl.pallas_call(functools.partial(fetch_kernel, [first for _, first, _ in...]
    ppermute x13 -> x16, starting transfers between devices: 15.4 us -> 15 us  [from_partner(): return lax.ppermute(value, 'hid', pairs)]
  transfers between devices with their start and end apart: 13 -> 16, of which waited for: 12 -> 13; matrix products, arithmetic and copies ran while one was open for 0% -> 0% of each run, Pallas kernels for 10% -> 16%
where the time goes in v4:
time: 55.6 us; the launch traced here: 55.4 us
  Pallas kernels  17.2 us (31%)
  starting transfers between devices  15 us (27%)
  blocking collectives  12.9 us (23%)
  waiting for transfers between devices  9.77 us (18%)
    ppermute x16, starting transfers between devices, from_partner(): return lax.ppermute(value, 'hid', pairs)  15 us
    all_to_all x1, blocking collectives, on_device(): lax.all_to_all(ffn_part, 'hid', split_axis=0, concat_axis=0, tiled=True)  12.9 us
    ppermute x16, waiting for transfers between devices, from_partner(): return lax.ppermute(value, 'hid', pairs)  9.77 us
    pallas_call x3, Pallas kernels, fetch(): pl.pallas_call(functools.partial(fetch_kernel, [first for _, first, _ in...  8.96 us
    pallas_call x1, Pallas kernels, attend(): pl.pallas_call(functools.partial(attend_kernel, width // size), out_shape...  3.52 us
    pallas_call x1, Pallas kernels, gate_up(): pl.pallas_call(gate_up_kernel, out_shape=(pltpu.VMEM((rows // 2, wide), j...  2.64 us
    pallas_call x1, Pallas kernels, down(): pl.pallas_call(down_kernel, out_shape=pltpu.VMEM((devices, rows, weights....  1.39 us
  transfers between devices with their start and end apart: 16, of which 13 were waited for; matrix products, arithmetic and copies ran while one was open for 0% of the time, Pallas kernels for 16%

profile of v4, /device:TPU:0, one launch (start us, length us, event | category | flops | bytes accessed | tf_op | source)
XLA Modules:
  0.0 55.4 jit_solution(10639992236876622756)
XLA Ops:
  0.0 3.5 %attend.1 = (f32[4,8192]{1,0:T(4,128)S(1)}, bf16[4,4,1024]{2,1,0:T(4,128)(2,1)S(1)}, bf16[4,4,1024]{2,1,0:T(4,128)(2,1)S(1)}, s32[2,28]{1,0:T(2,128)S(1)}, f32[1...) custom-call(s32[4]{0:T(128)} %len_hbm.1, bf16[4,64,128]{2,1,0:T(8,128)(2,1)} %q_hbm.1, bf16[4,192,1024]{2,1,0:T(8,128)(2,1)} %k_hbm.1, ...), custom_call_target="tpu_custom_call" | custom-call | tf_op jit(solution)/shard_map/attend/pallas_call | solution.py:163
  3.5 0.5 collective-permute-start
  4.0 0.9 %collective-permute-done = bf16[4,4,1024]{2,1,0:T(4,128)(2,1)S(1)} collective-permute-done((bf16[4,4,1024]{2,1,0:T(4,128)(2,1)S(1)}, bf16[4,4,1024]{2,1,0:T(4,128)(2,1)S(1)}, u32[]{:S(2)}, u32[]{:S(2)}) %collective-permute-start) | collective-permute-done | bytes 32800 | tf_op jit(solution)/shard_map/ppermute | solution.py:23
  5.0 2.9 %collective-permute-start.1 = (bf16[2,4,1024]{2,1,0:T(4,128)(2,1)S(1)}, bf16[2,4,1024]{2,1,0:T(4,128)(2,1)S(1)}, u32[]{:S(2)}, u32[]{:S(2)}) collective-permute-start(bf16[2,4,1024]{2,1,0:T(4,128)(2,1)S(1)} %get-tuple-element.37), channel_id=1, source_target_pairs={{0,2},{1,3},{2,0},{3,1},{4,6},{5,7},{6,4},{7,5},{8,10},{9,11},{10,... | collective-permute-start | bytes 49160 | tf_op jit(solution)/shard_map/ppermute | solution.py:23
  7.9 1.5 %collective-permute-start.3 = (bf16[2,4,1024]{2,1,0:T(4,128)(2,1)S(1)}, bf16[2,4,1024]{2,1,0:T(4,128)(2,1)S(1)}, u32[]{:S(2)}, u32[]{:S(2)}) collective-permute-start(bf16[2,4,1024]{2,1,0:T(4,128)(2,1)S(1)} %get-tuple-element.38), channel_id=1, source_target_pairs={{0,6},{1,7},{2,4},{3,5},{4,2},{5,3},{6,0},{7,1},{8,14},{9,15},{10,... | collective-permute-start | bytes 49160 | tf_op jit(solution)/shard_map/ppermute | solution.py:23
  9.5 2.8 %fetch_middle.1 = (bf16[12,1024,128]{2,1,0:T(8,128)(2,1)S(1)}, bf16[8,1024,128]{2,1,0:T(8,128)(2,1)S(1)}, bf16[2,4,1024]{2,1,0:T(4,128)(2,1)S(1)}) custom-call(s32[2,28]{1,0:T(2,128)S(1)} %get-tuple-element.19.rows_ref, bf16[1,56,1024,128]{3,2,1,0:T(8,128)(2,1)} %rest_0_.3, bf16[1,56,1024,128]{3,2,1,0:T(8,128)(2,1)} %rest_0_.4, ...), custom_call_target="tpu_custom_call", output_to_operand_aliasing={{2}: (3, {})} | custom-call | bytes 10485760 | tf_op jit(solution)/shard_map/fetch_middle/pallas_call | solution.py:229
  12.2 0.3 collective-permute-done.3
  12.5 0.6 %collective-permute-done.2 = bf16[2,4,1024]{2,1,0:T(4,128)(2,1)S(1)} collective-permute-done((bf16[2,4,1024]{2,1,0:T(4,128)(2,1)S(1)}, bf16[2,4,1024]{2,1,0:T(4,128)(2,1)S(1)}, u32[]{:S(2)}, u32[]{:S(2)}) %collective-permute-start.2) | collective-permute-done | bytes 16416 | tf_op jit(solution)/shard_map/ppermute | solution.py:23
  13.2 2.7 %collective-permute-start.4 = (bf16[1,4,2,4,1024]{4,3,2,1,0:T(4,128)(2,1)S(1)}, bf16[1,4,2,4,1024]{4,3,2,1,0:T(4,128)(2,1)S(1)}, u32[]{:S(2)}, u32[]{:S(2)}) collective-permute-start(bf16[1,4,2,4,1024]{4,3,2,1,0:T(4,128)(2,1)S(1)} %maximum_bitcast_fusion.rest_1_), channel_id=1, source_target_pairs={{0,8},{1,9},{2,10},{3,11},{4,12},{5,13},{6,14},{7,15},{8,0},{9,1},... | collective-permute-start | bytes 196616 | tf_op jit(solution)/shard_map/ppermute | solution.py:23
  15.9 2.8 %fetch_up.1.up_far = bf16[20,1024,128]{2,1,0:T(8,128)(2,1)S(1)} custom-call(s32[2,28]{1,0:T(2,128)S(1)} %get-tuple-element.19.rows_ref, bf16[1,56,1024,128]{3,2,1,0:T(8,128)(2,1)} %rest_0_.4, bf16[1,4,2,4,1024]{4,3,2,1,0:T(4,128)(2,1)S(1)} %maximum_bitcast_fusion.rest_1_), custom_call_target="tpu_custom_call" | custom-call | bytes 10485760 | tf_op jit(solution)/shard_map/fetch_up/pallas_call | solution.py:229
  18.6 0.5 collective-permute-done.4
  19.2 2.6 %gate_up.1 = (f32[32,7168]{1,0:T(8,128)S(1)}, bf16[32,7168]{1,0:T(8,128)(2,1)S(1)}) custom-call(bf16[2,4,2,4,1024]{4,3,2,1,0:T(4,128)(2,1)S(1)} %pad_maximum_fusion.arrived_ref, bf16[16,1024,128]{2,1,0:T(8,128)(2,1)S(1)} %get-tuple-element.23.gate_near, bf16[12,1024,128]{2,1,0:T(8,128)(2,1)S(1)} %get-tuple-element.24.gate_far, ...), custom_call_target="tpu_custom_call" | custom-call | tf_op jit(solution)/shard_map/gate_up/pallas_call | solution.py:272
  22.0 1.8 %collective-permute-done.5 = bf16[32,7168]{1,0:T(8,128)(2,1)S(1)} collective-permute-done((bf16[32,7168]{1,0:T(8,128)(2,1)S(1)}, bf16[32,7168]{1,0:T(8,128)(2,1)S(1)}, u32[]{:S(2)}, u32[]{:S(2)}) %collective-permute-start.5) | collective-permute-done | bytes 458784 | tf_op jit(solution)/shard_map/ppermute | solution.py:23
  23.8 0.1 fusion.8
  23.9 1.6 %collective-permute-start.6 = (bf16[8,7168]{1,0:T(8,128)(2,1)S(1)}, bf16[8,7168]{1,0:T(8,128)(2,1)S(1)}, u32[]{:S(2)}, u32[]{:S(2)}) collective-permute-start(bf16[8,7168]{1,0:T(8,128)(2,1)S(1)} %get-tuple-element.33), channel_id=1, source_target_pairs={{0,6},{1,7},{2,4},{3,5},{4,2},{5,3},{6,0},{7,1},{8,14},{9,15},{10,... | collective-permute-start | bytes 344072 | tf_op jit(solution)/shard_map/ppermute | solution.py:23
  25.5 0.5 collective-permute-start.8
  26.0 1.4 %collective-permute-start.7 = (bf16[8,7168]{1,0:T(8,128)(2,1)S(1)}, bf16[8,7168]{1,0:T(8,128)(2,1)S(1)}, u32[]{:S(2)}, u32[]{:S(2)}) collective-permute-start(bf16[8,7168]{1,0:T(8,128)(2,1)S(1)} %get-tuple-element.35), channel_id=1, source_target_pairs={{0,4},{1,5},{2,6},{3,7},{4,0},{5,1},{6,2},{7,3},{8,12},{9,13},{10,... | collective-permute-start | bytes 344072 | tf_op jit(solution)/shard_map/ppermute | solution.py:23
  27.5 3.4 %fetch_down.1 = (bf16[28,128,1024]{2,1,0:T(8,128)(2,1)S(1)}, f32[8,7168]{1,0:T(8,128)S(1)}) custom-call(s32[2,28]{1,0:T(2,128)S(1)} %get-tuple-element.19.rows_ref, bf16[1,56,128,1024]{3,2,1,0:T(8,128)(2,1)} %rest_0_.5, f32[8,7168]{1,0:T(8,128)S(1)} %slice.53.rest_1_), custom_call_target="tpu_custom_call", output_to_operand_aliasing={{1}: (2, {})} | custom-call | bytes 14680064 | tf_op jit(solution)/shard_map/fetch_down/pallas_call | solution.py:229
  30.9 1.6 %collective-permute-done.8 = bf16[8,7168]{1,0:T(8,128)(2,1)S(1)} collective-permute-done((bf16[8,7168]{1,0:T(8,128)(2,1)S(1)}, bf16[8,7168]{1,0:T(8,128)(2,1)S(1)}, u32[]{:S(2)}, u32[]{:S(2)}) %collective-permute-start.8) | collective-permute-done | bytes 114720 | tf_op jit(solution)/shard_map/ppermute | solution.py:23
  32.5 0.1 collective-permute-done.7
  32.7 1.5 %collective-permute-start.11 = (bf16[8,3584]{1,0:T(8,128)(2,1)S(1)}, bf16[8,3584]{1,0:T(8,128)(2,1)S(1)}, u32[]{:S(2)}, u32[]{:S(2)}) collective-permute-start(bf16[8,3584]{1,0:T(8,128)(2,1)S(1)} %fusion.refs_0_), channel_id=1, source_target_pairs={{0,6},{1,7},{2,4},{3,5},{4,2},{5,3},{6,0},{7,1},{8,14},{9,15},{10,... | collective-permute-start | bytes 172040 | tf_op jit(solution)/shard_map/ppermute | solution.py:23
  34.2 0.8 %collective-permute-start.10 = (bf16[8,3584]{1,0:T(8,128)(2,1)S(1)}, bf16[8,3584]{1,0:T(8,128)(2,1)S(1)}, u32[]{:S(2)}, u32[]{:S(2)}) collective-permute-start(bf16[8,3584]{1,0:T(8,128)(2,1)S(1)} %fusion.refs_0_), channel_id=1, source_target_pairs={{0,4},{1,5},{2,6},{3,7},{4,0},{5,1},{6,2},{7,3},{8,12},{9,13},{10,... | collective-permute-start | bytes 172040 | tf_op jit(solution)/shard_map/ppermute | solution.py:23
  35.0 1.3 %collective-permute-start.9 = (bf16[8,3584]{1,0:T(8,128)(2,1)S(1)}, bf16[8,3584]{1,0:T(8,128)(2,1)S(1)}, u32[]{:S(2)}, u32[]{:S(2)}) collective-permute-start(bf16[8,3584]{1,0:T(8,128)(2,1)S(1)} %fusion.refs_0_), channel_id=1, source_target_pairs={{0,2},{1,3},{2,0},{3,1},{4,6},{5,7},{6,4},{7,5},{8,10},{9,11},{10,... | collective-permute-start | bytes 172040 | tf_op jit(solution)/shard_map/ppermute | solution.py:23
  36.2 1.8 %collective-permute-done.11.refs_3_ = bf16[8,3584]{1,0:T(8,128)(2,1)S(1)} collective-permute-done((bf16[8,3584]{1,0:T(8,128)(2,1)S(1)}, bf16[8,3584]{1,0:T(8,128)(2,1)S(1)}, u32[]{:S(2)}, u32[]{:S(2)}) %collective-permute-start.11) | collective-permute-done | bytes 57376 | tf_op jit(solution)/shard_map/ppermute | solution.py:23
  38.0 0.4 collective-permute-done.10.refs_2_
  38.4 0.1 collective-permute-start.14
  38.5 0.6 %collective-permute-done.9.refs_1_ = bf16[8,3584]{1,0:T(8,128)(2,1)S(1)} collective-permute-done((bf16[8,3584]{1,0:T(8,128)(2,1)S(1)}, bf16[8,3584]{1,0:T(8,128)(2,1)S(1)}, u32[]{:S(2)}, u32[]{:S(2)}) %collective-permute-start.9) | collective-permute-done | bytes 57376 | tf_op jit(solution)/shard_map/ppermute | solution.py:23
  39.2 0.4 collective-permute-done.14.refs_6_
  39.6 0.8 %collective-permute-done.13.refs_5_ = bf16[8,3584]{1,0:T(8,128)(2,1)S(1)} collective-permute-done((bf16[8,3584]{1,0:T(8,128)(2,1)S(1)}, bf16[8,3584]{1,0:T(8,128)(2,1)S(1)}, u32[]{:S(2)}, u32[]{:S(2)}) %collective-permute-start.13) | collective-permute-done | bytes 57376 | tf_op jit(solution)/shard_map/ppermute | solution.py:23
  40.4 1.4 %down.1 = bf16[16,4,1024]{2,1,0:T(4,128)(2,1)S(1)} custom-call(bf16[8,3584]{1,0:T(8,128)(2,1)S(1)} %fusion.refs_0_, bf16[8,3584]{1,0:T(8,128)(2,1)S(1)} %collective-permute-done.9.refs_1_, bf16[8,3584]{1,0:T(8,128)(2,1)S(1)} %collective-permute-done.10.refs_2_, bf16[8,3584]{1,0:T(8,128)(2,1)S(1)} %collective-permute-done.11.refs_3_, ...), custom_call_target="tpu_custom_call" | custom-call | tf_op jit(solution)/shard_map/down/pallas_call | solution.py:306
  41.8 12.9 %all_to_all.5.back_ref = bf16[16,4,1024]{2,1,0:T(4,128)(2,1)S(1)} all-to-all(bf16[16,4,1024]{2,1,0:T(4,128)(2,1)S(1)} %down.1), channel_id=1, replica_groups=mesh['groups'=2,'hid'=16] {'hid'}, dimensions={0} | all-to-all | bytes 262144 | tf_op jit(solution)/shard_map/all_to_all | solution.py:395
  54.7 0.7 %finish.1 = bf16[4,8192]{1,0:T(4,128)(2,1)} custom-call(f32[4,8192]{1,0:T(4,128)S(1)} %get-tuple-element.18.mixed_ref, bf16[16,4,1024]{2,1,0:T(4,128)(2,1)S(1)} %all_to_all.5.back_ref), custom_call_target="tpu_custom_call" | custom-call | tf_op jit(solution)/shard_map/finish/pallas_call | solution.py:326
  (16 shorter events, 0.5 us)
Async XLA Ops:
  3.5 1.4 %collective-permute-start = (bf16[4,4,1024]{2,1,0:T(4,128)(2,1)S(1)}, bf16[4,4,1024]{2,1,0:T(4,128)(2,1)S(1)}, u32[]{:S(2)}, u32[]{:S(2)}) collective-permute-start(bf16[4,4,1024]{2,1,0:T(4,128)(2,1)S(1)} %get-tuple-element.21), channel_id=1, source_target_pairs={{0,1},{1,0},{2,3},{3,2},{4,5},{5,4},{6,7},{7,6},{8,9},{9,8},{10,11... | collective-permute-start | bytes 98312 | tf_op jit(solution)/shard_map/ppermute | solution.py:23
  5.0 7.3 %collective-permute-start.1 = (bf16[2,4,1024]{2,1,0:T(4,128)(2,1)S(1)}, bf16[2,4,1024]{2,1,0:T(4,128)(2,1)S(1)}, u32[]{:S(2)}, u32[]{:S(2)}) collective-permute-start(bf16[2,4,1024]{2,1,0:T(4,128)(2,1)S(1)} %get-tuple-element.37), channel_id=1, source_target_pairs={{0,2},{1,3},{2,0},{3,1},{4,6},{5,7},{6,4},{7,5},{8,10},{9,11},{10,... | collective-permute-start | bytes 49160 | tf_op jit(solution)/shard_map/ppermute | solution.py:23
  7.9 4.6 %collective-permute-start.3 = (bf16[2,4,1024]{2,1,0:T(4,128)(2,1)S(1)}, bf16[2,4,1024]{2,1,0:T(4,128)(2,1)S(1)}, u32[]{:S(2)}, u32[]{:S(2)}) collective-permute-start(bf16[2,4,1024]{2,1,0:T(4,128)(2,1)S(1)} %get-tuple-element.38), channel_id=1, source_target_pairs={{0,6},{1,7},{2,4},{3,5},{4,2},{5,3},{6,0},{7,1},{8,14},{9,15},{10,... | collective-permute-start | bytes 49160 | tf_op jit(solution)/shard_map/ppermute | solution.py:23
  9.4 3.7 %collective-permute-start.2 = (bf16[2,4,1024]{2,1,0:T(4,128)(2,1)S(1)}, bf16[2,4,1024]{2,1,0:T(4,128)(2,1)S(1)}, u32[]{:S(2)}, u32[]{:S(2)}) collective-permute-start(bf16[2,4,1024]{2,1,0:T(4,128)(2,1)S(1)} %get-tuple-element.39), channel_id=1, source_target_pairs={{0,4},{1,5},{2,6},{3,7},{4,0},{5,1},{6,2},{7,3},{8,12},{9,13},{10,... | collective-permute-start | bytes 49160 | tf_op jit(solution)/shard_map/ppermute | solution.py:23
  13.2 5.9 %collective-permute-start.4 = (bf16[1,4,2,4,1024]{4,3,2,1,0:T(4,128)(2,1)S(1)}, bf16[1,4,2,4,1024]{4,3,2,1,0:T(4,128)(2,1)S(1)}, u32[]{:S(2)}, u32[]{:S(2)}) collective-permute-start(bf16[1,4,2,4,1024]{4,3,2,1,0:T(4,128)(2,1)S(1)} %maximum_bitcast_fusion.rest_1_), channel_id=1, source_target_pairs={{0,8},{1,9},{2,10},{3,11},{4,12},{5,13},{6,14},{7,15},{8,0},{9,1},... | collective-permute-start | bytes 196616 | tf_op jit(solution)/shard_map/ppermute | solution.py:23
  21.9 1.9 %collective-permute-start.5 = (bf16[32,7168]{1,0:T(8,128)(2,1)S(1)}, bf16[32,7168]{1,0:T(8,128)(2,1)S(1)}, u32[]{:S(2)}, u32[]{:S(2)}) collective-permute-start(bf16[32,7168]{1,0:T(8,128)(2,1)S(1)} %get-tuple-element.28), channel_id=1, source_target_pairs={{0,1},{1,0},{2,3},{3,2},{4,5},{5,4},{6,7},{7,6},{8,9},{9,8},{10,11... | collective-permute-start | bytes 1376264 | tf_op jit(solution)/shard_map/ppermute | solution.py:23
  23.9 7.0 %collective-permute-start.6 = (bf16[8,7168]{1,0:T(8,128)(2,1)S(1)}, bf16[8,7168]{1,0:T(8,128)(2,1)S(1)}, u32[]{:S(2)}, u32[]{:S(2)}) collective-permute-start(bf16[8,7168]{1,0:T(8,128)(2,1)S(1)} %get-tuple-element.33), channel_id=1, source_target_pairs={{0,6},{1,7},{2,4},{3,5},{4,2},{5,3},{6,0},{7,1},{8,14},{9,15},{10,... | collective-permute-start | bytes 344072 | tf_op jit(solution)/shard_map/ppermute | solution.py:23
  25.5 7.0 %collective-permute-start.8 = (bf16[8,7168]{1,0:T(8,128)(2,1)S(1)}, bf16[8,7168]{1,0:T(8,128)(2,1)S(1)}, u32[]{:S(2)}, u32[]{:S(2)}) collective-permute-start(bf16[8,7168]{1,0:T(8,128)(2,1)S(1)} %get-tuple-element.34), channel_id=1, source_target_pairs={{0,2},{1,3},{2,0},{3,1},{4,6},{5,7},{6,4},{7,5},{8,10},{9,11},{10,... | collective-permute-start | bytes 344072 | tf_op jit(solution)/shard_map/ppermute | solution.py:23
  26.0 6.6 %collective-permute-start.7 = (bf16[8,7168]{1,0:T(8,128)(2,1)S(1)}, bf16[8,7168]{1,0:T(8,128)(2,1)S(1)}, u32[]{:S(2)}, u32[]{:S(2)}) collective-permute-start(bf16[8,7168]{1,0:T(8,128)(2,1)S(1)} %get-tuple-element.35), channel_id=1, source_target_pairs={{0,4},{1,5},{2,6},{3,7},{4,0},{5,1},{6,2},{7,3},{8,12},{9,13},{10,... | collective-permute-start | bytes 344072 | tf_op jit(solution)/shard_map/ppermute | solution.py:23
  32.7 5.3 %collective-permute-start.11 = (bf16[8,3584]{1,0:T(8,128)(2,1)S(1)}, bf16[8,3584]{1,0:T(8,128)(2,1)S(1)}, u32[]{:S(2)}, u32[]{:S(2)}) collective-permute-start(bf16[8,3584]{1,0:T(8,128)(2,1)S(1)} %fusion.refs_0_), channel_id=1, source_target_pairs={{0,6},{1,7},{2,4},{3,5},{4,2},{5,3},{6,0},{7,1},{8,14},{9,15},{10,... | collective-permute-start | bytes 172040 | tf_op jit(solution)/shard_map/ppermute | solution.py:23
  34.2 4.2 %collective-permute-start.10 = (bf16[8,3584]{1,0:T(8,128)(2,1)S(1)}, bf16[8,3584]{1,0:T(8,128)(2,1)S(1)}, u32[]{:S(2)}, u32[]{:S(2)}) collective-permute-start(bf16[8,3584]{1,0:T(8,128)(2,1)S(1)} %fusion.refs_0_), channel_id=1, source_target_pairs={{0,4},{1,5},{2,6},{3,7},{4,0},{5,1},{6,2},{7,3},{8,12},{9,13},{10,... | collective-permute-start | bytes 172040 | tf_op jit(solution)/shard_map/ppermute | solution.py:23
  35.0 4.2 %collective-permute-start.9 = (bf16[8,3584]{1,0:T(8,128)(2,1)S(1)}, bf16[8,3584]{1,0:T(8,128)(2,1)S(1)}, u32[]{:S(2)}, u32[]{:S(2)}) collective-permute-start(bf16[8,3584]{1,0:T(8,128)(2,1)S(1)} %fusion.refs_0_), channel_id=1, source_target_pairs={{0,2},{1,3},{2,0},{3,1},{4,6},{5,7},{6,4},{7,5},{8,10},{9,11},{10,... | collective-permute-start | bytes 172040 | tf_op jit(solution)/shard_map/ppermute | solution.py:23
  36.2 2.9 %collective-permute-start.12 = (bf16[8,3584]{1,0:T(8,128)(2,1)S(1)}, bf16[8,3584]{1,0:T(8,128)(2,1)S(1)}, u32[]{:S(2)}, u32[]{:S(2)}) collective-permute-start(bf16[8,3584]{1,0:T(8,128)(2,1)S(1)} %fusion.refs_0_), channel_id=1, source_target_pairs={{0,1},{1,0},{2,3},{3,2},{4,5},{5,4},{6,7},{7,6},{8,9},{9,8},{10,11... | collective-permute-start | bytes 172040 | tf_op jit(solution)/shard_map/ppermute | solution.py:23
  38.0 1.2 %collective-permute-start.15 = (bf16[8,3584]{1,0:T(8,128)(2,1)S(1)}, bf16[8,3584]{1,0:T(8,128)(2,1)S(1)}, u32[]{:S(2)}, u32[]{:S(2)}) collective-permute-start(bf16[8,3584]{1,0:T(8,128)(2,1)S(1)} %collective-permute-done.11.refs_3_), channel_id=1, source_target_pairs={{0,1},{1,0},{2,3},{3,2},{4,5},{5,4},{6,7},{7,6},{8,9},{9,8},{10,11... | collective-permute-start | bytes 172040 | tf_op jit(solution)/shard_map/ppermute | solution.py:23
  38.4 1.2 %collective-permute-start.14 = (bf16[8,3584]{1,0:T(8,128)(2,1)S(1)}, bf16[8,3584]{1,0:T(8,128)(2,1)S(1)}, u32[]{:S(2)}, u32[]{:S(2)}) collective-permute-start(bf16[8,3584]{1,0:T(8,128)(2,1)S(1)} %collective-permute-done.10.refs_2_), channel_id=1, source_target_pairs={{0,1},{1,0},{2,3},{3,2},{4,5},{5,4},{6,7},{7,6},{8,9},{9,8},{10,11... | collective-permute-start | bytes 172040 | tf_op jit(solution)/shard_map/ppermute | solution.py:23
  39.2 1.2 %collective-permute-start.13 = (bf16[8,3584]{1,0:T(8,128)(2,1)S(1)}, bf16[8,3584]{1,0:T(8,128)(2,1)S(1)}, u32[]{:S(2)}, u32[]{:S(2)}) collective-permute-start(bf16[8,3584]{1,0:T(8,128)(2,1)S(1)} %collective-permute-done.9.refs_1_), channel_id=1, source_target_pairs={{0,1},{1,0},{2,3},{3,2},{4,5},{5,4},{6,7},{7,6},{8,9},{9,8},{10,11... | collective-permute-start | bytes 172040 | tf_op jit(solution)/shard_map/ppermute | solution.py:23

commit v5 on v4

--- a/solution.py
+++ b/solution.py
@@ -239,9 +239,11 @@
     )(rows, *(in_hbm(w) for w, _, _ in parts), held)
 
 
-def gate_up_kernel(arrived_ref, gate_near, gate_far, up_near, up_far, live_ref, keep_ref, sent_ref, x_ref):
+def gate_up_kernel(arrived_ref, gate_near, gate_far, up_near, up_far, live_ref, *rest):
+    *out_refs, x_ref = rest
+    keep_refs, sent_refs = out_refs[:CHIPS], out_refs[CHIPS:]
     groups, _, _, rows, _ = arrived_ref.shape
-    half = keep_ref.shape[0]
+    few = keep_refs[0].shape[0]
     unit = gate_near.shape[2]
     gates = [near_or_far.at[c] for near_or_far in (gate_near, gate_far) for c in range(near_or_far.shape[0])]
     ups = [near_or_far.at[c] for near_or_far in (up_near, up_far) for c in range(near_or_far.shape[0])]
@@ -253,16 +255,16 @@
                 x_ref[at : at + rows, :] = arrived_ref[group, chip, core].astype(jnp.float32)
     x = x_ref[...].astype(jnp.bfloat16)
     for c in range(count):
-        both = jnp.concatenate([gates[c][...], ups[c][...]], axis=1)
-        pair = jnp.dot(x, both, preferred_element_type=jnp.float32)
-        for k in range(2):
-            part = pair[:, k * unit : (k + 1) * unit]
+        for k, w in enumerate((gates[c], ups[c])):
+            part = jnp.dot(x, w[...], preferred_element_type=jnp.float32)
             if k == 0:
                 live = live_ref[:, c * unit : (c + 1) * unit] > 0.0
                 part = jnp.where(live, part, 0.0)
             at = pl.ds((k * count + c) * unit, unit)
-            keep_ref[:, at] = part[:half]
-            sent_ref[:, at] = part[half:].astype(jnp.bfloat16)
+            for chip in range(CHIPS):
+                far = (CHIPS + chip) * few
+                keep_refs[chip][:, at] = part[chip * few : (chip + 1) * few]
+                sent_refs[chip][:, at] = part[far : far + few].astype(jnp.bfloat16)
 
 
 def gate_up(arrived, gate, up, live):
@@ -271,12 +273,10 @@
     wide = 2 * unit * sum(part.shape[0] for part in gate)
     return pl.pallas_call(
         gate_up_kernel,
-        out_shape=(
-            pltpu.VMEM((rows // 2, wide), jnp.float32),
-            pltpu.VMEM((rows // 2, wide), jnp.bfloat16),
-        ),
+        out_shape=[pltpu.VMEM((rows // MDL, wide), jnp.float32)] * CHIPS
+        + [pltpu.VMEM((rows // MDL, wide), jnp.bfloat16)] * CHIPS,
         in_specs=[VMEM] * 6,
-        out_specs=(VMEM, VMEM),
+        out_specs=[VMEM] * (2 * CHIPS),
         scratch_shapes=[pltpu.VMEM((rows, depth), jnp.float32)],
         compiler_params=pltpu.CompilerParams(vmem_limit_bytes=24 * 2**20),
         name="gate_up",
@@ -377,11 +377,12 @@
     for level in range(group_total.bit_length() - 1):
         arrived = jnp.concatenate([arrived, from_partner(arrived, MDL << level)], axis=0)
 
-    part, sent = gate_up(arrived, (gate_near, gate_far), (up_near, up_far), live)
-    part = part + from_partner(sent, 1).astype(jnp.float32)
-    part = part.reshape(CHIPS, group_total * rows_dev, 2 * units)
+    parts = gate_up(arrived, (gate_near, gate_far), (up_near, up_far), live)
+    part = {}
+    for chip in (*far_first, 0):
+        part[chip] = parts[chip] + from_partner(parts[CHIPS + chip], 1).astype(jnp.float32)
     came = [from_partner(part[chip].astype(jnp.bfloat16), masks[chip]) for chip in far_first]
-    down_rows, total = fetch(listed, [(down_w, 0, count)], part[0], "fetch_down", True)
+    (down_rows, total) = fetch(listed, [(down_w, 0, count)], part[0], "fetch_down", True)
     for piece in came:
         total = total + piece.astype(jnp.float32)
     hidden = (jnp.maximum(total[:, :units], 0.0) * total[:, units:]).astype(jnp.bfloat16)

time: 55.6 us -> 54.4 us (0.978)
  starting transfers between devices: 15 us -> 16 us
  waiting for transfers between devices: 9.77 us -> 8.84 us
  blocking collectives: 12.9 us -> 12.2 us
  Pallas kernels: 17.2 us -> 16.6 us
    ppermute x16 -> x19, starting transfers between devices: 15 us -> 16 us  [from_partner(): return lax.ppermute(value, 'hid', pairs)]
    ppermute x16 -> x19, waiting for transfers between devices: 9.77 us -> 8.84 us  [from_partner(): return lax.ppermute(value, 'hid', pairs)]
    all_to_all x1, blocking collectives: 12.9 us -> 12.2 us  [on_device(): lax.all_to_all(ffn_part, 'hid', split_axis=0, concat_axis=0, tiled=True)]
  transfers between devices with their start and end apart: 16 -> 19, of which waited for: 13 -> 10; matrix products, arithmetic and copies ran while one was open for 0% -> 0% of each run, Pallas kernels for 16% -> 17%
where the time goes in v5:
time: 54.4 us; the launch traced here: 54.2 us
  Pallas kernels  16.6 us (31%)
  starting transfers between devices  16 us (29%)
  blocking collectives  12.2 us (22%)
  waiting for transfers between devices  8.84 us (16%)
    ppermute x19, starting transfers between devices, from_partner(): return lax.ppermute(value, 'hid', pairs)  16 us
    all_to_all x1, blocking collectives, on_device(): lax.all_to_all(ffn_part, 'hid', split_axis=0, concat_axis=0, tiled=True)  12.2 us
    pallas_call x3, Pallas kernels, fetch(): pl.pallas_call(functools.partial(fetch_kernel, [first for _, first, _ in...  8.96 us
    ppermute x19, waiting for transfers between devices, from_partner(): return lax.ppermute(value, 'hid', pairs)  8.84 us
    pallas_call x1, Pallas kernels, attend(): pl.pallas_call(functools.partial(attend_kernel, width // size), out_shape...  3.52 us
    pallas_call x1, Pallas kernels, gate_up(): pl.pallas_call(gate_up_kernel, out_shape=[pltpu.VMEM((rows // MDL, wide),...  2.09 us
    pallas_call x1, Pallas kernels, down(): pl.pallas_call(down_kernel, out_shape=pltpu.VMEM((devices, rows, weights....  1.39 us
  transfers between devices with their start and end apart: 19, of which 10 were waited for; matrix products, arithmetic and copies ran while one was open for 0% of the time, Pallas kernels for 17%

profile of v5, /device:TPU:0, one launch (start us, length us, event | category | flops | bytes accessed | tf_op | source)
XLA Modules:
  0.0 54.2 jit_solution(13879212467084204311)
XLA Ops:
  0.0 3.5 %attend.1 = (f32[4,8192]{1,0:T(4,128)S(1)}, bf16[4,4,1024]{2,1,0:T(4,128)(2,1)S(1)}, bf16[4,4,1024]{2,1,0:T(4,128)(2,1)S(1)}, s32[2,28]{1,0:T(2,128)S(1)}, f32[1...) custom-call(s32[4]{0:T(128)} %len_hbm.1, bf16[4,64,128]{2,1,0:T(8,128)(2,1)} %q_hbm.1, bf16[4,192,1024]{2,1,0:T(8,128)(2,1)} %k_hbm.1, ...), custom_call_target="tpu_custom_call" | custom-call | tf_op jit(solution)/shard_map/attend/pallas_call | solution.py:163
  3.5 0.5 collective-permute-start
  4.0 0.9 %collective-permute-done = bf16[4,4,1024]{2,1,0:T(4,128)(2,1)S(1)} collective-permute-done((bf16[4,4,1024]{2,1,0:T(4,128)(2,1)S(1)}, bf16[4,4,1024]{2,1,0:T(4,128)(2,1)S(1)}, u32[]{:S(2)}, u32[]{:S(2)}) %collective-permute-start) | collective-permute-done | bytes 32800 | tf_op jit(solution)/shard_map/ppermute | solution.py:23
  5.0 2.9 %collective-permute-start.1 = (bf16[2,4,1024]{2,1,0:T(4,128)(2,1)S(1)}, bf16[2,4,1024]{2,1,0:T(4,128)(2,1)S(1)}, u32[]{:S(2)}, u32[]{:S(2)}) collective-permute-start(bf16[2,4,1024]{2,1,0:T(4,128)(2,1)S(1)} %get-tuple-element.44), channel_id=1, source_target_pairs={{0,2},{1,3},{2,0},{3,1},{4,6},{5,7},{6,4},{7,5},{8,10},{9,11},{10,... | collective-permute-start | bytes 49160 | tf_op jit(solution)/shard_map/ppermute | solution.py:23
  7.9 1.5 %collective-permute-start.3 = (bf16[2,4,1024]{2,1,0:T(4,128)(2,1)S(1)}, bf16[2,4,1024]{2,1,0:T(4,128)(2,1)S(1)}, u32[]{:S(2)}, u32[]{:S(2)}) collective-permute-start(bf16[2,4,1024]{2,1,0:T(4,128)(2,1)S(1)} %get-tuple-element.45), channel_id=1, source_target_pairs={{0,6},{1,7},{2,4},{3,5},{4,2},{5,3},{6,0},{7,1},{8,14},{9,15},{10,... | collective-permute-start | bytes 49160 | tf_op jit(solution)/shard_map/ppermute | solution.py:23
  9.5 2.8 %fetch_middle.1 = (bf16[12,1024,128]{2,1,0:T(8,128)(2,1)S(1)}, bf16[8,1024,128]{2,1,0:T(8,128)(2,1)S(1)}, bf16[2,4,1024]{2,1,0:T(4,128)(2,1)S(1)}) custom-call(s32[2,28]{1,0:T(2,128)S(1)} %get-tuple-element.25.rows_ref, bf16[1,56,1024,128]{3,2,1,0:T(8,128)(2,1)} %rest_0_.3, bf16[1,56,1024,128]{3,2,1,0:T(8,128)(2,1)} %rest_0_.4, ...), custom_call_target="tpu_custom_call", output_to_operand_aliasing={{2}: (3, {})} | custom-call | bytes 10485760 | tf_op jit(solution)/shard_map/fetch_middle/pallas_call | solution.py:229
  12.2 0.3 collective-permute-done.3
  12.5 0.6 %collective-permute-done.2 = bf16[2,4,1024]{2,1,0:T(4,128)(2,1)S(1)} collective-permute-done((bf16[2,4,1024]{2,1,0:T(4,128)(2,1)S(1)}, bf16[2,4,1024]{2,1,0:T(4,128)(2,1)S(1)}, u32[]{:S(2)}, u32[]{:S(2)}) %collective-permute-start.2) | collective-permute-done | bytes 16416 | tf_op jit(solution)/shard_map/ppermute | solution.py:23
  13.2 2.7 %collective-permute-start.4 = (bf16[1,4,2,4,1024]{4,3,2,1,0:T(4,128)(2,1)S(1)}, bf16[1,4,2,4,1024]{4,3,2,1,0:T(4,128)(2,1)S(1)}, u32[]{:S(2)}, u32[]{:S(2)}) collective-permute-start(bf16[1,4,2,4,1024]{4,3,2,1,0:T(4,128)(2,1)S(1)} %maximum_bitcast_fusion.rest_1_), channel_id=1, source_target_pairs={{0,8},{1,9},{2,10},{3,11},{4,12},{5,13},{6,14},{7,15},{8,0},{9,1},... | collective-permute-start | bytes 196616 | tf_op jit(solution)/shard_map/ppermute | solution.py:23
  15.9 2.8 %fetch_up.1.up_far = bf16[20,1024,128]{2,1,0:T(8,128)(2,1)S(1)} custom-call(s32[2,28]{1,0:T(2,128)S(1)} %get-tuple-element.25.rows_ref, bf16[1,56,1024,128]{3,2,1,0:T(8,128)(2,1)} %rest_0_.4, bf16[1,4,2,4,1024]{4,3,2,1,0:T(4,128)(2,1)S(1)} %maximum_bitcast_fusion.rest_1_), custom_call_target="tpu_custom_call" | custom-call | bytes 10485760 | tf_op jit(solution)/shard_map/fetch_up/pallas_call | solution.py:229
  18.6 0.5 collective-permute-done.4
  19.1 0.1 pad_maximum_fusion.arrived_ref
  19.2 2.1 %gate_up.1 = (f32[8,7168]{1,0:T(8,128)S(1)}, f32[8,7168]{1,0:T(8,128)S(1)}, f32[8,7168]{1,0:T(8,128)S(1)}, f32[8,7168]{1,0:T(8,128)S(1)}, bf16[8,7168]{1,0:T(8,1...) custom-call(bf16[2,4,2,4,1024]{4,3,2,1,0:T(4,128)(2,1)S(1)} %pad_maximum_fusion., ...), custom_call_target="tpu_custom_call" | custom-call | tf_op jit(solution)/shard_map/gate_up/pallas_call | solution.py:274
  21.4 0.5 collective-permute-start.5
  21.9 0.1 collective-permute-start.8
  22.0 0.4 collective-permute-start.10
  22.4 0.3 collective-permute-done.6
  22.8 1.6 %collective-permute-start.7 = (bf16[8,7168]{1,0:T(8,128)(2,1)S(1)}, bf16[8,7168]{1,0:T(8,128)(2,1)S(1)}, u32[]{:S(2)}, u32[]{:S(2)}) collective-permute-start(bf16[8,7168]{1,0:T(8,128)(2,1)S(1)} %add_convert_fusion.2), channel_id=1, source_target_pairs={{0,6},{1,7},{2,4},{3,5},{4,2},{5,3},{6,0},{7,1},{8,14},{9,15},{10,... | collective-permute-start | bytes 344072 | tf_op jit(solution)/shard_map/ppermute | solution.py:23
  24.4 1.5 %collective-permute-start.9 = (bf16[8,7168]{1,0:T(8,128)(2,1)S(1)}, bf16[8,7168]{1,0:T(8,128)(2,1)S(1)}, u32[]{:S(2)}, u32[]{:S(2)}) collective-permute-start(bf16[8,7168]{1,0:T(8,128)(2,1)S(1)} %add_convert_fusion.1), channel_id=1, source_target_pairs={{0,4},{1,5},{2,6},{3,7},{4,0},{5,1},{6,2},{7,3},{8,12},{9,13},{10,... | collective-permute-start | bytes 344072 | tf_op jit(solution)/shard_map/ppermute | solution.py:23
  25.9 0.6 %collective-permute-start.11 = (bf16[8,7168]{1,0:T(8,128)(2,1)S(1)}, bf16[8,7168]{1,0:T(8,128)(2,1)S(1)}, u32[]{:S(2)}, u32[]{:S(2)}) collective-permute-start(bf16[8,7168]{1,0:T(8,128)(2,1)S(1)} %add_convert_fusion), channel_id=1, source_target_pairs={{0,2},{1,3},{2,0},{3,1},{4,6},{5,7},{6,4},{7,5},{8,10},{9,11},{10,... | collective-permute-start | bytes 344072 | tf_op jit(solution)/shard_map/ppermute | solution.py:23
  26.5 3.4 %fetch_down.1 = (bf16[28,128,1024]{2,1,0:T(8,128)(2,1)S(1)}, f32[8,7168]{1,0:T(8,128)S(1)}) custom-call(s32[2,28]{1,0:T(2,128)S(1)} %get-tuple-element.25.rows_ref, bf16[1,56,128,1024]{3,2,1,0:T(8,128)(2,1)} %rest_0_.5, f32[8,7168]{1,0:T(8,128)S(1)} %convert_add_fusion.1.rest_1_), custom_call_target="tpu_custom_call", output_to_operand_aliasing={{1}: (2, {})} | custom-call | bytes 14680064 | tf_op jit(solution)/shard_map/fetch_down/pallas_call | solution.py:229
  30.0 1.4 %collective-permute-done.9 = bf16[8,7168]{1,0:T(8,128)(2,1)S(1)} collective-permute-done((bf16[8,7168]{1,0:T(8,128)(2,1)S(1)}, bf16[8,7168]{1,0:T(8,128)(2,1)S(1)}, u32[]{:S(2)}, u32[]{:S(2)}) %collective-permute-start.9) | collective-permute-done | bytes 114720 | tf_op jit(solution)/shard_map/ppermute | solution.py:23
  31.5 1.5 %collective-permute-start.14 = (bf16[8,3584]{1,0:T(8,128)(2,1)S(1)}, bf16[8,3584]{1,0:T(8,128)(2,1)S(1)}, u32[]{:S(2)}, u32[]{:S(2)}) collective-permute-start(bf16[8,3584]{1,0:T(8,128)(2,1)S(1)} %fusion.refs_0_), channel_id=1, source_target_pairs={{0,6},{1,7},{2,4},{3,5},{4,2},{5,3},{6,0},{7,1},{8,14},{9,15},{10,... | collective-permute-start | bytes 172040 | tf_op jit(solution)/shard_map/ppermute | solution.py:23
  33.1 1.4 %collective-permute-start.13 = (bf16[8,3584]{1,0:T(8,128)(2,1)S(1)}, bf16[8,3584]{1,0:T(8,128)(2,1)S(1)}, u32[]{:S(2)}, u32[]{:S(2)}) collective-permute-start(bf16[8,3584]{1,0:T(8,128)(2,1)S(1)} %fusion.refs_0_), channel_id=1, source_target_pairs={{0,4},{1,5},{2,6},{3,7},{4,0},{5,1},{6,2},{7,3},{8,12},{9,13},{10,... | collective-permute-start | bytes 172040 | tf_op jit(solution)/shard_map/ppermute | solution.py:23
  34.5 0.6 %collective-permute-start.12 = (bf16[8,3584]{1,0:T(8,128)(2,1)S(1)}, bf16[8,3584]{1,0:T(8,128)(2,1)S(1)}, u32[]{:S(2)}, u32[]{:S(2)}) collective-permute-start(bf16[8,3584]{1,0:T(8,128)(2,1)S(1)} %fusion.refs_0_), channel_id=1, source_target_pairs={{0,2},{1,3},{2,0},{3,1},{4,6},{5,7},{6,4},{7,5},{8,10},{9,11},{10,... | collective-permute-start | bytes 172040 | tf_op jit(solution)/shard_map/ppermute | solution.py:23
  35.1 1.6 %collective-permute-done.14.refs_3_ = bf16[8,3584]{1,0:T(8,128)(2,1)S(1)} collective-permute-done((bf16[8,3584]{1,0:T(8,128)(2,1)S(1)}, bf16[8,3584]{1,0:T(8,128)(2,1)S(1)}, u32[]{:S(2)}, u32[]{:S(2)}) %collective-permute-start.14) | collective-permute-done | bytes 57376 | tf_op jit(solution)/shard_map/ppermute | solution.py:23
  36.7 0.7 %collective-permute-done.13.refs_2_ = bf16[8,3584]{1,0:T(8,128)(2,1)S(1)} collective-permute-done((bf16[8,3584]{1,0:T(8,128)(2,1)S(1)}, bf16[8,3584]{1,0:T(8,128)(2,1)S(1)}, u32[]{:S(2)}, u32[]{:S(2)}) %collective-permute-start.13) | collective-permute-done | bytes 57376 | tf_op jit(solution)/shard_map/ppermute | solution.py:23
  37.4 1.2 %collective-permute-done.12.refs_1_ = bf16[8,3584]{1,0:T(8,128)(2,1)S(1)} collective-permute-done((bf16[8,3584]{1,0:T(8,128)(2,1)S(1)}, bf16[8,3584]{1,0:T(8,128)(2,1)S(1)}, u32[]{:S(2)}, u32[]{:S(2)}) %collective-permute-start.12) | collective-permute-done | bytes 57376 | tf_op jit(solution)/shard_map/ppermute | solution.py:23
  38.7 1.2 %collective-permute-done.16.refs_5_ = bf16[8,3584]{1,0:T(8,128)(2,1)S(1)} collective-permute-done((bf16[8,3584]{1,0:T(8,128)(2,1)S(1)}, bf16[8,3584]{1,0:T(8,128)(2,1)S(1)}, u32[]{:S(2)}, u32[]{:S(2)}) %collective-permute-start.16) | collective-permute-done | bytes 57376 | tf_op jit(solution)/shard_map/ppermute | solution.py:23
  39.9 1.4 %down.1 = bf16[16,4,1024]{2,1,0:T(4,128)(2,1)S(1)} custom-call(bf16[8,3584]{1,0:T(8,128)(2,1)S(1)} %fusion.refs_0_, bf16[8,3584]{1,0:T(8,128)(2,1)S(1)} %collective-permute-done.12.refs_1_, bf16[8,3584]{1,0:T(8,128)(2,1)S(1)} %collective-permute-done.13.refs_2_, bf16[8,3584]{1,0:T(8,128)(2,1)S(1)} %collective-permute-done.14.refs_3_, ...), custom_call_target="tpu_custom_call" | custom-call | tf_op jit(solution)/shard_map/down/pallas_call | solution.py:306
  41.3 12.2 %all_to_all.5.back_ref = bf16[16,4,1024]{2,1,0:T(4,128)(2,1)S(1)} all-to-all(bf16[16,4,1024]{2,1,0:T(4,128)(2,1)S(1)} %down.1), channel_id=1, replica_groups=mesh['groups'=2,'hid'=16] {'hid'}, dimensions={0} | all-to-all | bytes 262144 | tf_op jit(solution)/shard_map/all_to_all | solution.py:396
  53.6 0.7 %finish.1 = bf16[4,8192]{1,0:T(4,128)(2,1)} custom-call(f32[4,8192]{1,0:T(4,128)S(1)} %get-tuple-element.24.mixed_ref, bf16[16,4,1024]{2,1,0:T(4,128)(2,1)S(1)} %all_to_all.5.back_ref), custom_call_target="tpu_custom_call" | custom-call | tf_op jit(solution)/shard_map/finish/pallas_call | solution.py:326
  (23 shorter events, 0.5 us)
Async XLA Ops:
  3.5 1.4 %collective-permute-start = (bf16[4,4,1024]{2,1,0:T(4,128)(2,1)S(1)}, bf16[4,4,1024]{2,1,0:T(4,128)(2,1)S(1)}, u32[]{:S(2)}, u32[]{:S(2)}) collective-permute-start(bf16[4,4,1024]{2,1,0:T(4,128)(2,1)S(1)} %get-tuple-element.27), channel_id=1, source_target_pairs={{0,1},{1,0},{2,3},{3,2},{4,5},{5,4},{6,7},{7,6},{8,9},{9,8},{10,11... | collective-permute-start | bytes 98312 | tf_op jit(solution)/shard_map/ppermute | solution.py:23
  5.0 7.3 %collective-permute-start.1 = (bf16[2,4,1024]{2,1,0:T(4,128)(2,1)S(1)}, bf16[2,4,1024]{2,1,0:T(4,128)(2,1)S(1)}, u32[]{:S(2)}, u32[]{:S(2)}) collective-permute-start(bf16[2,4,1024]{2,1,0:T(4,128)(2,1)S(1)} %get-tuple-element.44), channel_id=1, source_target_pairs={{0,2},{1,3},{2,0},{3,1},{4,6},{5,7},{6,4},{7,5},{8,10},{9,11},{10,... | collective-permute-start | bytes 49160 | tf_op jit(solution)/shard_map/ppermute | solution.py:23
  7.9 4.6 %collective-permute-start.3 = (bf16[2,4,1024]{2,1,0:T(4,128)(2,1)S(1)}, bf16[2,4,1024]{2,1,0:T(4,128)(2,1)S(1)}, u32[]{:S(2)}, u32[]{:S(2)}) collective-permute-start(bf16[2,4,1024]{2,1,0:T(4,128)(2,1)S(1)} %get-tuple-element.45), channel_id=1, source_target_pairs={{0,6},{1,7},{2,4},{3,5},{4,2},{5,3},{6,0},{7,1},{8,14},{9,15},{10,... | collective-permute-start | bytes 49160 | tf_op jit(solution)/shard_map/ppermute | solution.py:23
  9.4 3.7 %collective-permute-start.2 = (bf16[2,4,1024]{2,1,0:T(4,128)(2,1)S(1)}, bf16[2,4,1024]{2,1,0:T(4,128)(2,1)S(1)}, u32[]{:S(2)}, u32[]{:S(2)}) collective-permute-start(bf16[2,4,1024]{2,1,0:T(4,128)(2,1)S(1)} %get-tuple-element.46), channel_id=1, source_target_pairs={{0,4},{1,5},{2,6},{3,7},{4,0},{5,1},{6,2},{7,3},{8,12},{9,13},{10,... | collective-permute-start | bytes 49160 | tf_op jit(solution)/shard_map/ppermute | solution.py:23
  13.2 5.9 %collective-permute-start.4 = (bf16[1,4,2,4,1024]{4,3,2,1,0:T(4,128)(2,1)S(1)}, bf16[1,4,2,4,1024]{4,3,2,1,0:T(4,128)(2,1)S(1)}, u32[]{:S(2)}, u32[]{:S(2)}) collective-permute-start(bf16[1,4,2,4,1024]{4,3,2,1,0:T(4,128)(2,1)S(1)} %maximum_bitcast_fusion.rest_1_), channel_id=1, source_target_pairs={{0,8},{1,9},{2,10},{3,11},{4,12},{5,13},{6,14},{7,15},{8,0},{9,1},... | collective-permute-start | bytes 196616 | tf_op jit(solution)/shard_map/ppermute | solution.py:23
  21.3 1.4 %collective-permute-start.6 = (bf16[8,7168]{1,0:T(8,128)(2,1)S(1)}, bf16[8,7168]{1,0:T(8,128)(2,1)S(1)}, u32[]{:S(2)}, u32[]{:S(2)}) collective-permute-start(bf16[8,7168]{1,0:T(8,128)(2,1)S(1)} %get-tuple-element.37), channel_id=1, source_target_pairs={{0,1},{1,0},{2,3},{3,2},{4,5},{5,4},{6,7},{7,6},{8,9},{9,8},{10,11... | collective-permute-start | bytes 344072 | tf_op jit(solution)/shard_map/ppermute | solution.py:23
  21.4 5.1 %collective-permute-start.5 = (bf16[8,7168]{1,0:T(8,128)(2,1)S(1)}, bf16[8,7168]{1,0:T(8,128)(2,1)S(1)}, u32[]{:S(2)}, u32[]{:S(2)}) collective-permute-start(bf16[8,7168]{1,0:T(8,128)(2,1)S(1)} %get-tuple-element.34), channel_id=1, source_target_pairs={{0,1},{1,0},{2,3},{3,2},{4,5},{5,4},{6,7},{7,6},{8,9},{9,8},{10,11... | collective-permute-start | bytes 344072 | tf_op jit(solution)/shard_map/ppermute | solution.py:23
  21.9 2.5 %collective-permute-start.8 = (bf16[8,7168]{1,0:T(8,128)(2,1)S(1)}, bf16[8,7168]{1,0:T(8,128)(2,1)S(1)}, u32[]{:S(2)}, u32[]{:S(2)}) collective-permute-start(bf16[8,7168]{1,0:T(8,128)(2,1)S(1)} %get-tuple-element.39), channel_id=1, source_target_pairs={{0,1},{1,0},{2,3},{3,2},{4,5},{5,4},{6,7},{7,6},{8,9},{9,8},{10,11... | collective-permute-start | bytes 344072 | tf_op jit(solution)/shard_map/ppermute | solution.py:23
  22.0 3.9 %collective-permute-start.10 = (bf16[8,7168]{1,0:T(8,128)(2,1)S(1)}, bf16[8,7168]{1,0:T(8,128)(2,1)S(1)}, u32[]{:S(2)}, u32[]{:S(2)}) collective-permute-start(bf16[8,7168]{1,0:T(8,128)(2,1)S(1)} %get-tuple-element.41), channel_id=1, source_target_pairs={{0,1},{1,0},{2,3},{3,2},{4,5},{5,4},{6,7},{7,6},{8,9},{9,8},{10,11... | collective-permute-start | bytes 344072 | tf_op jit(solution)/shard_map/ppermute | solution.py:23
  22.8 7.3 %collective-permute-start.7 = (bf16[8,7168]{1,0:T(8,128)(2,1)S(1)}, bf16[8,7168]{1,0:T(8,128)(2,1)S(1)}, u32[]{:S(2)}, u32[]{:S(2)}) collective-permute-start(bf16[8,7168]{1,0:T(8,128)(2,1)S(1)} %add_convert_fusion.2), channel_id=1, source_target_pairs={{0,6},{1,7},{2,4},{3,5},{4,2},{5,3},{6,0},{7,1},{8,14},{9,15},{10,... | collective-permute-start | bytes 344072 | tf_op jit(solution)/shard_map/ppermute | solution.py:23
  24.4 7.0 %collective-permute-start.9 = (bf16[8,7168]{1,0:T(8,128)(2,1)S(1)}, bf16[8,7168]{1,0:T(8,128)(2,1)S(1)}, u32[]{:S(2)}, u32[]{:S(2)}) collective-permute-start(bf16[8,7168]{1,0:T(8,128)(2,1)S(1)} %add_convert_fusion.1), channel_id=1, source_target_pairs={{0,4},{1,5},{2,6},{3,7},{4,0},{5,1},{6,2},{7,3},{8,12},{9,13},{10,... | collective-permute-start | bytes 344072 | tf_op jit(solution)/shard_map/ppermute | solution.py:23
  25.9 5.5 %collective-permute-start.11 = (bf16[8,7168]{1,0:T(8,128)(2,1)S(1)}, bf16[8,7168]{1,0:T(8,128)(2,1)S(1)}, u32[]{:S(2)}, u32[]{:S(2)}) collective-permute-start(bf16[8,7168]{1,0:T(8,128)(2,1)S(1)} %add_convert_fusion), channel_id=1, source_target_pairs={{0,2},{1,3},{2,0},{3,1},{4,6},{5,7},{6,4},{7,5},{8,10},{9,11},{10,... | collective-permute-start | bytes 344072 | tf_op jit(solution)/shard_map/ppermute | solution.py:23
  31.5 5.2 %collective-permute-start.14 = (bf16[8,3584]{1,0:T(8,128)(2,1)S(1)}, bf16[8,3584]{1,0:T(8,128)(2,1)S(1)}, u32[]{:S(2)}, u32[]{:S(2)}) collective-permute-start(bf16[8,3584]{1,0:T(8,128)(2,1)S(1)} %fusion.refs_0_), channel_id=1, source_target_pairs={{0,6},{1,7},{2,4},{3,5},{4,2},{5,3},{6,0},{7,1},{8,14},{9,15},{10,... | collective-permute-start | bytes 172040 | tf_op jit(solution)/shard_map/ppermute | solution.py:23
  33.1 4.4 %collective-permute-start.13 = (bf16[8,3584]{1,0:T(8,128)(2,1)S(1)}, bf16[8,3584]{1,0:T(8,128)(2,1)S(1)}, u32[]{:S(2)}, u32[]{:S(2)}) collective-permute-start(bf16[8,3584]{1,0:T(8,128)(2,1)S(1)} %fusion.refs_0_), channel_id=1, source_target_pairs={{0,4},{1,5},{2,6},{3,7},{4,0},{5,1},{6,2},{7,3},{8,12},{9,13},{10,... | collective-permute-start | bytes 172040 | tf_op jit(solution)/shard_map/ppermute | solution.py:23
  34.5 4.2 %collective-permute-start.12 = (bf16[8,3584]{1,0:T(8,128)(2,1)S(1)}, bf16[8,3584]{1,0:T(8,128)(2,1)S(1)}, u32[]{:S(2)}, u32[]{:S(2)}) collective-permute-start(bf16[8,3584]{1,0:T(8,128)(2,1)S(1)} %fusion.refs_0_), channel_id=1, source_target_pairs={{0,2},{1,3},{2,0},{3,1},{4,6},{5,7},{6,4},{7,5},{8,10},{9,11},{10,... | collective-permute-start | bytes 172040 | tf_op jit(solution)/shard_map/ppermute | solution.py:23
  35.1 3.6 %collective-permute-start.15 = (bf16[8,3584]{1,0:T(8,128)(2,1)S(1)}, bf16[8,3584]{1,0:T(8,128)(2,1)S(1)}, u32[]{:S(2)}, u32[]{:S(2)}) collective-permute-start(bf16[8,3584]{1,0:T(8,128)(2,1)S(1)} %fusion.refs_0_), channel_id=1, source_target_pairs={{0,1},{1,0},{2,3},{3,2},{4,5},{5,4},{6,7},{7,6},{8,9},{9,8},{10,11... | collective-permute-start | bytes 172040 | tf_op jit(solution)/shard_map/ppermute | solution.py:23
  36.7 2.0 %collective-permute-start.18 = (bf16[8,3584]{1,0:T(8,128)(2,1)S(1)}, bf16[8,3584]{1,0:T(8,128)(2,1)S(1)}, u32[]{:S(2)}, u32[]{:S(2)}) collective-permute-start(bf16[8,3584]{1,0:T(8,128)(2,1)S(1)} %collective-permute-done.14.refs_3_), channel_id=1, source_target_pairs={{0,1},{1,0},{2,3},{3,2},{4,5},{5,4},{6,7},{7,6},{8,9},{9,8},{10,11... | collective-permute-start | bytes 172040 | tf_op jit(solution)/shard_map/ppermute | solution.py:23
  37.4 1.3 %collective-permute-start.17 = (bf16[8,3584]{1,0:T(8,128)(2,1)S(1)}, bf16[8,3584]{1,0:T(8,128)(2,1)S(1)}, u32[]{:S(2)}, u32[]{:S(2)}) collective-permute-start(bf16[8,3584]{1,0:T(8,128)(2,1)S(1)} %collective-permute-done.13.refs_2_), channel_id=1, source_target_pairs={{0,1},{1,0},{2,3},{3,2},{4,5},{5,4},{6,7},{7,6},{8,9},{9,8},{10,11... | collective-permute-start | bytes 172040 | tf_op jit(solution)/shard_map/ppermute | solution.py:23
  38.7 1.2 %collective-permute-start.16 = (bf16[8,3584]{1,0:T(8,128)(2,1)S(1)}, bf16[8,3584]{1,0:T(8,128)(2,1)S(1)}, u32[]{:S(2)}, u32[]{:S(2)}) collective-permute-start(bf16[8,3584]{1,0:T(8,128)(2,1)S(1)} %collective-permute-done.12.refs_1_), channel_id=1, source_target_pairs={{0,1},{1,0},{2,3},{3,2},{4,5},{5,4},{6,7},{7,6},{8,9},{9,8},{10,11... | collective-permute-start | bytes 172040 | tf_op jit(solution)/shard_map/ppermute | solution.py:23

commit v6 on v5

--- a/solution.py
+++ b/solution.py
@@ -233,26 +233,28 @@
         out_specs=out_specs,
         input_output_aliases={1 + len(parts): len(parts)} if passed else {},
         scratch_shapes=[pltpu.SemaphoreType.DMA((stop - first,)) for _, first, stop in parts],
-        compiler_params=pltpu.CompilerParams(vmem_limit_bytes=12 * 2**20),
+        compiler_params=pltpu.CompilerParams(vmem_limit_bytes=14 * 2**20),
         cost_estimate=pl.CostEstimate(flops=0, bytes_accessed=2 * size, transcendentals=0),
         name=name,
     )(rows, *(in_hbm(w) for w, _, _ in parts), held)
 
 
-def gate_up_kernel(arrived_ref, gate_near, gate_far, up_near, up_far, live_ref, *rest):
+def gate_up_kernel(levels, *refs):
+    arrived, (gate_near, gate_far, up_ref, live_ref, *rest) = refs[:levels], refs[levels:]
     *out_refs, x_ref = rest
     keep_refs, sent_refs = out_refs[:CHIPS], out_refs[CHIPS:]
-    groups, _, _, rows, _ = arrived_ref.shape
+    arrived = [ref.at[g] for ref in arrived for g in range(ref.shape[0])]
+    groups, rows = len(arrived), arrived[0].shape[2]
     few = keep_refs[0].shape[0]
     unit = gate_near.shape[2]
     gates = [near_or_far.at[c] for near_or_far in (gate_near, gate_far) for c in range(near_or_far.shape[0])]
-    ups = [near_or_far.at[c] for near_or_far in (up_near, up_far) for c in range(near_or_far.shape[0])]
+    ups = [up_ref.at[c] for c in range(up_ref.shape[0])]
     count = len(gates)
     for core in range(CORES):
         for chip in range(CHIPS):
             for group in range(groups):
                 at = ((core * CHIPS + chip) * groups + group) * rows
-                x_ref[at : at + rows, :] = arrived_ref[group, chip, core].astype(jnp.float32)
+                x_ref[at : at + rows, :] = arrived[group][chip, core].astype(jnp.float32)
     x = x_ref[...].astype(jnp.bfloat16)
     for c in range(count):
         for k, w in enumerate((gates[c], ups[c])):
@@ -268,19 +270,19 @@
 
 
 def gate_up(arrived, gate, up, live):
-    rows = math.prod(arrived.shape[:4])
+    rows = sum(math.prod(level.shape[:4]) for level in arrived)
     _, depth, unit = gate[0].shape
     wide = 2 * unit * sum(part.shape[0] for part in gate)
     return pl.pallas_call(
-        gate_up_kernel,
+        functools.partial(gate_up_kernel, len(arrived)),
         out_shape=[pltpu.VMEM((rows // MDL, wide), jnp.float32)] * CHIPS
         + [pltpu.VMEM((rows // MDL, wide), jnp.bfloat16)] * CHIPS,
-        in_specs=[VMEM] * 6,
+        in_specs=[VMEM] * (len(arrived) + 4),
         out_specs=[VMEM] * (2 * CHIPS),
         scratch_shapes=[pltpu.VMEM((rows, depth), jnp.float32)],
         compiler_params=pltpu.CompilerParams(vmem_limit_bytes=24 * 2**20),
         name="gate_up",
-    )(arrived, *gate, *up, live)
+    )(*arrived, *gate, up, live)
 
 
 def down_kernel(*refs):
@@ -354,7 +356,6 @@
     masks = [chip * CORES for chip in range(CHIPS)]
     far_first = range(CHIPS - 1, 0, -1)
     gate_early = max(1, count * 4 // 7)
-    up_early = max(1, count * 2 // 7)
 
     mixed_rows, kept, sent, listed, live, gate_near = attend(
         queries,
@@ -370,14 +371,15 @@
     )
     pair = jnp.stack([kept, from_partner(sent, 1)], axis=1)
     came = {chip: from_partner(pair[chip], masks[chip]) for chip in far_first}
-    middle = [(gate_w, gate_early, count), (up_w, 0, up_early)]
-    gate_far, up_near, own = fetch(listed, middle, pair[0], "fetch_middle", True)
-    arrived = jnp.stack([own] + [came[chip] for chip in range(1, CHIPS)])[None]
-    (up_far,) = fetch(listed, [(up_w, up_early, count)], arrived, "fetch_up", False)
+    arrived = jnp.stack([pair[0]] + [came[chip] for chip in range(1, CHIPS)])[None]
+    later = [(gate_w, gate_early, count), (up_w, 0, count)]
+    gate_far, up = fetch(listed, later, arrived, "fetch_later", False)
+    levels = [arrived]
     for level in range(group_total.bit_length() - 1):
-        arrived = jnp.concatenate([arrived, from_partner(arrived, MDL << level)], axis=0)
-
-    parts = gate_up(arrived, (gate_near, gate_far), (up_near, up_far), live)
+        held = levels[0] if level == 0 else jnp.concatenate(levels, axis=0)
+        levels.append(from_partner(held, MDL << level))
+
+    parts = gate_up(levels, (gate_near, gate_far), up, live)
     part = {}
     for chip in (*far_first, 0):
         part[chip] = parts[chip] + from_partner(parts[CHIPS + chip], 1).astype(jnp.float32)

time: 54.4 us -> 54.1 us (level)
  waiting for transfers between devices: 8.84 us -> 11.2 us
  blocking collectives: 12.2 us -> 10.8 us
  Pallas kernels: 16.6 us -> 15.6 us
    ppermute x19, waiting for transfers between devices: 8.84 us -> 11.2 us  [from_partner(): return lax.ppermute(value, 'hid', pairs)]
    all_to_all x1, blocking collectives: 12.2 us -> 10.8 us  [on_device(): lax.all_to_all(ffn_part, 'hid', split_axis=0, concat_axis=0, tiled=True)]
    pallas_call x3 -> x2, Pallas kernels: 8.96 us -> 7.9 us  [fetch(): pl.pallas_call(functools.partial(fetch_kernel, [first for _, first, _ in...]
  transfers between devices with their start and end apart: 19 -> 19, of which waited for: 10 -> 10; matrix products, arithmetic and copies ran while one was open for 0% -> 0% of each run, Pallas kernels for 17% -> 15%
where the time goes in v6:
time: 54.1 us; the launch traced here: 53.9 us
  starting transfers between devices  16 us (30%)
  Pallas kernels  15.6 us (29%)
  waiting for transfers between devices  11.2 us (21%)
  blocking collectives  10.8 us (20%)
    ppermute x19, starting transfers between devices, from_partner(): return lax.ppermute(value, 'hid', pairs)  16 us
    ppermute x19, waiting for transfers between devices, from_partner(): return lax.ppermute(value, 'hid', pairs)  11.2 us
    all_to_all x1, blocking collectives, on_device(): lax.all_to_all(ffn_part, 'hid', split_axis=0, concat_axis=0, tiled=True)  10.8 us
    pallas_call x2, Pallas kernels, fetch(): pl.pallas_call(functools.partial(fetch_kernel, [first for _, first, _ in...  7.9 us
    pallas_call x1, Pallas kernels, attend(): pl.pallas_call(functools.partial(attend_kernel, width // size), out_shape...  3.52 us
    pallas_call x1, Pallas kernels, gate_up(): pl.pallas_call(functools.partial(gate_up_kernel, len(arrived)), out_shape...  2.09 us
    pallas_call x1, Pallas kernels, down(): pl.pallas_call(down_kernel, out_shape=pltpu.VMEM((devices, rows, weights....  1.39 us
  transfers between devices with their start and end apart: 19, of which 10 were waited for; matrix products, arithmetic and copies ran while one was open for 0% of the time, Pallas kernels for 15%

profile of v6, /device:TPU:0, one launch (start us, length us, event | category | flops | bytes accessed | tf_op | source)
XLA Modules:
  0.0 53.9 jit_solution(6249433794113627302)
XLA Ops:
  0.0 3.5 %attend.1 = (f32[4,8192]{1,0:T(4,128)S(1)}, bf16[4,4,1024]{2,1,0:T(4,128)(2,1)S(1)}, bf16[4,4,1024]{2,1,0:T(4,128)(2,1)S(1)}, s32[2,28]{1,0:T(2,128)S(1)}, f32[1...) custom-call(s32[4]{0:T(128)} %len_hbm.1, bf16[4,64,128]{2,1,0:T(8,128)(2,1)} %q_hbm.1, bf16[4,192,1024]{2,1,0:T(8,128)(2,1)} %k_hbm.1, ...), custom_call_target="tpu_custom_call" | custom-call | tf_op jit(solution)/shard_map/attend/pallas_call | solution.py:163
  3.5 0.5 collective-permute-start
  4.0 0.9 %collective-permute-done = bf16[4,4,1024]{2,1,0:T(4,128)(2,1)S(1)} collective-permute-done((bf16[4,4,1024]{2,1,0:T(4,128)(2,1)S(1)}, bf16[4,4,1024]{2,1,0:T(4,128)(2,1)S(1)}, u32[]{:S(2)}, u32[]{:S(2)}) %collective-permute-start) | collective-permute-done | bytes 32800 | tf_op jit(solution)/shard_map/ppermute | solution.py:23
  5.0 2.9 %collective-permute-start.1 = (bf16[2,4,1024]{2,1,0:T(4,128)(2,1)S(1)}, bf16[2,4,1024]{2,1,0:T(4,128)(2,1)S(1)}, u32[]{:S(2)}, u32[]{:S(2)}) collective-permute-start(bf16[2,4,1024]{2,1,0:T(4,128)(2,1)S(1)} %get-tuple-element.42), channel_id=1, source_target_pairs={{0,2},{1,3},{2,0},{3,1},{4,6},{5,7},{6,4},{7,5},{8,10},{9,11},{10,... | collective-permute-start | bytes 49160 | tf_op jit(solution)/shard_map/ppermute | solution.py:23
  7.9 1.5 %collective-permute-start.3 = (bf16[2,4,1024]{2,1,0:T(4,128)(2,1)S(1)}, bf16[2,4,1024]{2,1,0:T(4,128)(2,1)S(1)}, u32[]{:S(2)}, u32[]{:S(2)}) collective-permute-start(bf16[2,4,1024]{2,1,0:T(4,128)(2,1)S(1)} %get-tuple-element.43), channel_id=1, source_target_pairs={{0,6},{1,7},{2,4},{3,5},{4,2},{5,3},{6,0},{7,1},{8,14},{9,15},{10,... | collective-permute-start | bytes 49160 | tf_op jit(solution)/shard_map/ppermute | solution.py:23
  9.4 0.1 collective-permute-start.2
  9.5 0.1 collective-permute-done.1
  9.6 2.9 %collective-permute-done.3 = bf16[2,4,1024]{2,1,0:T(4,128)(2,1)S(1)} collective-permute-done((bf16[2,4,1024]{2,1,0:T(4,128)(2,1)S(1)}, bf16[2,4,1024]{2,1,0:T(4,128)(2,1)S(1)}, u32[]{:S(2)}, u32[]{:S(2)}) %collective-permute-start.3) | collective-permute-done | bytes 16416 | tf_op jit(solution)/shard_map/ppermute | solution.py:23
  12.5 0.6 %collective-permute-done.2 = bf16[2,4,1024]{2,1,0:T(4,128)(2,1)S(1)} collective-permute-done((bf16[2,4,1024]{2,1,0:T(4,128)(2,1)S(1)}, bf16[2,4,1024]{2,1,0:T(4,128)(2,1)S(1)}, u32[]{:S(2)}, u32[]{:S(2)}) %collective-permute-start.2) | collective-permute-done | bytes 16416 | tf_op jit(solution)/shard_map/ppermute | solution.py:23
  13.2 2.7 %collective-permute-start.4 = (bf16[1,4,2,4,1024]{4,3,2,1,0:T(4,128)(2,1)S(1)}, bf16[1,4,2,4,1024]{4,3,2,1,0:T(4,128)(2,1)S(1)}, u32[]{:S(2)}, u32[]{:S(2)}) collective-permute-start(bf16[1,4,2,4,1024]{4,3,2,1,0:T(4,128)(2,1)S(1)} %maximum_bitcast_fusion.rest_2_.refs_0_), channel_id=1, source_target_pairs={{0,8},{1,9},{2,10},{3,11},{4,12},{5,13},{6,14},{7,15},{8,0},{9,1},... | collective-permute-start | bytes 196616 | tf_op jit(solution)/shard_map/ppermute | solution.py:23
  15.9 4.5 %fetch_later.1 = (bf16[12,1024,128]{2,1,0:T(8,128)(2,1)S(1)}, bf16[28,1024,128]{2,1,0:T(8,128)(2,1)S(1)}) custom-call(s32[2,28]{1,0:T(2,128)S(1)} %get-tuple-element.24.rows_ref, bf16[1,56,1024,128]{3,2,1,0:T(8,128)(2,1)} %rest_0_.2, bf16[1,56,1024,128]{3,2,1,0:T(8,128)(2,1)} %rest_1_.1, bf16[1,4,2,4,1024]{4,3,2,1,0:T(4,128)(2,1)S(1)} %maximum_bitcast_fusion.rest_2_.refs_0_), custom_call_target="tpu_custom_call" | custom-call | bytes 20971520 | tf_op jit(solution)/shard_map/fetch_later/pallas_call | solution.py:229
  20.3 2.1 %gate_up.1 = (f32[8,7168]{1,0:T(8,128)S(1)}, f32[8,7168]{1,0:T(8,128)S(1)}, f32[8,7168]{1,0:T(8,128)S(1)}, f32[8,7168]{1,0:T(8,128)S(1)}, bf16[8,7168]{1,0:T(8,1...) custom-call(bf16[1,4,2,4,1024]{4,3,2,1,0:T(4,128)(2,1)S(1)} %maximum_bitcast_fus, ...), custom_call_target="tpu_custom_call" | custom-call | tf_op jit(solution)/shard_map/gate_up/pallas_call | solution.py:276
  22.4 0.1 collective-permute-start.6
  22.5 0.5 collective-permute-start.5
  23.0 0.1 collective-permute-start.8
  23.1 0.4 collective-permute-start.10
  23.5 0.3 collective-permute-done.6
  23.8 1.5 %collective-permute-start.7 = (bf16[8,7168]{1,0:T(8,128)(2,1)S(1)}, bf16[8,7168]{1,0:T(8,128)(2,1)S(1)}, u32[]{:S(2)}, u32[]{:S(2)}) collective-permute-start(bf16[8,7168]{1,0:T(8,128)(2,1)S(1)} %add_convert_fusion.2), channel_id=1, source_target_pairs={{0,6},{1,7},{2,4},{3,5},{4,2},{5,3},{6,0},{7,1},{8,14},{9,15},{10,... | collective-permute-start | bytes 344072 | tf_op jit(solution)/shard_map/ppermute | solution.py:23
  25.4 1.7 %collective-permute-start.9 = (bf16[8,7168]{1,0:T(8,128)(2,1)S(1)}, bf16[8,7168]{1,0:T(8,128)(2,1)S(1)}, u32[]{:S(2)}, u32[]{:S(2)}) collective-permute-start(bf16[8,7168]{1,0:T(8,128)(2,1)S(1)} %add_convert_fusion.1), channel_id=1, source_target_pairs={{0,4},{1,5},{2,6},{3,7},{4,0},{5,1},{6,2},{7,3},{8,12},{9,13},{10,... | collective-permute-start | bytes 344072 | tf_op jit(solution)/shard_map/ppermute | solution.py:23
  27.1 0.5 collective-permute-start.11
  27.6 3.4 %fetch_down.1 = (bf16[28,128,1024]{2,1,0:T(8,128)(2,1)S(1)}, f32[8,7168]{1,0:T(8,128)S(1)}) custom-call(s32[2,28]{1,0:T(2,128)S(1)} %get-tuple-element.24.rows_ref, bf16[1,56,128,1024]{3,2,1,0:T(8,128)(2,1)} %rest_0_.3, f32[8,7168]{1,0:T(8,128)S(1)} %convert_add_fusion.1.rest_1_), custom_call_target="tpu_custom_call", output_to_operand_aliasing={{1}: (2, {})} | custom-call | bytes 14680064 | tf_op jit(solution)/shard_map/fetch_down/pallas_call | solution.py:229
  31.1 1.5 %collective-permute-done.9 = bf16[8,7168]{1,0:T(8,128)(2,1)S(1)} collective-permute-done((bf16[8,7168]{1,0:T(8,128)(2,1)S(1)}, bf16[8,7168]{1,0:T(8,128)(2,1)S(1)}, u32[]{:S(2)}, u32[]{:S(2)}) %collective-permute-start.9) | collective-permute-done | bytes 114720 | tf_op jit(solution)/shard_map/ppermute | solution.py:23
  32.7 1.3 %collective-permute-start.14 = (bf16[8,3584]{1,0:T(8,128)(2,1)S(1)}, bf16[8,3584]{1,0:T(8,128)(2,1)S(1)}, u32[]{:S(2)}, u32[]{:S(2)}) collective-permute-start(bf16[8,3584]{1,0:T(8,128)(2,1)S(1)} %fusion.refs_0_), channel_id=1, source_target_pairs={{0,6},{1,7},{2,4},{3,5},{4,2},{5,3},{6,0},{7,1},{8,14},{9,15},{10,... | collective-permute-start | bytes 172040 | tf_op jit(solution)/shard_map/ppermute | solution.py:23
  34.0 1.6 %collective-permute-start.13 = (bf16[8,3584]{1,0:T(8,128)(2,1)S(1)}, bf16[8,3584]{1,0:T(8,128)(2,1)S(1)}, u32[]{:S(2)}, u32[]{:S(2)}) collective-permute-start(bf16[8,3584]{1,0:T(8,128)(2,1)S(1)} %fusion.refs_0_), channel_id=1, source_target_pairs={{0,4},{1,5},{2,6},{3,7},{4,0},{5,1},{6,2},{7,3},{8,12},{9,13},{10,... | collective-permute-start | bytes 172040 | tf_op jit(solution)/shard_map/ppermute | solution.py:23
  35.7 0.6 %collective-permute-start.12 = (bf16[8,3584]{1,0:T(8,128)(2,1)S(1)}, bf16[8,3584]{1,0:T(8,128)(2,1)S(1)}, u32[]{:S(2)}, u32[]{:S(2)}) collective-permute-start(bf16[8,3584]{1,0:T(8,128)(2,1)S(1)} %fusion.refs_0_), channel_id=1, source_target_pairs={{0,2},{1,3},{2,0},{3,1},{4,6},{5,7},{6,4},{7,5},{8,10},{9,11},{10,... | collective-permute-start | bytes 172040 | tf_op jit(solution)/shard_map/ppermute | solution.py:23
  36.2 1.6 %collective-permute-done.14.refs_3_ = bf16[8,3584]{1,0:T(8,128)(2,1)S(1)} collective-permute-done((bf16[8,3584]{1,0:T(8,128)(2,1)S(1)}, bf16[8,3584]{1,0:T(8,128)(2,1)S(1)}, u32[]{:S(2)}, u32[]{:S(2)}) %collective-permute-start.14) | collective-permute-done | bytes 57376 | tf_op jit(solution)/shard_map/ppermute | solution.py:23
  37.8 0.8 %collective-permute-done.13.refs_2_ = bf16[8,3584]{1,0:T(8,128)(2,1)S(1)} collective-permute-done((bf16[8,3584]{1,0:T(8,128)(2,1)S(1)}, bf16[8,3584]{1,0:T(8,128)(2,1)S(1)}, u32[]{:S(2)}, u32[]{:S(2)}) %collective-permute-start.13) | collective-permute-done | bytes 57376 | tf_op jit(solution)/shard_map/ppermute | solution.py:23
  38.6 1.2 %collective-permute-done.12.refs_1_ = bf16[8,3584]{1,0:T(8,128)(2,1)S(1)} collective-permute-done((bf16[8,3584]{1,0:T(8,128)(2,1)S(1)}, bf16[8,3584]{1,0:T(8,128)(2,1)S(1)}, u32[]{:S(2)}, u32[]{:S(2)}) %collective-permute-start.12) | collective-permute-done | bytes 57376 | tf_op jit(solution)/shard_map/ppermute | solution.py:23
  39.9 1.2 %collective-permute-done.16.refs_5_ = bf16[8,3584]{1,0:T(8,128)(2,1)S(1)} collective-permute-done((bf16[8,3584]{1,0:T(8,128)(2,1)S(1)}, bf16[8,3584]{1,0:T(8,128)(2,1)S(1)}, u32[]{:S(2)}, u32[]{:S(2)}) %collective-permute-start.16) | collective-permute-done | bytes 57376 | tf_op jit(solution)/shard_map/ppermute | solution.py:23
  41.1 1.4 %down.1 = bf16[16,4,1024]{2,1,0:T(4,128)(2,1)S(1)} custom-call(bf16[8,3584]{1,0:T(8,128)(2,1)S(1)} %fusion.refs_0_, bf16[8,3584]{1,0:T(8,128)(2,1)S(1)} %collective-permute-done.12.refs_1_, bf16[8,3584]{1,0:T(8,128)(2,1)S(1)} %collective-permute-done.13.refs_2_, bf16[8,3584]{1,0:T(8,128)(2,1)S(1)} %collective-permute-done.14.refs_3_, ...), custom_call_target="tpu_custom_call" | custom-call | tf_op jit(solution)/shard_map/down/pallas_call | solution.py:308
  42.5 10.8 %all_to_all.5.back_ref = bf16[16,4,1024]{2,1,0:T(4,128)(2,1)S(1)} all-to-all(bf16[16,4,1024]{2,1,0:T(4,128)(2,1)S(1)} %down.1), channel_id=1, replica_groups=mesh['groups'=2,'hid'=16] {'hid'}, dimensions={0} | all-to-all | bytes 262144 | tf_op jit(solution)/shard_map/all_to_all | solution.py:398
  53.3 0.7 %finish.1 = bf16[4,8192]{1,0:T(4,128)(2,1)} custom-call(f32[4,8192]{1,0:T(4,128)S(1)} %get-tuple-element.23.mixed_ref, bf16[16,4,1024]{2,1,0:T(4,128)(2,1)S(1)} %all_to_all.5.back_ref), custom_call_target="tpu_custom_call" | custom-call | tf_op jit(solution)/shard_map/finish/pallas_call | solution.py:328
  (21 shorter events, 0.3 us)
Async XLA Ops:
  3.5 1.4 %collective-permute-start = (bf16[4,4,1024]{2,1,0:T(4,128)(2,1)S(1)}, bf16[4,4,1024]{2,1,0:T(4,128)(2,1)S(1)}, u32[]{:S(2)}, u32[]{:S(2)}) collective-permute-start(bf16[4,4,1024]{2,1,0:T(4,128)(2,1)S(1)} %get-tuple-element.26), channel_id=1, source_target_pairs={{0,1},{1,0},{2,3},{3,2},{4,5},{5,4},{6,7},{7,6},{8,9},{9,8},{10,11... | collective-permute-start | bytes 98312 | tf_op jit(solution)/shard_map/ppermute | solution.py:23
  5.0 4.6 %collective-permute-start.1 = (bf16[2,4,1024]{2,1,0:T(4,128)(2,1)S(1)}, bf16[2,4,1024]{2,1,0:T(4,128)(2,1)S(1)}, u32[]{:S(2)}, u32[]{:S(2)}) collective-permute-start(bf16[2,4,1024]{2,1,0:T(4,128)(2,1)S(1)} %get-tuple-element.42), channel_id=1, source_target_pairs={{0,2},{1,3},{2,0},{3,1},{4,6},{5,7},{6,4},{7,5},{8,10},{9,11},{10,... | collective-permute-start | bytes 49160 | tf_op jit(solution)/shard_map/ppermute | solution.py:23
  7.9 4.6 %collective-permute-start.3 = (bf16[2,4,1024]{2,1,0:T(4,128)(2,1)S(1)}, bf16[2,4,1024]{2,1,0:T(4,128)(2,1)S(1)}, u32[]{:S(2)}, u32[]{:S(2)}) collective-permute-start(bf16[2,4,1024]{2,1,0:T(4,128)(2,1)S(1)} %get-tuple-element.43), channel_id=1, source_target_pairs={{0,6},{1,7},{2,4},{3,5},{4,2},{5,3},{6,0},{7,1},{8,14},{9,15},{10,... | collective-permute-start | bytes 49160 | tf_op jit(solution)/shard_map/ppermute | solution.py:23
  9.4 3.7 %collective-permute-start.2 = (bf16[2,4,1024]{2,1,0:T(4,128)(2,1)S(1)}, bf16[2,4,1024]{2,1,0:T(4,128)(2,1)S(1)}, u32[]{:S(2)}, u32[]{:S(2)}) collective-permute-start(bf16[2,4,1024]{2,1,0:T(4,128)(2,1)S(1)} %get-tuple-element.44), channel_id=1, source_target_pairs={{0,4},{1,5},{2,6},{3,7},{4,0},{5,1},{6,2},{7,3},{8,12},{9,13},{10,... | collective-permute-start | bytes 49160 | tf_op jit(solution)/shard_map/ppermute | solution.py:23
  13.2 7.1 %collective-permute-start.4 = (bf16[1,4,2,4,1024]{4,3,2,1,0:T(4,128)(2,1)S(1)}, bf16[1,4,2,4,1024]{4,3,2,1,0:T(4,128)(2,1)S(1)}, u32[]{:S(2)}, u32[]{:S(2)}) collective-permute-start(bf16[1,4,2,4,1024]{4,3,2,1,0:T(4,128)(2,1)S(1)} %maximum_bitcast_fusion.rest_2_.refs_0_), channel_id=1, source_target_pairs={{0,8},{1,9},{2,10},{3,11},{4,12},{5,13},{6,14},{7,15},{8,0},{9,1},... | collective-permute-start | bytes 196616 | tf_op jit(solution)/shard_map/ppermute | solution.py:23
  22.4 1.4 %collective-permute-start.6 = (bf16[8,7168]{1,0:T(8,128)(2,1)S(1)}, bf16[8,7168]{1,0:T(8,128)(2,1)S(1)}, u32[]{:S(2)}, u32[]{:S(2)}) collective-permute-start(bf16[8,7168]{1,0:T(8,128)(2,1)S(1)} %get-tuple-element.35), channel_id=1, source_target_pairs={{0,1},{1,0},{2,3},{3,2},{4,5},{5,4},{6,7},{7,6},{8,9},{9,8},{10,11... | collective-permute-start | bytes 344072 | tf_op jit(solution)/shard_map/ppermute | solution.py:23
  22.5 5.1 %collective-permute-start.5 = (bf16[8,7168]{1,0:T(8,128)(2,1)S(1)}, bf16[8,7168]{1,0:T(8,128)(2,1)S(1)}, u32[]{:S(2)}, u32[]{:S(2)}) collective-permute-start(bf16[8,7168]{1,0:T(8,128)(2,1)S(1)} %get-tuple-element.32), channel_id=1, source_target_pairs={{0,1},{1,0},{2,3},{3,2},{4,5},{5,4},{6,7},{7,6},{8,9},{9,8},{10,11... | collective-permute-start | bytes 344072 | tf_op jit(solution)/shard_map/ppermute | solution.py:23
  23.0 2.3 %collective-permute-start.8 = (bf16[8,7168]{1,0:T(8,128)(2,1)S(1)}, bf16[8,7168]{1,0:T(8,128)(2,1)S(1)}, u32[]{:S(2)}, u32[]{:S(2)}) collective-permute-start(bf16[8,7168]{1,0:T(8,128)(2,1)S(1)} %get-tuple-element.37), channel_id=1, source_target_pairs={{0,1},{1,0},{2,3},{3,2},{4,5},{5,4},{6,7},{7,6},{8,9},{9,8},{10,11... | collective-permute-start | bytes 344072 | tf_op jit(solution)/shard_map/ppermute | solution.py:23
  23.1 4.0 %collective-permute-start.10 = (bf16[8,7168]{1,0:T(8,128)(2,1)S(1)}, bf16[8,7168]{1,0:T(8,128)(2,1)S(1)}, u32[]{:S(2)}, u32[]{:S(2)}) collective-permute-start(bf16[8,7168]{1,0:T(8,128)(2,1)S(1)} %get-tuple-element.39), channel_id=1, source_target_pairs={{0,1},{1,0},{2,3},{3,2},{4,5},{5,4},{6,7},{7,6},{8,9},{9,8},{10,11... | collective-permute-start | bytes 344072 | tf_op jit(solution)/shard_map/ppermute | solution.py:23
  23.8 7.3 %collective-permute-start.7 = (bf16[8,7168]{1,0:T(8,128)(2,1)S(1)}, bf16[8,7168]{1,0:T(8,128)(2,1)S(1)}, u32[]{:S(2)}, u32[]{:S(2)}) collective-permute-start(bf16[8,7168]{1,0:T(8,128)(2,1)S(1)} %add_convert_fusion.2), channel_id=1, source_target_pairs={{0,6},{1,7},{2,4},{3,5},{4,2},{5,3},{6,0},{7,1},{8,14},{9,15},{10,... | collective-permute-start | bytes 344072 | tf_op jit(solution)/shard_map/ppermute | solution.py:23
  25.4 7.2 %collective-permute-start.9 = (bf16[8,7168]{1,0:T(8,128)(2,1)S(1)}, bf16[8,7168]{1,0:T(8,128)(2,1)S(1)}, u32[]{:S(2)}, u32[]{:S(2)}) collective-permute-start(bf16[8,7168]{1,0:T(8,128)(2,1)S(1)} %add_convert_fusion.1), channel_id=1, source_target_pairs={{0,4},{1,5},{2,6},{3,7},{4,0},{5,1},{6,2},{7,3},{8,12},{9,13},{10,... | collective-permute-start | bytes 344072 | tf_op jit(solution)/shard_map/ppermute | solution.py:23
  27.1 5.5 %collective-permute-start.11 = (bf16[8,7168]{1,0:T(8,128)(2,1)S(1)}, bf16[8,7168]{1,0:T(8,128)(2,1)S(1)}, u32[]{:S(2)}, u32[]{:S(2)}) collective-permute-start(bf16[8,7168]{1,0:T(8,128)(2,1)S(1)} %add_convert_fusion), channel_id=1, source_target_pairs={{0,2},{1,3},{2,0},{3,1},{4,6},{5,7},{6,4},{7,5},{8,10},{9,11},{10,... | collective-permute-start | bytes 344072 | tf_op jit(solution)/shard_map/ppermute | solution.py:23
  32.7 5.2 %collective-permute-start.14 = (bf16[8,3584]{1,0:T(8,128)(2,1)S(1)}, bf16[8,3584]{1,0:T(8,128)(2,1)S(1)}, u32[]{:S(2)}, u32[]{:S(2)}) collective-permute-start(bf16[8,3584]{1,0:T(8,128)(2,1)S(1)} %fusion.refs_0_), channel_id=1, source_target_pairs={{0,6},{1,7},{2,4},{3,5},{4,2},{5,3},{6,0},{7,1},{8,14},{9,15},{10,... | collective-permute-start | bytes 172040 | tf_op jit(solution)/shard_map/ppermute | solution.py:23
  34.0 4.6 %collective-permute-start.13 = (bf16[8,3584]{1,0:T(8,128)(2,1)S(1)}, bf16[8,3584]{1,0:T(8,128)(2,1)S(1)}, u32[]{:S(2)}, u32[]{:S(2)}) collective-permute-start(bf16[8,3584]{1,0:T(8,128)(2,1)S(1)} %fusion.refs_0_), channel_id=1, source_target_pairs={{0,4},{1,5},{2,6},{3,7},{4,0},{5,1},{6,2},{7,3},{8,12},{9,13},{10,... | collective-permute-start | bytes 172040 | tf_op jit(solution)/shard_map/ppermute | solution.py:23
  35.7 4.2 %collective-permute-start.12 = (bf16[8,3584]{1,0:T(8,128)(2,1)S(1)}, bf16[8,3584]{1,0:T(8,128)(2,1)S(1)}, u32[]{:S(2)}, u32[]{:S(2)}) collective-permute-start(bf16[8,3584]{1,0:T(8,128)(2,1)S(1)} %fusion.refs_0_), channel_id=1, source_target_pairs={{0,2},{1,3},{2,0},{3,1},{4,6},{5,7},{6,4},{7,5},{8,10},{9,11},{10,... | collective-permute-start | bytes 172040 | tf_op jit(solution)/shard_map/ppermute | solution.py:23
  36.2 3.6 %collective-permute-start.15 = (bf16[8,3584]{1,0:T(8,128)(2,1)S(1)}, bf16[8,3584]{1,0:T(8,128)(2,1)S(1)}, u32[]{:S(2)}, u32[]{:S(2)}) collective-permute-start(bf16[8,3584]{1,0:T(8,128)(2,1)S(1)} %fusion.refs_0_), channel_id=1, source_target_pairs={{0,1},{1,0},{2,3},{3,2},{4,5},{5,4},{6,7},{7,6},{8,9},{9,8},{10,11... | collective-permute-start | bytes 172040 | tf_op jit(solution)/shard_map/ppermute | solution.py:23
  37.8 2.0 %collective-permute-start.18 = (bf16[8,3584]{1,0:T(8,128)(2,1)S(1)}, bf16[8,3584]{1,0:T(8,128)(2,1)S(1)}, u32[]{:S(2)}, u32[]{:S(2)}) collective-permute-start(bf16[8,3584]{1,0:T(8,128)(2,1)S(1)} %collective-permute-done.14.refs_3_), channel_id=1, source_target_pairs={{0,1},{1,0},{2,3},{3,2},{4,5},{5,4},{6,7},{7,6},{8,9},{9,8},{10,11... | collective-permute-start | bytes 172040 | tf_op jit(solution)/shard_map/ppermute | solution.py:23
  38.6 1.2 %collective-permute-start.17 = (bf16[8,3584]{1,0:T(8,128)(2,1)S(1)}, bf16[8,3584]{1,0:T(8,128)(2,1)S(1)}, u32[]{:S(2)}, u32[]{:S(2)}) collective-permute-start(bf16[8,3584]{1,0:T(8,128)(2,1)S(1)} %collective-permute-done.13.refs_2_), channel_id=1, source_target_pairs={{0,1},{1,0},{2,3},{3,2},{4,5},{5,4},{6,7},{7,6},{8,9},{9,8},{10,11... | collective-permute-start | bytes 172040 | tf_op jit(solution)/shard_map/ppermute | solution.py:23
  39.8 1.2 %collective-permute-start.16 = (bf16[8,3584]{1,0:T(8,128)(2,1)S(1)}, bf16[8,3584]{1,0:T(8,128)(2,1)S(1)}, u32[]{:S(2)}, u32[]{:S(2)}) collective-permute-start(bf16[8,3584]{1,0:T(8,128)(2,1)S(1)} %collective-permute-done.12.refs_1_), channel_id=1, source_target_pairs={{0,1},{1,0},{2,3},{3,2},{4,5},{5,4},{6,7},{7,6},{8,9},{9,8},{10,11... | collective-permute-start | bytes 172040 | tf_op jit(solution)/shard_map/ppermute | solution.py:23

commit v7 on v6

--- a/solution.py
+++ b/solution.py
@@ -83,8 +83,15 @@
         (list_hbm, row_ref),
     ]
     copies = [pltpu.make_async_copy(s, d, sems.at[i]) for i, (s, d) in enumerate(pairs)]
-    for copy in copies[6:] + copies[:6]:
+    for copy in copies[1:3] + copies[6:8] + copies[:1] + copies[3:6] + copies[8:]:
         copy.start()
+    line = lax.broadcasted_iota(jnp.int32, (lines, lines), 0)
+    taken = lax.broadcasted_iota(jnp.int32, (lines, lines), 1)
+    swap = (taken == line % rows * heads + line // rows).astype(jnp.float32).astype(jnp.bfloat16)
+    own = (
+        lax.broadcasted_iota(jnp.int32, (lines, width), 0) // (per_kv * rows)
+        == lax.broadcasted_iota(jnp.int32, (lines, width), 1) // size
+    )
     copies[6].wait()
     copies[7].wait()
     group, chip, core = place()
@@ -95,13 +102,6 @@
     live_lanes = count_ref[group] * (live_ref.shape[1] // list_ref.shape[1])
     lane = lax.broadcasted_iota(jnp.int32, live_ref.shape, 1)
     live_ref[...] = (lane < live_lanes).astype(jnp.float32)
-    line = lax.broadcasted_iota(jnp.int32, (lines, lines), 0)
-    taken = lax.broadcasted_iota(jnp.int32, (lines, lines), 1)
-    swap = (taken == line % rows * heads + line // rows).astype(jnp.float32).astype(jnp.bfloat16)
-    own = (
-        lax.broadcasted_iota(jnp.int32, (lines, width), 0) // (per_kv * rows)
-        == lax.broadcasted_iota(jnp.int32, (lines, width), 1) // size
-    )
     copies[0].wait()
     request = lax.broadcasted_iota(jnp.int32, (lines, 1), 0) % rows
     first = request * slots

time: 54.1 us -> 54.1 us (level)
  no operation moved by 1% of the time
where the time goes in v7:
time: 54.1 us; the launch traced here: 54 us
  starting transfers between devices  16 us (30%)
  Pallas kernels  15.6 us (29%)
  waiting for transfers between devices  11.2 us (21%)
  blocking collectives  10.7 us (20%)
    ppermute x19, starting transfers between devices, from_partner(): return lax.ppermute(value, 'hid', pairs)  16 us
    ppermute x19, waiting for transfers between devices, from_partner(): return lax.ppermute(value, 'hid', pairs)  11.2 us
    all_to_all x1, blocking collectives, on_device(): lax.all_to_all(ffn_part, 'hid', split_axis=0, concat_axis=0, tiled=True)  10.7 us
    pallas_call x2, Pallas kernels, fetch(): pl.pallas_call(functools.partial(fetch_kernel, [first for _, first, _ in...  7.95 us
    pallas_call x1, Pallas kernels, attend(): pl.pallas_call(functools.partial(attend_kernel, width // size), out_shape...  3.55 us
    pallas_call x1, Pallas kernels, gate_up(): pl.pallas_call(functools.partial(gate_up_kernel, len(arrived)), out_shape...  2.09 us
    pallas_call x1, Pallas kernels, down(): pl.pallas_call(down_kernel, out_shape=pltpu.VMEM((devices, rows, weights....  1.39 us
  transfers between devices with their start and end apart: 19, of which 10 were waited for; matrix products, arithmetic and copies ran while one was open for 0% of the time, Pallas kernels for 15%

profile of v7, /device:TPU:0, one launch (start us, length us, event | category | flops | bytes accessed | tf_op | source)
XLA Modules:
  0.0 54.0 jit_solution(7004831018994819961)
XLA Ops:
  0.0 3.5 %attend.1 = (f32[4,8192]{1,0:T(4,128)S(1)}, bf16[4,4,1024]{2,1,0:T(4,128)(2,1)S(1)}, bf16[4,4,1024]{2,1,0:T(4,128)(2,1)S(1)}, s32[2,28]{1,0:T(2,128)S(1)}, f32[1...) custom-call(s32[4]{0:T(128)} %len_hbm.1, bf16[4,64,128]{2,1,0:T(8,128)(2,1)} %q_hbm.1, bf16[4,192,1024]{2,1,0:T(8,128)(2,1)} %k_hbm.1, ...), custom_call_target="tpu_custom_call" | custom-call | tf_op jit(solution)/shard_map/attend/pallas_call | solution.py:163
  3.6 0.5 collective-permute-start
  4.1 0.9 %collective-permute-done = bf16[4,4,1024]{2,1,0:T(4,128)(2,1)S(1)} collective-permute-done((bf16[4,4,1024]{2,1,0:T(4,128)(2,1)S(1)}, bf16[4,4,1024]{2,1,0:T(4,128)(2,1)S(1)}, u32[]{:S(2)}, u32[]{:S(2)}) %collective-permute-start) | collective-permute-done | bytes 32800 | tf_op jit(solution)/shard_map/ppermute | solution.py:23
  5.0 2.9 %collective-permute-start.1 = (bf16[2,4,1024]{2,1,0:T(4,128)(2,1)S(1)}, bf16[2,4,1024]{2,1,0:T(4,128)(2,1)S(1)}, u32[]{:S(2)}, u32[]{:S(2)}) collective-permute-start(bf16[2,4,1024]{2,1,0:T(4,128)(2,1)S(1)} %get-tuple-element.42), channel_id=1, source_target_pairs={{0,2},{1,3},{2,0},{3,1},{4,6},{5,7},{6,4},{7,5},{8,10},{9,11},{10,... | collective-permute-start | bytes 49160 | tf_op jit(solution)/shard_map/ppermute | solution.py:23
  7.9 1.5 %collective-permute-start.3 = (bf16[2,4,1024]{2,1,0:T(4,128)(2,1)S(1)}, bf16[2,4,1024]{2,1,0:T(4,128)(2,1)S(1)}, u32[]{:S(2)}, u32[]{:S(2)}) collective-permute-start(bf16[2,4,1024]{2,1,0:T(4,128)(2,1)S(1)} %get-tuple-element.43), channel_id=1, source_target_pairs={{0,6},{1,7},{2,4},{3,5},{4,2},{5,3},{6,0},{7,1},{8,14},{9,15},{10,... | collective-permute-start | bytes 49160 | tf_op jit(solution)/shard_map/ppermute | solution.py:23
  9.4 0.1 collective-permute-start.2
  9.5 0.1 collective-permute-done.1
  9.6 2.9 %collective-permute-done.3 = bf16[2,4,1024]{2,1,0:T(4,128)(2,1)S(1)} collective-permute-done((bf16[2,4,1024]{2,1,0:T(4,128)(2,1)S(1)}, bf16[2,4,1024]{2,1,0:T(4,128)(2,1)S(1)}, u32[]{:S(2)}, u32[]{:S(2)}) %collective-permute-start.3) | collective-permute-done | bytes 16416 | tf_op jit(solution)/shard_map/ppermute | solution.py:23
  12.6 0.6 %collective-permute-done.2 = bf16[2,4,1024]{2,1,0:T(4,128)(2,1)S(1)} collective-permute-done((bf16[2,4,1024]{2,1,0:T(4,128)(2,1)S(1)}, bf16[2,4,1024]{2,1,0:T(4,128)(2,1)S(1)}, u32[]{:S(2)}, u32[]{:S(2)}) %collective-permute-start.2) | collective-permute-done | bytes 16416 | tf_op jit(solution)/shard_map/ppermute | solution.py:23
  13.2 2.7 %collective-permute-start.4 = (bf16[1,4,2,4,1024]{4,3,2,1,0:T(4,128)(2,1)S(1)}, bf16[1,4,2,4,1024]{4,3,2,1,0:T(4,128)(2,1)S(1)}, u32[]{:S(2)}, u32[]{:S(2)}) collective-permute-start(bf16[1,4,2,4,1024]{4,3,2,1,0:T(4,128)(2,1)S(1)} %maximum_bitcast_fusion.rest_2_.refs_0_), channel_id=1, source_target_pairs={{0,8},{1,9},{2,10},{3,11},{4,12},{5,13},{6,14},{7,15},{8,0},{9,1},... | collective-permute-start | bytes 196616 | tf_op jit(solution)/shard_map/ppermute | solution.py:23
  15.9 4.5 %fetch_later.1 = (bf16[12,1024,128]{2,1,0:T(8,128)(2,1)S(1)}, bf16[28,1024,128]{2,1,0:T(8,128)(2,1)S(1)}) custom-call(s32[2,28]{1,0:T(2,128)S(1)} %get-tuple-element.24.rows_ref, bf16[1,56,1024,128]{3,2,1,0:T(8,128)(2,1)} %rest_0_.2, bf16[1,56,1024,128]{3,2,1,0:T(8,128)(2,1)} %rest_1_.1, bf16[1,4,2,4,1024]{4,3,2,1,0:T(4,128)(2,1)S(1)} %maximum_bitcast_fusion.rest_2_.refs_0_), custom_call_target="tpu_custom_call" | custom-call | bytes 20971520 | tf_op jit(solution)/shard_map/fetch_later/pallas_call | solution.py:229
  20.4 2.1 %gate_up.1 = (f32[8,7168]{1,0:T(8,128)S(1)}, f32[8,7168]{1,0:T(8,128)S(1)}, f32[8,7168]{1,0:T(8,128)S(1)}, f32[8,7168]{1,0:T(8,128)S(1)}, bf16[8,7168]{1,0:T(8,1...) custom-call(bf16[1,4,2,4,1024]{4,3,2,1,0:T(4,128)(2,1)S(1)} %maximum_bitcast_fus, ...), custom_call_target="tpu_custom_call" | custom-call | tf_op jit(solution)/shard_map/gate_up/pallas_call | solution.py:276
  22.5 0.1 collective-permute-start.6
  22.6 0.5 collective-permute-start.5
  23.1 0.1 collective-permute-start.8
  23.2 0.4 collective-permute-start.10
  23.6 0.3 collective-permute-done.6
  23.9 1.5 %collective-permute-start.7 = (bf16[8,7168]{1,0:T(8,128)(2,1)S(1)}, bf16[8,7168]{1,0:T(8,128)(2,1)S(1)}, u32[]{:S(2)}, u32[]{:S(2)}) collective-permute-start(bf16[8,7168]{1,0:T(8,128)(2,1)S(1)} %add_convert_fusion.2), channel_id=1, source_target_pairs={{0,6},{1,7},{2,4},{3,5},{4,2},{5,3},{6,0},{7,1},{8,14},{9,15},{10,... | collective-permute-start | bytes 344072 | tf_op jit(solution)/shard_map/ppermute | solution.py:23
  25.4 1.7 %collective-permute-start.9 = (bf16[8,7168]{1,0:T(8,128)(2,1)S(1)}, bf16[8,7168]{1,0:T(8,128)(2,1)S(1)}, u32[]{:S(2)}, u32[]{:S(2)}) collective-permute-start(bf16[8,7168]{1,0:T(8,128)(2,1)S(1)} %add_convert_fusion.1), channel_id=1, source_target_pairs={{0,4},{1,5},{2,6},{3,7},{4,0},{5,1},{6,2},{7,3},{8,12},{9,13},{10,... | collective-permute-start | bytes 344072 | tf_op jit(solution)/shard_map/ppermute | solution.py:23
  27.2 0.5 collective-permute-start.11
  27.7 3.4 %fetch_down.1 = (bf16[28,128,1024]{2,1,0:T(8,128)(2,1)S(1)}, f32[8,7168]{1,0:T(8,128)S(1)}) custom-call(s32[2,28]{1,0:T(2,128)S(1)} %get-tuple-element.24.rows_ref, bf16[1,56,128,1024]{3,2,1,0:T(8,128)(2,1)} %rest_0_.3, f32[8,7168]{1,0:T(8,128)S(1)} %convert_add_fusion.1.rest_1_), custom_call_target="tpu_custom_call", output_to_operand_aliasing={{1}: (2, {})} | custom-call | bytes 14680064 | tf_op jit(solution)/shard_map/fetch_down/pallas_call | solution.py:229
  31.2 1.5 %collective-permute-done.9 = bf16[8,7168]{1,0:T(8,128)(2,1)S(1)} collective-permute-done((bf16[8,7168]{1,0:T(8,128)(2,1)S(1)}, bf16[8,7168]{1,0:T(8,128)(2,1)S(1)}, u32[]{:S(2)}, u32[]{:S(2)}) %collective-permute-start.9) | collective-permute-done | bytes 114720 | tf_op jit(solution)/shard_map/ppermute | solution.py:23
  32.8 1.3 %collective-permute-start.14 = (bf16[8,3584]{1,0:T(8,128)(2,1)S(1)}, bf16[8,3584]{1,0:T(8,128)(2,1)S(1)}, u32[]{:S(2)}, u32[]{:S(2)}) collective-permute-start(bf16[8,3584]{1,0:T(8,128)(2,1)S(1)} %fusion.refs_0_), channel_id=1, source_target_pairs={{0,6},{1,7},{2,4},{3,5},{4,2},{5,3},{6,0},{7,1},{8,14},{9,15},{10,... | collective-permute-start | bytes 172040 | tf_op jit(solution)/shard_map/ppermute | solution.py:23
  34.1 1.6 %collective-permute-start.13 = (bf16[8,3584]{1,0:T(8,128)(2,1)S(1)}, bf16[8,3584]{1,0:T(8,128)(2,1)S(1)}, u32[]{:S(2)}, u32[]{:S(2)}) collective-permute-start(bf16[8,3584]{1,0:T(8,128)(2,1)S(1)} %fusion.refs_0_), channel_id=1, source_target_pairs={{0,4},{1,5},{2,6},{3,7},{4,0},{5,1},{6,2},{7,3},{8,12},{9,13},{10,... | collective-permute-start | bytes 172040 | tf_op jit(solution)/shard_map/ppermute | solution.py:23
  35.7 0.6 %collective-permute-start.12 = (bf16[8,3584]{1,0:T(8,128)(2,1)S(1)}, bf16[8,3584]{1,0:T(8,128)(2,1)S(1)}, u32[]{:S(2)}, u32[]{:S(2)}) collective-permute-start(bf16[8,3584]{1,0:T(8,128)(2,1)S(1)} %fusion.refs_0_), channel_id=1, source_target_pairs={{0,2},{1,3},{2,0},{3,1},{4,6},{5,7},{6,4},{7,5},{8,10},{9,11},{10,... | collective-permute-start | bytes 172040 | tf_op jit(solution)/shard_map/ppermute | solution.py:23
  36.3 1.6 %collective-permute-done.14.refs_3_ = bf16[8,3584]{1,0:T(8,128)(2,1)S(1)} collective-permute-done((bf16[8,3584]{1,0:T(8,128)(2,1)S(1)}, bf16[8,3584]{1,0:T(8,128)(2,1)S(1)}, u32[]{:S(2)}, u32[]{:S(2)}) %collective-permute-start.14) | collective-permute-done | bytes 57376 | tf_op jit(solution)/shard_map/ppermute | solution.py:23
  37.9 0.8 %collective-permute-done.13.refs_2_ = bf16[8,3584]{1,0:T(8,128)(2,1)S(1)} collective-permute-done((bf16[8,3584]{1,0:T(8,128)(2,1)S(1)}, bf16[8,3584]{1,0:T(8,128)(2,1)S(1)}, u32[]{:S(2)}, u32[]{:S(2)}) %collective-permute-start.13) | collective-permute-done | bytes 57376 | tf_op jit(solution)/shard_map/ppermute | solution.py:23
  38.7 1.2 %collective-permute-done.12.refs_1_ = bf16[8,3584]{1,0:T(8,128)(2,1)S(1)} collective-permute-done((bf16[8,3584]{1,0:T(8,128)(2,1)S(1)}, bf16[8,3584]{1,0:T(8,128)(2,1)S(1)}, u32[]{:S(2)}, u32[]{:S(2)}) %collective-permute-start.12) | collective-permute-done | bytes 57376 | tf_op jit(solution)/shard_map/ppermute | solution.py:23
  39.9 1.2 %collective-permute-done.16.refs_5_ = bf16[8,3584]{1,0:T(8,128)(2,1)S(1)} collective-permute-done((bf16[8,3584]{1,0:T(8,128)(2,1)S(1)}, bf16[8,3584]{1,0:T(8,128)(2,1)S(1)}, u32[]{:S(2)}, u32[]{:S(2)}) %collective-permute-start.16) | collective-permute-done | bytes 57376 | tf_op jit(solution)/shard_map/ppermute | solution.py:23
  41.2 1.4 %down.1 = bf16[16,4,1024]{2,1,0:T(4,128)(2,1)S(1)} custom-call(bf16[8,3584]{1,0:T(8,128)(2,1)S(1)} %fusion.refs_0_, bf16[8,3584]{1,0:T(8,128)(2,1)S(1)} %collective-permute-done.12.refs_1_, bf16[8,3584]{1,0:T(8,128)(2,1)S(1)} %collective-permute-done.13.refs_2_, bf16[8,3584]{1,0:T(8,128)(2,1)S(1)} %collective-permute-done.14.refs_3_, ...), custom_call_target="tpu_custom_call" | custom-call | tf_op jit(solution)/shard_map/down/pallas_call | solution.py:308
  42.6 10.7 %all_to_all.5.back_ref = bf16[16,4,1024]{2,1,0:T(4,128)(2,1)S(1)} all-to-all(bf16[16,4,1024]{2,1,0:T(4,128)(2,1)S(1)} %down.1), channel_id=1, replica_groups=mesh['groups'=2,'hid'=16] {'hid'}, dimensions={0} | all-to-all | bytes 262144 | tf_op jit(solution)/shard_map/all_to_all | solution.py:398
  53.3 0.7 %finish.1 = bf16[4,8192]{1,0:T(4,128)(2,1)} custom-call(f32[4,8192]{1,0:T(4,128)S(1)} %get-tuple-element.23.mixed_ref, bf16[16,4,1024]{2,1,0:T(4,128)(2,1)S(1)} %all_to_all.5.back_ref), custom_call_target="tpu_custom_call" | custom-call | tf_op jit(solution)/shard_map/finish/pallas_call | solution.py:328
  (21 shorter events, 0.3 us)
Async XLA Ops:
  3.6 1.4 %collective-permute-start = (bf16[4,4,1024]{2,1,0:T(4,128)(2,1)S(1)}, bf16[4,4,1024]{2,1,0:T(4,128)(2,1)S(1)}, u32[]{:S(2)}, u32[]{:S(2)}) collective-permute-start(bf16[4,4,1024]{2,1,0:T(4,128)(2,1)S(1)} %get-tuple-element.26), channel_id=1, source_target_pairs={{0,1},{1,0},{2,3},{3,2},{4,5},{5,4},{6,7},{7,6},{8,9},{9,8},{10,11... | collective-permute-start | bytes 98312 | tf_op jit(solution)/shard_map/ppermute | solution.py:23
  5.0 4.6 %collective-permute-start.1 = (bf16[2,4,1024]{2,1,0:T(4,128)(2,1)S(1)}, bf16[2,4,1024]{2,1,0:T(4,128)(2,1)S(1)}, u32[]{:S(2)}, u32[]{:S(2)}) collective-permute-start(bf16[2,4,1024]{2,1,0:T(4,128)(2,1)S(1)} %get-tuple-element.42), channel_id=1, source_target_pairs={{0,2},{1,3},{2,0},{3,1},{4,6},{5,7},{6,4},{7,5},{8,10},{9,11},{10,... | collective-permute-start | bytes 49160 | tf_op jit(solution)/shard_map/ppermute | solution.py:23
  7.9 4.6 %collective-permute-start.3 = (bf16[2,4,1024]{2,1,0:T(4,128)(2,1)S(1)}, bf16[2,4,1024]{2,1,0:T(4,128)(2,1)S(1)}, u32[]{:S(2)}, u32[]{:S(2)}) collective-permute-start(bf16[2,4,1024]{2,1,0:T(4,128)(2,1)S(1)} %get-tuple-element.43), channel_id=1, source_target_pairs={{0,6},{1,7},{2,4},{3,5},{4,2},{5,3},{6,0},{7,1},{8,14},{9,15},{10,... | collective-permute-start | bytes 49160 | tf_op jit(solution)/shard_map/ppermute | solution.py:23
  9.4 3.7 %collective-permute-start.2 = (bf16[2,4,1024]{2,1,0:T(4,128)(2,1)S(1)}, bf16[2,4,1024]{2,1,0:T(4,128)(2,1)S(1)}, u32[]{:S(2)}, u32[]{:S(2)}) collective-permute-start(bf16[2,4,1024]{2,1,0:T(4,128)(2,1)S(1)} %get-tuple-element.44), channel_id=1, source_target_pairs={{0,4},{1,5},{2,6},{3,7},{4,0},{5,1},{6,2},{7,3},{8,12},{9,13},{10,... | collective-permute-start | bytes 49160 | tf_op jit(solution)/shard_map/ppermute | solution.py:23
  13.2 7.2 %collective-permute-start.4 = (bf16[1,4,2,4,1024]{4,3,2,1,0:T(4,128)(2,1)S(1)}, bf16[1,4,2,4,1024]{4,3,2,1,0:T(4,128)(2,1)S(1)}, u32[]{:S(2)}, u32[]{:S(2)}) collective-permute-start(bf16[1,4,2,4,1024]{4,3,2,1,0:T(4,128)(2,1)S(1)} %maximum_bitcast_fusion.rest_2_.refs_0_), channel_id=1, source_target_pairs={{0,8},{1,9},{2,10},{3,11},{4,12},{5,13},{6,14},{7,15},{8,0},{9,1},... | collective-permute-start | bytes 196616 | tf_op jit(solution)/shard_map/ppermute | solution.py:23
  22.5 1.4 %collective-permute-start.6 = (bf16[8,7168]{1,0:T(8,128)(2,1)S(1)}, bf16[8,7168]{1,0:T(8,128)(2,1)S(1)}, u32[]{:S(2)}, u32[]{:S(2)}) collective-permute-start(bf16[8,7168]{1,0:T(8,128)(2,1)S(1)} %get-tuple-element.35), channel_id=1, source_target_pairs={{0,1},{1,0},{2,3},{3,2},{4,5},{5,4},{6,7},{7,6},{8,9},{9,8},{10,11... | collective-permute-start | bytes 344072 | tf_op jit(solution)/shard_map/ppermute | solution.py:23
  22.6 5.1 %collective-permute-start.5 = (bf16[8,7168]{1,0:T(8,128)(2,1)S(1)}, bf16[8,7168]{1,0:T(8,128)(2,1)S(1)}, u32[]{:S(2)}, u32[]{:S(2)}) collective-permute-start(bf16[8,7168]{1,0:T(8,128)(2,1)S(1)} %get-tuple-element.32), channel_id=1, source_target_pairs={{0,1},{1,0},{2,3},{3,2},{4,5},{5,4},{6,7},{7,6},{8,9},{9,8},{10,11... | collective-permute-start | bytes 344072 | tf_op jit(solution)/shard_map/ppermute | solution.py:23
  23.1 2.3 %collective-permute-start.8 = (bf16[8,7168]{1,0:T(8,128)(2,1)S(1)}, bf16[8,7168]{1,0:T(8,128)(2,1)S(1)}, u32[]{:S(2)}, u32[]{:S(2)}) collective-permute-start(bf16[8,7168]{1,0:T(8,128)(2,1)S(1)} %get-tuple-element.37), channel_id=1, source_target_pairs={{0,1},{1,0},{2,3},{3,2},{4,5},{5,4},{6,7},{7,6},{8,9},{9,8},{10,11... | collective-permute-start | bytes 344072 | tf_op jit(solution)/shard_map/ppermute | solution.py:23
  23.2 4.0 %collective-permute-start.10 = (bf16[8,7168]{1,0:T(8,128)(2,1)S(1)}, bf16[8,7168]{1,0:T(8,128)(2,1)S(1)}, u32[]{:S(2)}, u32[]{:S(2)}) collective-permute-start(bf16[8,7168]{1,0:T(8,128)(2,1)S(1)} %get-tuple-element.39), channel_id=1, source_target_pairs={{0,1},{1,0},{2,3},{3,2},{4,5},{5,4},{6,7},{7,6},{8,9},{9,8},{10,11... | collective-permute-start | bytes 344072 | tf_op jit(solution)/shard_map/ppermute | solution.py:23
  23.9 7.3 %collective-permute-start.7 = (bf16[8,7168]{1,0:T(8,128)(2,1)S(1)}, bf16[8,7168]{1,0:T(8,128)(2,1)S(1)}, u32[]{:S(2)}, u32[]{:S(2)}) collective-permute-start(bf16[8,7168]{1,0:T(8,128)(2,1)S(1)} %add_convert_fusion.2), channel_id=1, source_target_pairs={{0,6},{1,7},{2,4},{3,5},{4,2},{5,3},{6,0},{7,1},{8,14},{9,15},{10,... | collective-permute-start | bytes 344072 | tf_op jit(solution)/shard_map/ppermute | solution.py:23
  25.4 7.2 %collective-permute-start.9 = (bf16[8,7168]{1,0:T(8,128)(2,1)S(1)}, bf16[8,7168]{1,0:T(8,128)(2,1)S(1)}, u32[]{:S(2)}, u32[]{:S(2)}) collective-permute-start(bf16[8,7168]{1,0:T(8,128)(2,1)S(1)} %add_convert_fusion.1), channel_id=1, source_target_pairs={{0,4},{1,5},{2,6},{3,7},{4,0},{5,1},{6,2},{7,3},{8,12},{9,13},{10,... | collective-permute-start | bytes 344072 | tf_op jit(solution)/shard_map/ppermute | solution.py:23
  27.2 5.5 %collective-permute-start.11 = (bf16[8,7168]{1,0:T(8,128)(2,1)S(1)}, bf16[8,7168]{1,0:T(8,128)(2,1)S(1)}, u32[]{:S(2)}, u32[]{:S(2)}) collective-permute-start(bf16[8,7168]{1,0:T(8,128)(2,1)S(1)} %add_convert_fusion), channel_id=1, source_target_pairs={{0,2},{1,3},{2,0},{3,1},{4,6},{5,7},{6,4},{7,5},{8,10},{9,11},{10,... | collective-permute-start | bytes 344072 | tf_op jit(solution)/shard_map/ppermute | solution.py:23
  32.8 5.2 %collective-permute-start.14 = (bf16[8,3584]{1,0:T(8,128)(2,1)S(1)}, bf16[8,3584]{1,0:T(8,128)(2,1)S(1)}, u32[]{:S(2)}, u32[]{:S(2)}) collective-permute-start(bf16[8,3584]{1,0:T(8,128)(2,1)S(1)} %fusion.refs_0_), channel_id=1, source_target_pairs={{0,6},{1,7},{2,4},{3,5},{4,2},{5,3},{6,0},{7,1},{8,14},{9,15},{10,... | collective-permute-start | bytes 172040 | tf_op jit(solution)/shard_map/ppermute | solution.py:23
  34.1 4.6 %collective-permute-start.13 = (bf16[8,3584]{1,0:T(8,128)(2,1)S(1)}, bf16[8,3584]{1,0:T(8,128)(2,1)S(1)}, u32[]{:S(2)}, u32[]{:S(2)}) collective-permute-start(bf16[8,3584]{1,0:T(8,128)(2,1)S(1)} %fusion.refs_0_), channel_id=1, source_target_pairs={{0,4},{1,5},{2,6},{3,7},{4,0},{5,1},{6,2},{7,3},{8,12},{9,13},{10,... | collective-permute-start | bytes 172040 | tf_op jit(solution)/shard_map/ppermute | solution.py:23
  35.7 4.2 %collective-permute-start.12 = (bf16[8,3584]{1,0:T(8,128)(2,1)S(1)}, bf16[8,3584]{1,0:T(8,128)(2,1)S(1)}, u32[]{:S(2)}, u32[]{:S(2)}) collective-permute-start(bf16[8,3584]{1,0:T(8,128)(2,1)S(1)} %fusion.refs_0_), channel_id=1, source_target_pairs={{0,2},{1,3},{2,0},{3,1},{4,6},{5,7},{6,4},{7,5},{8,10},{9,11},{10,... | collective-permute-start | bytes 172040 | tf_op jit(solution)/shard_map/ppermute | solution.py:23
  36.3 3.6 %collective-permute-start.15 = (bf16[8,3584]{1,0:T(8,128)(2,1)S(1)}, bf16[8,3584]{1,0:T(8,128)(2,1)S(1)}, u32[]{:S(2)}, u32[]{:S(2)}) collective-permute-start(bf16[8,3584]{1,0:T(8,128)(2,1)S(1)} %fusion.refs_0_), channel_id=1, source_target_pairs={{0,1},{1,0},{2,3},{3,2},{4,5},{5,4},{6,7},{7,6},{8,9},{9,8},{10,11... | collective-permute-start | bytes 172040 | tf_op jit(solution)/shard_map/ppermute | solution.py:23
  37.9 2.0 %collective-permute-start.18 = (bf16[8,3584]{1,0:T(8,128)(2,1)S(1)}, bf16[8,3584]{1,0:T(8,128)(2,1)S(1)}, u32[]{:S(2)}, u32[]{:S(2)}) collective-permute-start(bf16[8,3584]{1,0:T(8,128)(2,1)S(1)} %collective-permute-done.14.refs_3_), channel_id=1, source_target_pairs={{0,1},{1,0},{2,3},{3,2},{4,5},{5,4},{6,7},{7,6},{8,9},{9,8},{10,11... | collective-permute-start | bytes 172040 | tf_op jit(solution)/shard_map/ppermute | solution.py:23
  38.7 1.2 %collective-permute-start.17 = (bf16[8,3584]{1,0:T(8,128)(2,1)S(1)}, bf16[8,3584]{1,0:T(8,128)(2,1)S(1)}, u32[]{:S(2)}, u32[]{:S(2)}) collective-permute-start(bf16[8,3584]{1,0:T(8,128)(2,1)S(1)} %collective-permute-done.13.refs_2_), channel_id=1, source_target_pairs={{0,1},{1,0},{2,3},{3,2},{4,5},{5,4},{6,7},{7,6},{8,9},{9,8},{10,11... | collective-permute-start | bytes 172040 | tf_op jit(solution)/shard_map/ppermute | solution.py:23
  39.9 1.2 %collective-permute-start.16 = (bf16[8,3584]{1,0:T(8,128)(2,1)S(1)}, bf16[8,3584]{1,0:T(8,128)(2,1)S(1)}, u32[]{:S(2)}, u32[]{:S(2)}) collective-permute-start(bf16[8,3584]{1,0:T(8,128)(2,1)S(1)} %collective-permute-done.12.refs_1_), channel_id=1, source_target_pairs={{0,1},{1,0},{2,3},{3,2},{4,5},{5,4},{6,7},{7,6},{8,9},{9,8},{10,11... | collective-permute-start | bytes 172040 | tf_op jit(solution)/shard_map/ppermute | solution.py:23
